TPU v7x, 32 devices: a whole 2x2x4 slice. The times are simulated.
32 devices in a mesh: blk: 8 (over y, x, core), rep: 4 (over z).
Axes of the slice: x: 2, y: 2, z: 4, core: 2. Of those that a mesh axis runs over, the one named last changes fastest.
Arguments:
- features: bfloat16 [4096, 256], P(('blk', 'rep')), may hold values from -6 to 6
- weight: bfloat16 [256, 256], replicated, may hold values from -0.375 to 0.375
- cotangent: bfloat16 [4096, 256], P(('blk', 'rep')), may hold values from -6 to 6
- block_rows: int32 [8, 8, 4, 2], P('blk', None, 'rep'), may hold values from 0 to 3, as said below
- block_counts: int32 [8, 8, 4], P('blk', None, 'rep'), may hold values from 1 to 2, as said below
- block_values: bfloat16 [8, 8, 4, 128, 256], P('blk', None, 'rep'), as said below
Outputs:
- activation: bfloat16 [4096, 256], P(('blk', 'rep'))
- grad_weight: float32 [256, 256], replicated
- grad_features: bfloat16 [4096, 256], P(('blk', 'rep'))
Inputs may be any that keep to these rules, and one draw needn't show every extreme that they name: `block_rows`: within one block row, column block and column set the 2 row-block numbers are distinct; slots at or beyond the count hold valid numbers and are not part of A. block_counts[i, j, r] does not depend on r, equals block_counts[j, i, r], and block_counts[i, i, r] = 2. `block_values`: Positive, and the adjacency A built from the three adjacency arguments is exactly symmetric.
All inputs are finite; a program needn't handle non-finite values.
Results may differ from a plain program's by a relative error of at most 0.017.
Values may be sent and summed in bfloat16 or wider, within the bound.
No kernel may reach another device: no remote copies, remote signals or barrier semaphores. Data moves between devices by JAX's collectives and lax.ppermute only.
A program may use at most 64 MiB of HBM per device.

v0:
```python
import math

import jax
import jax.numpy as jnp
from jax import lax
from jax.sharding import PartitionSpec as P


def replica_total(partial_value):
    return lax.psum_scatter(
        partial_value.astype(jnp.bfloat16), "rep", scatter_dimension=0, tiled=True
    ).astype(jnp.float32)


def add_tile(running, column_block, node_slab, tiles, slot_rows, slot_counts):
    block_size = node_slab.shape[0]
    tile_now = lax.dynamic_index_in_dim(tiles, column_block, 0, keepdims=False)
    rows_now = lax.dynamic_index_in_dim(slot_rows, column_block, 0, keepdims=False)
    count_now = lax.dynamic_index_in_dim(slot_counts, column_block, 0, keepdims=False)

    def one_slot(slot_index, carried):
        weights_now = lax.dynamic_slice_in_dim(tile_now, slot_index * block_size, block_size, 1)
        product = jnp.dot(weights_now, node_slab, preferred_element_type=jnp.float32)
        first_row = rows_now[slot_index] * block_size
        current = lax.dynamic_slice_in_dim(carried, first_row, block_size, 0)
        return lax.dynamic_update_slice_in_dim(carried, current + product, first_row, 0)

    return lax.fori_loop(0, count_now, one_slot, running)


def aggregate(node_slab, tiles, slot_rows, slot_counts):
    block_size = node_slab.shape[0]
    running = jnp.zeros((block_size * lax.axis_size("rep"), node_slab.shape[1]), jnp.float32)
    piece = lax.all_gather(node_slab, "blk", axis=0, tiled=True)
    piece_count = piece.shape[0] // block_size

    def one_piece(inner, running_now):
        slab_now = lax.dynamic_slice_in_dim(piece, inner * block_size, block_size, 0)
        return add_tile(running_now, inner, slab_now, tiles, slot_rows, slot_counts)

    return lax.fori_loop(0, piece_count, one_piece, running)


def shards(features, weight, cotangent, block_rows, block_counts, block_values):
    tiles = block_values[0, :, 0]
    slot_rows = block_rows[0, :, 0]
    slot_counts = block_counts[0, :, 0]
    agg = replica_total(aggregate(features, tiles, slot_rows, slot_counts)).astype(jnp.bfloat16)
    pre = jnp.dot(agg, weight, preferred_element_type=jnp.float32)
    sig = jax.nn.sigmoid(pre)
    activation = (pre * sig).astype(jnp.bfloat16)
    dpre = (cotangent.astype(jnp.float32) * sig * (1.0 + pre * (1.0 - sig))).astype(jnp.bfloat16)
    local_grad = lax.dot_general(
        agg, dpre, (((0,), (0,)), ((), ())), preferred_element_type=jnp.float32
    )
    node_count = features.shape[0] * lax.axis_size("blk") * lax.axis_size("rep")
    grad_weight = lax.psum(local_grad, ("blk", "rep")) / math.sqrt(node_count)
    back = lax.dot_general(
        dpre, weight, (((1,), (1,)), ((), ())), preferred_element_type=jnp.float32
    ).astype(jnp.bfloat16)
    grad_features = replica_total(aggregate(back, tiles, slot_rows, slot_counts)).astype(
        jnp.bfloat16
    )
    return (activation, grad_weight, grad_features)


def solution(mesh):
    placed = (
        P(("blk", "rep"), None),
        P(),
        P(("blk", "rep"), None),
        P("blk", None, "rep", None),
        P("blk", None, "rep"),
        P("blk", None, "rep", None, None),
    )
    return jax.shard_map(
        shards,
        mesh=mesh,
        in_specs=placed,
        out_specs=(P(("blk", "rep"), None), P(), P(("blk", "rep"), None)),
        check_vma=False,
    )
```

profile of v0, /device:TPU:0, one launch (start us, length us, event | category | flops | bytes accessed | tf_op | source)
XLA Modules:
  0.0 249.7 jit_solution(9514217086973705413)
XLA Ops:
  7.2 0.7 copy-done.2
  8.0 11.6 %all_gather.6 = bf16[1024,256]{1,0:T(8,128)(2,1)S(1)} all-gather(bf16[128,256]{1,0:T(8,128)(2,1)} %param.14), channel_id=1, replica_groups=mesh['blk'=8,'rep'=4] {'blk'}, dimensions={0}, use_global_device_ids=true | all-gather | bytes 589824 | tf_op jit(solution)/shard_map/all_gather | solution.py:34
  19.6 0.6 copy-done.4
  20.3 37.8 %while.67 = (s32[]{:T(128)}, f32[512,256]{1,0:T(8,128)S(1)}, s32[8]{0:T(128)S(1)}, bf16[8,128,256]{2,1,0:T(8,128)(2,1)}, bf16[1024,256]{1,0:T(8,128)(2,1)S(1)}, ...) while((s32[]{:T(128)}, f32[512,256]{1,0:T(8,128)S(1)}, ...), condition=%wide.region_3.4_spmd, body=%wide.region_0.3_spmd.sunk | while | flops 8421395 | bytes 623234 | solution.py:41
  20.8 0.8 dynamic-slice_bitcast_fusion.4
  21.7 4.8 %while.70 = (s32[]{:T(128)}, f32[512,256]{1,0:T(8,128)S(1)}, s32[]{:T(128)}, s32[2]{0:T(128)S(1)}, bf16[128,256]{1,0:T(8,128)(2,1)S(1)}, /*index=5*/bf16[128,256...) while((s32[]{:T(128)}, f32[512,256]{1,0:T(8,128)S(1)}, ...), condition=%wide.region_2.2_spmd, body=%wide.region_1.1_spmd.sunk | while | flops 8421389 | bytes 360727 | solution.py:28
  22.4 0.6 dynamic_slice.120
  24.5 0.6 dynamic_slice.120
  27.1 0.8 dynamic-slice_bitcast_fusion.4
  28.0 2.7 %while.70 = (s32[]{:T(128)}, f32[512,256]{1,0:T(8,128)S(1)}, s32[]{:T(128)}, s32[2]{0:T(128)S(1)}, bf16[128,256]{1,0:T(8,128)(2,1)S(1)}, /*index=5*/bf16[128,256...) while((s32[]{:T(128)}, f32[512,256]{1,0:T(8,128)S(1)}, ...), condition=%wide.region_2.2_spmd, body=%wide.region_1.1_spmd.sunk | while | flops 8421389 | bytes 360727 | solution.py:28
  28.7 0.6 dynamic_slice.120
  31.3 0.8 dynamic-slice_bitcast_fusion.4
  32.2 2.7 %while.70 = (s32[]{:T(128)}, f32[512,256]{1,0:T(8,128)S(1)}, s32[]{:T(128)}, s32[2]{0:T(128)S(1)}, bf16[128,256]{1,0:T(8,128)(2,1)S(1)}, /*index=5*/bf16[128,256...) while((s32[]{:T(128)}, f32[512,256]{1,0:T(8,128)S(1)}, ...), condition=%wide.region_2.2_spmd, body=%wide.region_1.1_spmd.sunk | while | flops 8421389 | bytes 360727 | solution.py:28
  32.9 0.6 dynamic_slice.120
  35.6 0.8 dynamic-slice_bitcast_fusion.4
  36.4 2.7 %while.70 = (s32[]{:T(128)}, f32[512,256]{1,0:T(8,128)S(1)}, s32[]{:T(128)}, s32[2]{0:T(128)S(1)}, bf16[128,256]{1,0:T(8,128)(2,1)S(1)}, /*index=5*/bf16[128,256...) while((s32[]{:T(128)}, f32[512,256]{1,0:T(8,128)S(1)}, ...), condition=%wide.region_2.2_spmd, body=%wide.region_1.1_spmd.sunk | while | flops 8421389 | bytes 360727 | solution.py:28
  37.1 0.6 dynamic_slice.120
  39.8 0.8 dynamic-slice_bitcast_fusion.4
  40.6 4.8 %while.70 = (s32[]{:T(128)}, f32[512,256]{1,0:T(8,128)S(1)}, s32[]{:T(128)}, s32[2]{0:T(128)S(1)}, bf16[128,256]{1,0:T(8,128)(2,1)S(1)}, /*index=5*/bf16[128,256...) while((s32[]{:T(128)}, f32[512,256]{1,0:T(8,128)S(1)}, ...), condition=%wide.region_2.2_spmd, body=%wide.region_1.1_spmd.sunk | while | flops 8421389 | bytes 360727 | solution.py:28
  41.3 0.6 dynamic_slice.120
  43.4 0.6 dynamic_slice.120
  46.1 0.8 dynamic-slice_bitcast_fusion.4
  46.9 2.7 %while.70 = (s32[]{:T(128)}, f32[512,256]{1,0:T(8,128)S(1)}, s32[]{:T(128)}, s32[2]{0:T(128)S(1)}, bf16[128,256]{1,0:T(8,128)(2,1)S(1)}, /*index=5*/bf16[128,256...) while((s32[]{:T(128)}, f32[512,256]{1,0:T(8,128)S(1)}, ...), condition=%wide.region_2.2_spmd, body=%wide.region_1.1_spmd.sunk | while | flops 8421389 | bytes 360727 | solution.py:28
  50.3 0.8 dynamic-slice_bitcast_fusion.4
  51.1 2.7 %while.70 = (s32[]{:T(128)}, f32[512,256]{1,0:T(8,128)S(1)}, s32[]{:T(128)}, s32[2]{0:T(128)S(1)}, bf16[128,256]{1,0:T(8,128)(2,1)S(1)}, /*index=5*/bf16[128,256...) while((s32[]{:T(128)}, f32[512,256]{1,0:T(8,128)S(1)}, ...), condition=%wide.region_2.2_spmd, body=%wide.region_1.1_spmd.sunk | while | flops 8421389 | bytes 360727 | solution.py:28
  54.5 0.8 dynamic-slice_bitcast_fusion.4
  55.3 2.7 %while.70 = (s32[]{:T(128)}, f32[512,256]{1,0:T(8,128)S(1)}, s32[]{:T(128)}, s32[2]{0:T(128)S(1)}, bf16[128,256]{1,0:T(8,128)(2,1)S(1)}, /*index=5*/bf16[128,256...) while((s32[]{:T(128)}, f32[512,256]{1,0:T(8,128)S(1)}, ...), condition=%wide.region_2.2_spmd, body=%wide.region_1.1_spmd.sunk | while | flops 8421389 | bytes 360727 | solution.py:28
  58.1 0.7 convert_element_type.22
  58.9 32.2 %reduce-scatter.3.cloned.1.call-done = bf16[128,256]{1,0:T(8,128)(2,1)} async-done(((bf16[512,256]{1,0:T(8,128)(2,1)}), bf16[128,256]{1,0:T(8,128)(2,1)}) %reduce-scatter.3.cloned.1.call-update) | async-done | bytes 65552 | tf_op jit(solution)/shard_map/reduce_scatter | solution.py:10
  91.1 1.7 multiply_convert_fusion
  93.0 0.6 copy-done.1
  93.7 0.9 fusion.8
  94.6 9.9 %all_gather.7 = bf16[1024,256]{1,0:T(8,128)(2,1)S(1)} all-gather(bf16[128,256]{1,0:T(8,128)(2,1)S(1)} %convolution_convert_fusion), channel_id=1, replica_groups=mesh['blk'=8,'rep'=4] {'blk'}, dimensions={0}, use_global_device_ids=true | all-gather | bytes 589824 | tf_op jit(solution)/shard_map/all_gather | solution.py:34
  104.5 37.3 %while.69 = (s32[]{:T(128)}, f32[512,256]{1,0:T(8,128)S(1)}, s32[8]{0:T(128)S(1)}, bf16[8,128,256]{2,1,0:T(8,128)(2,1)}, bf16[1024,256]{1,0:T(8,128)(2,1)S(1)}, ...) while((s32[]{:T(128)}, f32[512,256]{1,0:T(8,128)S(1)}, ...), condition=%wide.region_9.10_spmd, body=%wide.region_6.9_spmd.sunk | while | flops 8421395 | bytes 623234 | solution.py:41
  105.2 0.8 dynamic-slice_bitcast_fusion.5
  106.0 4.7 %while.71 = (s32[]{:T(128)}, f32[512,256]{1,0:T(8,128)S(1)}, s32[]{:T(128)}, s32[2]{0:T(128)S(1)}, bf16[128,256]{1,0:T(8,128)(2,1)S(1)}, /*index=5*/bf16[128,256...) while((s32[]{:T(128)}, f32[512,256]{1,0:T(8,128)S(1)}, ...), condition=%wide.region_8.8_spmd, body=%wide.region_7.7_spmd.sunk | while | flops 8421389 | bytes 360727 | solution.py:28
  106.6 0.7 dynamic_slice.117
  108.7 0.7 dynamic_slice.117
  111.4 0.8 dynamic-slice_bitcast_fusion.5
  112.2 2.7 %while.71 = (s32[]{:T(128)}, f32[512,256]{1,0:T(8,128)S(1)}, s32[]{:T(128)}, s32[2]{0:T(128)S(1)}, bf16[128,256]{1,0:T(8,128)(2,1)S(1)}, /*index=5*/bf16[128,256...) while((s32[]{:T(128)}, f32[512,256]{1,0:T(8,128)S(1)}, ...), condition=%wide.region_8.8_spmd, body=%wide.region_7.7_spmd.sunk | while | flops 8421389 | bytes 360727 | solution.py:28
  112.8 0.7 dynamic_slice.117
  115.5 0.8 dynamic-slice_bitcast_fusion.5
  116.4 2.7 %while.71 = (s32[]{:T(128)}, f32[512,256]{1,0:T(8,128)S(1)}, s32[]{:T(128)}, s32[2]{0:T(128)S(1)}, bf16[128,256]{1,0:T(8,128)(2,1)S(1)}, /*index=5*/bf16[128,256...) while((s32[]{:T(128)}, f32[512,256]{1,0:T(8,128)S(1)}, ...), condition=%wide.region_8.8_spmd, body=%wide.region_7.7_spmd.sunk | while | flops 8421389 | bytes 360727 | solution.py:28
  117.0 0.7 dynamic_slice.117
  119.7 0.8 dynamic-slice_bitcast_fusion.5
  120.5 2.7 %while.71 = (s32[]{:T(128)}, f32[512,256]{1,0:T(8,128)S(1)}, s32[]{:T(128)}, s32[2]{0:T(128)S(1)}, bf16[128,256]{1,0:T(8,128)(2,1)S(1)}, /*index=5*/bf16[128,256...) while((s32[]{:T(128)}, f32[512,256]{1,0:T(8,128)S(1)}, ...), condition=%wide.region_8.8_spmd, body=%wide.region_7.7_spmd.sunk | while | flops 8421389 | bytes 360727 | solution.py:28
  121.1 0.7 dynamic_slice.117
  123.8 0.8 dynamic-slice_bitcast_fusion.5
  124.6 4.7 %while.71 = (s32[]{:T(128)}, f32[512,256]{1,0:T(8,128)S(1)}, s32[]{:T(128)}, s32[2]{0:T(128)S(1)}, bf16[128,256]{1,0:T(8,128)(2,1)S(1)}, /*index=5*/bf16[128,256...) while((s32[]{:T(128)}, f32[512,256]{1,0:T(8,128)S(1)}, ...), condition=%wide.region_8.8_spmd, body=%wide.region_7.7_spmd.sunk | while | flops 8421389 | bytes 360727 | solution.py:28
  125.2 0.7 dynamic_slice.117
  127.3 0.7 dynamic_slice.117
  130.0 0.8 dynamic-slice_bitcast_fusion.5
  130.9 2.7 %while.71 = (s32[]{:T(128)}, f32[512,256]{1,0:T(8,128)S(1)}, s32[]{:T(128)}, s32[2]{0:T(128)S(1)}, bf16[128,256]{1,0:T(8,128)(2,1)S(1)}, /*index=5*/bf16[128,256...) while((s32[]{:T(128)}, f32[512,256]{1,0:T(8,128)S(1)}, ...), condition=%wide.region_8.8_spmd, body=%wide.region_7.7_spmd.sunk | while | flops 8421389 | bytes 360727 | solution.py:28
  131.5 0.7 dynamic_slice.117
  134.1 0.8 dynamic-slice_bitcast_fusion.5
  135.0 2.7 %while.71 = (s32[]{:T(128)}, f32[512,256]{1,0:T(8,128)S(1)}, s32[]{:T(128)}, s32[2]{0:T(128)S(1)}, bf16[128,256]{1,0:T(8,128)(2,1)S(1)}, /*index=5*/bf16[128,256...) while((s32[]{:T(128)}, f32[512,256]{1,0:T(8,128)S(1)}, ...), condition=%wide.region_8.8_spmd, body=%wide.region_7.7_spmd.sunk | while | flops 8421389 | bytes 360727 | solution.py:28
  135.6 0.7 dynamic_slice.117
  138.3 0.8 dynamic-slice_bitcast_fusion.5
  139.1 2.7 %while.71 = (s32[]{:T(128)}, f32[512,256]{1,0:T(8,128)S(1)}, s32[]{:T(128)}, s32[2]{0:T(128)S(1)}, bf16[128,256]{1,0:T(8,128)(2,1)S(1)}, /*index=5*/bf16[128,256...) while((s32[]{:T(128)}, f32[512,256]{1,0:T(8,128)S(1)}, ...), condition=%wide.region_8.8_spmd, body=%wide.region_7.7_spmd.sunk | while | flops 8421389 | bytes 360727 | solution.py:28
  139.7 0.7 dynamic_slice.117
  141.8 0.7 convert_element_type.27
  142.6 79.0 %all-reduce.2.cloned.1.call-done = f32[256,256]{1,0:T(8,128)} async-done(((f32[256,256]{1,0:T(8,128)}), f32[256,256]{1,0:T(8,128)}) %all-reduce.2.cloned.1.call-update) | async-done | bytes 262160 | tf_op jit(solution)/shard_map/psum | solution.py:57
  221.6 1.7 broadcast_multiply_fusion
  223.2 20.0 %reduce-scatter.5.cloned.1.call-done = bf16[128,256]{1,0:T(8,128)(2,1)} async-done(((bf16[512,256]{1,0:T(8,128)(2,1)}), bf16[128,256]{1,0:T(8,128)(2,1)}) %reduce-scatter.5.cloned.1.call-update) | async-done | bytes 65552 | tf_op jit(solution)/shard_map/reduce_scatter | solution.py:10
  (88 shorter events, 15.0 us)
Async XLA Ops:
  7.2 84.0 %copy-start = (bf16[256,256]{1,0:T(8,128)(2,1)S(1)}, bf16[256,256]{1,0:T(8,128)(2,1)}, u32[]{:S(2)}) copy-start(bf16[256,256]{1,0:T(8,128)(2,1)} %param.15) | copy-start | bytes 393220
  7.2 83.9 %reduce-scatter.3.cloned.1.call-start = ((), (), s32[]{:S(2)}) async-start(), calls=%async_computation.2 | async-start | bytes 327680 | tf_op jit(solution)/shard_map/reduce_scatter | solution.py:10
  7.2 0.7 copy-start.2
  19.6 0.7 copy-start.4
  58.8 32.3 %copy-start.3 = (bf16[128,256]{1,0:T(8,128)(2,1)S(1)}, bf16[128,256]{1,0:T(8,128)(2,1)}, u32[]{:S(2)}) copy-start(bf16[128,256]{1,0:T(8,128)(2,1)} %param.16) | copy-start | bytes 196612
  58.8 162.7 %all-reduce.2.cloned.1.call-start = ((), (), s32[]{:S(2)}) async-start(), calls=%async_computation.3 | async-start | bytes 524288 | tf_op jit(solution)/shard_map/psum | solution.py:57
  92.8 0.8 copy-start.1
  94.6 148.6 %reduce-scatter.5.cloned.1.call-start = ((), (), s32[]{:S(2)}) async-start(), calls=%async_computation.4 | async-start | bytes 327680 | tf_op jit(solution)/shard_map/reduce_scatter | solution.py:10
Sparse Core Ops, SparseCore 0:
  59.0 32.1 reduce-scatter.2
  98.1 123.4 all-reduce.1
  224.5 18.6 reduce-scatter.4
where the time goes:
time: 252 us; the launch traced here: 250 us
  waiting for transfers between devices  131 us (52%)
  local copies, waits for them, and re-layouts  37.8 us (15%)
  loops' own time  36.4 us (14%)
  blocking collectives  21.4 us (8%)
  between operations  13.8 us (5%)
  matrix products  5.78 us (2%)
  other arithmetic  3.13 us (1%)
    psum x1, waiting for transfers between devices, shards(): grad_weight = lax.psum(local_grad, ('blk', 'rep')) / math.sqrt(node_count)  79 us
    reduce_scatter x2, waiting for transfers between devices, replica_total(): lax.psum_scatter(partial_value.astype(jnp.bfloat16), 'rep', scatter_dimen...  52.2 us
    another operation x16, loops' own time, add_tile(): return lax.fori_loop(0, count_now, one_slot, running)  35.9 us
    all_gather x2, blocking collectives, aggregate(): piece = lax.all_gather(node_slab, 'blk', axis=0, tiled=True)  21.4 us
    squeeze x16, local copies, waits for them, and re-layouts, add_tile(): tile_now = lax.dynamic_index_in_dim(tiles, column_block, 0, keepdims=False)  13.5 us
    dynamic_slice x20, local copies, waits for them, and re-layouts, one_slot(): first_row = rows_now[slot_index] * block_size  12.6 us
    dynamic_slice x16, local copies, waits for them, and re-layouts, add_tile(): lax.dynamic_index_in_dim(slot_counts, column_block, 0, keepdims=False)  9.44 us
  transfers between devices with their start and end apart: 3, of which 3 were waited for; matrix products, arithmetic and copies ran while one was open for 9% of the time, Pallas kernels for 0%

commit v1 on v0

v1 whole, which is shorter than its diff:
```python
import functools
import math

import jax
import jax.numpy as jnp
from jax import lax
from jax.experimental import pallas as pl
from jax.experimental.pallas import tpu as pltpu
from jax.sharding import PartitionSpec as P

F32 = jnp.float32
BF16 = jnp.bfloat16
VMEM_LIMIT = 8 * 1024 * 1024


def vmem():
    return pl.BlockSpec(memory_space=pltpu.VMEM)


def smem():
    return pl.BlockSpec(memory_space=pltpu.SMEM)


def params():
    return pltpu.CompilerParams(vmem_limit_bytes=VMEM_LIMIT)


def swap(value, axis, distance):
    size = lax.axis_size(axis)
    return lax.ppermute(value, axis, [(i, i ^ distance) for i in range(size)])


def dense_kernel(order, rows_ref, counts_ref, tiles_ref, out_ref):
    me, mine = lax.axis_index("blk"), lax.axis_index("rep")
    block = tiles_ref.shape[1]
    slots = tiles_ref.shape[2] // block
    subs = out_ref.shape[0] // block
    for q, distance in enumerate(order):
        slab = me ^ distance
        tile = tiles_ref[slab]
        places = [
            jnp.where(k < counts_ref[slab], rows_ref[slab, k] ^ mine, -1) for k in range(slots)
        ]
        for b in range(subs):
            value = jnp.zeros((block, block), tile.dtype)
            for k in range(slots):
                value = jnp.where(places[k] == b, tile[:, k * block : (k + 1) * block], value)
            out_ref[b * block : (b + 1) * block, q * block : (q + 1) * block] = value


def dense_adjacency(order, rows, counts, tiles):
    block = tiles.shape[1]
    shape = (lax.axis_size("rep") * block, len(order) * block)
    return pl.pallas_call(
        functools.partial(dense_kernel, order),
        out_shape=jax.ShapeDtypeStruct(shape, tiles.dtype),
        in_specs=[smem(), smem(), vmem()],
        out_specs=vmem(),
        compiler_params=params(),
        cost_estimate=pl.CostEstimate(flops=0, bytes_accessed=4 * tiles.size * 2, transcendentals=0),
    )(rows, counts, tiles)


def apply_kernel(n_pieces, dense_ref, *refs):
    pieces, outs = refs[:n_pieces], refs[n_pieces:]
    nodes = jnp.concatenate([piece[...] for piece in pieces], axis=0)
    block = outs[0].shape[0]
    for b in reversed(range(len(outs))):
        total = jnp.dot(
            dense_ref[b * block : (b + 1) * block, :], nodes, preferred_element_type=F32
        )
        outs[b][...] = total.astype(outs[b].dtype)


def apply_dense(dense, pieces):
    subs = lax.axis_size("rep")
    block, feat = dense.shape[0] // subs, pieces[0].shape[1]
    return pl.pallas_call(
        functools.partial(apply_kernel, len(pieces)),
        out_shape=[jax.ShapeDtypeStruct((block, feat), F32 if b == 0 else BF16) for b in range(subs)],
        in_specs=[vmem()] * (1 + len(pieces)),
        out_specs=[vmem()] * subs,
        compiler_params=params(),
        cost_estimate=pl.CostEstimate(
            flops=2 * dense.size * feat, bytes_accessed=2 * dense.size, transcendentals=0
        ),
    )(dense, *pieces)


def layer_kernel(n_parts, node_count, *refs):
    parts, (weight_ref, cotangent_ref, activation_ref, back_ref, grad_ref) = refs[:n_parts], refs[n_parts:]
    total = parts[0][...]
    for part in parts[1:]:
        total = total + part[...].astype(F32)
    agg = total.astype(BF16)
    weight = weight_ref[...]
    pre = jnp.dot(agg, weight, preferred_element_type=F32)
    sig = 1.0 / (1.0 + jnp.exp(-pre))
    activation_ref[...] = (pre * sig).astype(BF16)
    dpre = (cotangent_ref[...].astype(F32) * sig * (1.0 + pre * (1.0 - sig))).astype(BF16)
    back = lax.dot_general(dpre, weight, (((1,), (1,)), ((), ())), preferred_element_type=F32)
    back_ref[...] = back.astype(BF16)
    grad = lax.dot_general(agg, dpre, (((0,), (0,)), ((), ())), preferred_element_type=F32)
    grad_ref[...] = (grad * (1.0 / math.sqrt(node_count))).astype(grad_ref.dtype)


def layer(parts, weight, cotangent, node_count):
    block, feat = cotangent.shape
    small = jax.ShapeDtypeStruct((block, feat), BF16)
    return pl.pallas_call(
        functools.partial(layer_kernel, len(parts), node_count),
        out_shape=[small, small, jax.ShapeDtypeStruct((feat, feat), BF16)],
        in_specs=[vmem()] * (len(parts) + 2),
        out_specs=[vmem()] * 3,
        compiler_params=params(),
        cost_estimate=pl.CostEstimate(
            flops=6 * block * feat * feat, bytes_accessed=block * feat * 16, transcendentals=block * feat
        ),
    )(*parts, weight, cotangent)


def gather_direct(piece):
    size = lax.axis_size("blk")
    far = {d: swap(piece, "blk", d) for d in reversed(range(2, size, 2))}
    near = swap(piece, "blk", 1)
    mine = [far[d] for d in range(2, size, 2)]
    if not mine:
        return [piece, near]
    other = swap(jnp.concatenate(mine, axis=0), "blk", 1)
    return [piece, near] + mine + [other]


def gather_order(size):
    far = list(range(2, size, 2))
    return [0, 1] + far + [d + 1 for d in far]


def reduce_direct(parts):
    moved = {b: swap(parts[b], "rep", b) for b in reversed(range(1, len(parts)))}
    return [parts[0]] + [moved[b] for b in range(1, len(parts))]


def total_direct(value):
    for axis in ("blk", "rep"):
        distance = 1
        while distance < lax.axis_size(axis):
            value = lax.optimization_barrier(value)
            other = swap(value, axis, distance)
            value = value.astype(F32) + other.astype(F32)
            distance *= 2
            if not (axis == "rep" and distance >= lax.axis_size(axis)):
                value = value.astype(BF16)
    return value


def shards_direct(features, weight, cotangent, rows, counts, tiles):
    slabs = lax.axis_size("blk")
    node_count = features.shape[0] * slabs * lax.axis_size("rep")
    dense = dense_adjacency(gather_order(slabs), rows, counts, tiles)
    parts = reduce_direct(apply_dense(dense, gather_direct(features)))
    activation, back, grad = layer(parts, weight, cotangent, node_count)
    grad_weight = total_direct(grad)
    parts = reduce_direct(apply_dense(dense, gather_direct(back)))
    grad_features = parts[0]
    for part in parts[1:]:
        grad_features = grad_features + part.astype(F32)
    return activation, grad_weight.astype(F32), grad_features.astype(BF16)


def add_tile(running, column_block, node_slab, tiles, slot_rows, slot_counts):
    block_size = node_slab.shape[0]
    tile_now = lax.dynamic_index_in_dim(tiles, column_block, 0, keepdims=False)
    rows_now = lax.dynamic_index_in_dim(slot_rows, column_block, 0, keepdims=False)
    count_now = lax.dynamic_index_in_dim(slot_counts, column_block, 0, keepdims=False)

    def one_slot(slot_index, carried):
        weights_now = lax.dynamic_slice_in_dim(tile_now, slot_index * block_size, block_size, 1)
        product = jnp.dot(weights_now, node_slab, preferred_element_type=F32)
        first_row = rows_now[slot_index] * block_size
        current = lax.dynamic_slice_in_dim(carried, first_row, block_size, 0)
        return lax.dynamic_update_slice_in_dim(carried, current + product, first_row, 0)

    return lax.fori_loop(0, count_now, one_slot, running)


def aggregate(node_slab, tiles, slot_rows, slot_counts):
    block_size = node_slab.shape[0]
    running = jnp.zeros((block_size * lax.axis_size("rep"), node_slab.shape[1]), F32)
    piece = lax.all_gather(node_slab, "blk", axis=0, tiled=True)
    piece_count = piece.shape[0] // block_size

    def one_piece(inner, running_now):
        slab_now = lax.dynamic_slice_in_dim(piece, inner * block_size, block_size, 0)
        return add_tile(running_now, inner, slab_now, tiles, slot_rows, slot_counts)

    total = lax.fori_loop(0, piece_count, one_piece, running)
    return lax.psum_scatter(total.astype(BF16), "rep", scatter_dimension=0, tiled=True)


def shards_general(features, weight, cotangent, rows, counts, tiles):
    agg = aggregate(features, tiles, rows, counts)
    pre = jnp.dot(agg, weight, preferred_element_type=F32)
    sig = jax.nn.sigmoid(pre)
    activation = (pre * sig).astype(BF16)
    dpre = (cotangent.astype(F32) * sig * (1.0 + pre * (1.0 - sig))).astype(BF16)
    local_grad = lax.dot_general(agg, dpre, (((0,), (0,)), ((), ())), preferred_element_type=F32)
    node_count = features.shape[0] * lax.axis_size("blk") * lax.axis_size("rep")
    grad_weight = lax.psum(local_grad, ("blk", "rep")) / math.sqrt(node_count)
    back = lax.dot_general(dpre, weight, (((1,), (1,)), ((), ())), preferred_element_type=F32)
    return activation, grad_weight, aggregate(back.astype(BF16), tiles, rows, counts)


def shards(features, weight, cotangent, block_rows, block_counts, block_values):
    tiles = block_values[0, :, 0]
    rows = block_rows[0, :, 0]
    counts = block_counts[0, :, 0]
    sizes = lax.axis_size("blk"), lax.axis_size("rep")
    direct = all(size & (size - 1) == 0 for size in sizes) and sizes[0] <= 8 and sizes[1] <= 4
    return (shards_direct if direct else shards_general)(
        features, weight, cotangent, rows, counts, tiles
    )


def solution(mesh):
    placed = (
        P(("blk", "rep"), None),
        P(),
        P(("blk", "rep"), None),
        P("blk", None, "rep", None),
        P("blk", None, "rep"),
        P("blk", None, "rep", None, None),
    )
    return jax.shard_map(
        shards,
        mesh=mesh,
        in_specs=placed,
        out_specs=(P(("blk", "rep"), None), P(), P(("blk", "rep"), None)),
        check_vma=False,
    )
```

time: 252 us -> 58 us (0.23)
  waiting for transfers between devices: 131 us -> 30.5 us
  loops' own time: 36.4 us -> 0 us
  local copies, waits for them, and re-layouts: 37.8 us -> 1.89 us
  blocking collectives: 21.4 us -> 0 us
  starting transfers between devices: 0.12 us -> 20.4 us
  between operations: 13.8 us -> 0.77 us
  matrix products: 5.78 us -> 0 us
  Pallas kernels: 0 us -> 2.66 us
    psum x1 -> x0, waiting for transfers between devices: 79 us -> none  [shards(): grad_weight = lax.psum(local_grad, ('blk', 'rep')) / math.sqrt(node_count)]
    reduce_scatter x2 -> x0, waiting for transfers between devices: 52.2 us -> none  [replica_total(): lax.psum_scatter(partial_value.astype(jnp.bfloat16), 'rep', scatter_dimen...]
    another operation x18 -> x0, loops' own time: 36.4 us -> none  [the longest x16 35.9 us: add_tile(): return lax.fori_loop(0, count_now, one_slot, running)]
    ppermute x0 -> x21, waiting for transfers between devices: none -> 30.5 us  [swap(): return lax.ppermute(value, axis, [(i, i ^ distance) for i in range(size)])]
    dynamic_slice x52 -> x0, local copies, waits for them, and re-layouts: 22.1 us -> none  [the longest x20 12.6 us: one_slot(): first_row = rows_now[slot_index] * block_size]
    all_gather x2 -> x0, blocking collectives: 21.4 us -> none  [aggregate(): piece = lax.all_gather(node_slab, 'blk', axis=0, tiled=True)]
    ppermute x0 -> x21, starting transfers between devices: none -> 20.4 us  [swap(): return lax.ppermute(value, axis, [(i, i ^ distance) for i in range(size)])]
    squeeze x32 -> x1, local copies, waits for them, and re-layouts: 13.6 us -> 0.08 us  [shards(): rows = block_rows[0, :, 0]]
  transfers between devices with their start and end apart: 3 -> 21, of which waited for: 3 -> 13; matrix products, arithmetic and copies ran while one was open for 9% -> 1% of each run, Pallas kernels for 0% -> 2%
where the time goes in v1:
time: 58 us; the launch traced here: 57.8 us
  waiting for transfers between devices  30.5 us (53%)
  starting transfers between devices  20.4 us (35%)
  Pallas kernels  2.66 us (5%)
  local copies, waits for them, and re-layouts  1.89 us (3%)
  other arithmetic  1.55 us (3%)
  between operations  0.77 us (1%)
    ppermute x21, waiting for transfers between devices, swap(): return lax.ppermute(value, axis, [(i, i ^ distance) for i in range(size)])  30.5 us
    ppermute x21, starting transfers between devices, swap(): return lax.ppermute(value, axis, [(i, i ^ distance) for i in range(size)])  20.4 us
    unnamed x12, local copies, waits for them, and re-layouts  1.81 us
  transfers between devices with their start and end apart: 21, of which 13 were waited for; matrix products, arithmetic and copies ran while one was open for 1% of the time, Pallas kernels for 2%

profile of v1, /device:TPU:0, one launch (start us, length us, event | category | flops | bytes accessed | tf_op | source)
XLA Modules:
  0.0 57.8 jit_solution(16511015924337721181)
XLA Ops:
  0.6 0.0 copy-start.2
  0.6 3.0 %collective-permute-start.1 = (bf16[128,256]{1,0:T(8,128)(2,1)}, bf16[128,256]{1,0:T(8,128)(2,1)S(1)}, u32[]{:S(2)}, u32[]{:S(2)}) collective-permute-start(bf16[128,256]{1,0:T(8,128)(2,1)} %refs_0_.1), channel_id=1, source_target_pairs={{0,8},{4,12},{8,0},{12,4},{16,24},{20,28},{24,16},{28,20},{1,9},{5... | collective-permute-start | bytes 196616 | tf_op jit(solution)/shard_map/ppermute | solution.py:30
  3.6 1.5 %collective-permute-start.2 = (bf16[128,256]{1,0:T(8,128)(2,1)}, bf16[128,256]{1,0:T(8,128)(2,1)S(1)}, u32[]{:S(2)}, u32[]{:S(2)}) collective-permute-start(bf16[128,256]{1,0:T(8,128)(2,1)} %refs_0_.1), channel_id=1, source_target_pairs={{0,16},{4,20},{8,24},{12,28},{16,0},{20,4},{24,8},{28,12},{1,17},{... | collective-permute-start | bytes 196616 | tf_op jit(solution)/shard_map/ppermute | solution.py:30
  5.2 0.0 collective-permute-start.3
  5.2 1.1 %collective-permute-done.1.refs_2_ = bf16[128,256]{1,0:T(8,128)(2,1)S(1)} collective-permute-done((bf16[128,256]{1,0:T(8,128)(2,1)}, bf16[128,256]{1,0:T(8,128)(2,1)S(1)}, u32[]{:S(2)}, u32[]{:S(2)}) %collective-permute-start.1) | collective-permute-done | bytes 65568 | tf_op jit(solution)/shard_map/ppermute | solution.py:30
  6.3 1.8 %collective-permute-done.2.refs_3_ = bf16[128,256]{1,0:T(8,128)(2,1)S(1)} collective-permute-done((bf16[128,256]{1,0:T(8,128)(2,1)}, bf16[128,256]{1,0:T(8,128)(2,1)S(1)}, u32[]{:S(2)}, u32[]{:S(2)}) %collective-permute-start.2) | collective-permute-done | bytes 65568 | tf_op jit(solution)/shard_map/ppermute | solution.py:30
  8.1 2.4 %collective-permute-done.3.refs_4_ = bf16[128,256]{1,0:T(8,128)(2,1)S(1)} collective-permute-done((bf16[128,256]{1,0:T(8,128)(2,1)}, bf16[128,256]{1,0:T(8,128)(2,1)S(1)}, u32[]{:S(2)}, u32[]{:S(2)}) %collective-permute-start.3) | collective-permute-done | bytes 65568 | tf_op jit(solution)/shard_map/ppermute | solution.py:30
  10.6 0.0 copy-start.5
  10.6 0.1 collective-permute-start.4
  10.6 0.0 copy-done.2
  10.7 0.5 collective-permute-start
  11.1 0.1 copy-done.5
  11.2 0.1 copy.9.rows_ref
  11.3 0.0 copy-start.4
  11.3 0.7 %copy-done.4 = s32[1,8,1]{1,2,0:T(1,128)S(1)} copy-done((s32[1,8,1]{1,2,0:T(1,128)S(1)}, s32[1,8,1]{1,2,0:T(1,128)}, u32[]{:S(2)}) %copy-start.4) | copy-done | bytes 56
  12.0 0.0 copy-start
  12.0 1.0 %copy-done = bf16[1,8,1,128,256]{4,3,2,1,0:T(8,128)(2,1)S(1)} copy-done((bf16[1,8,1,128,256]{4,3,2,1,0:T(8,128)(2,1)S(1)}, bf16[1,8,1,128,256]{4,3,2,1,0:T(8,128)(2,1)}, u32[]{:S(2)}) %copy-start) | copy-done | bytes 524312
  13.0 0.9 %shard_map.85.dense_ref = bf16[512,1024]{1,0:T(8,128)(2,1)S(1)} custom-call(s32[8,2]{1,0:T(8,128)S(1)} %copy.9.rows_ref, s32[8]{0:T(128)S(1)} %bitcast.4, bf16[8,128,256]{2,1,0:T(8,128)(2,1)S(1)} %bitcast.3), custom_call_target="tpu_custom_call" | custom-call | bytes 2097152 | tf_op jit(solution)/shard_map/pallas_call | solution.py:54
  13.9 0.0 copy-start.1
  13.9 0.0 copy-start.3
  14.0 0.0 collective-permute-done.refs_1_
  14.0 0.0 collective-permute-done.4.refs_5_
  14.0 0.5 shard_map.86
  14.4 1.6 %collective-permute-start.5 = (bf16[128,256]{1,0:T(8,128)(2,1)S(1)}, bf16[128,256]{1,0:T(8,128)(2,1)S(1)}, u32[]{:S(2)}, u32[]{:S(2)}) collective-permute-start(bf16[128,256]{1,0:T(8,128)(2,1)S(1)} %get-tuple-element.15), channel_id=1, source_target_pairs={{0,1},{1,0},{2,3},{3,2},{4,5},{5,4},{6,7},{7,6},{8,9},{9,8},{10,11... | collective-permute-start | bytes 196616 | tf_op jit(solution)/shard_map/ppermute | solution.py:30
  16.1 2.6 %collective-permute-start.6 = (bf16[128,256]{1,0:T(8,128)(2,1)S(1)}, bf16[128,256]{1,0:T(8,128)(2,1)S(1)}, u32[]{:S(2)}, u32[]{:S(2)}) collective-permute-start(bf16[128,256]{1,0:T(8,128)(2,1)S(1)} %get-tuple-element.16), channel_id=1, source_target_pairs={{0,2},{1,3},{2,0},{3,1},{4,6},{5,7},{6,4},{7,5},{8,10},{9,11},{10,... | collective-permute-start | bytes 196616 | tf_op jit(solution)/shard_map/ppermute | solution.py:30
  18.7 0.2 collective-permute-start.7
  18.9 0.0 collective-permute-done.5.refs_1_
  18.9 4.7 %collective-permute-done.6.refs_2_ = bf16[128,256]{1,0:T(8,128)(2,1)S(1)} collective-permute-done((bf16[128,256]{1,0:T(8,128)(2,1)S(1)}, bf16[128,256]{1,0:T(8,128)(2,1)S(1)}, u32[]{:S(2)}, u32[]{:S(2)}) %collective-permute-start.6) | collective-permute-done | bytes 65568 | tf_op jit(solution)/shard_map/ppermute | solution.py:30
  23.5 1.3 %collective-permute-done.7.refs_3_ = bf16[128,256]{1,0:T(8,128)(2,1)S(1)} collective-permute-done((bf16[128,256]{1,0:T(8,128)(2,1)S(1)}, bf16[128,256]{1,0:T(8,128)(2,1)S(1)}, u32[]{:S(2)}, u32[]{:S(2)}) %collective-permute-start.7) | collective-permute-done | bytes 65568 | tf_op jit(solution)/shard_map/ppermute | solution.py:30
  24.8 0.0 copy-done.1
  24.8 0.0 copy-done.3
  24.8 0.8 %shard_map.87 = (bf16[128,256]{1,0:T(8,128)(2,1)}, bf16[128,256]{1,0:T(8,128)(2,1)S(1)}, bf16[256,256]{1,0:T(8,128)(2,1)S(1)}) custom-call(f32[128,256]{1,0:T(8,128)S(1)} %get-tuple-element.14.refs_0_, bf16[128,256]{1,0:T(8,128)(2,1)S(1)} %collective-permute-done.5.refs_1_, bf16[128,256]{1,0:T(8,128)(2,1)S(1)} %collective-permute-done.6.refs_2_, ...), custom_call_target="tpu_custom_call" | custom-call | flops 50331648 | bytes 524288 | tf_op jit(solution)/shard_map/pallas_call | solution.py:110
  25.7 0.0 collective-permute-start.8
  25.7 1.3 %collective-permute-done.8 = bf16[256,256]{1,0:T(8,128)(2,1)S(1)} collective-permute-done((bf16[256,256]{1,0:T(8,128)(2,1)S(1)}, bf16[256,256]{1,0:T(8,128)(2,1)S(1)}, u32[]{:S(2)}, u32[]{:S(2)}) %collective-permute-start.8) | collective-permute-done | bytes 131104 | tf_op jit(solution)/shard_map/ppermute | solution.py:30
  27.1 0.6 %collective-permute-start.9 = (bf16[256,256]{1,0:T(8,128)(2,1)S(1)}, bf16[256,256]{1,0:T(8,128)(2,1)S(1)}, u32[]{:S(2)}, u32[]{:S(2)}) collective-permute-start(bf16[256,256]{1,0:T(8,128)(2,1)S(1)} %add_convert_fusion.3), channel_id=1, source_target_pairs={{0,8},{4,12},{8,0},{12,4},{16,24},{20,28},{24,16},{28,20},{1,9},{5... | collective-permute-start | bytes 393224 | tf_op jit(solution)/shard_map/ppermute | solution.py:30
  27.7 1.5 %collective-permute-start.14 = (bf16[128,256]{1,0:T(8,128)(2,1)S(1)}, bf16[128,256]{1,0:T(8,128)(2,1)S(1)}, u32[]{:S(2)}, u32[]{:S(2)}) collective-permute-start(bf16[128,256]{1,0:T(8,128)(2,1)S(1)} %get-tuple-element.20.refs_0_), channel_id=1, source_target_pairs={{0,8},{4,12},{8,0},{12,4},{16,24},{20,28},{24,16},{28,20},{1,9},{5... | collective-permute-start | bytes 196616 | tf_op jit(solution)/shard_map/ppermute | solution.py:30
  29.2 0.5 collective-permute-start.15
  29.7 1.5 %collective-permute-start.16 = (bf16[128,256]{1,0:T(8,128)(2,1)S(1)}, bf16[128,256]{1,0:T(8,128)(2,1)S(1)}, u32[]{:S(2)}, u32[]{:S(2)}) collective-permute-start(bf16[128,256]{1,0:T(8,128)(2,1)S(1)} %get-tuple-element.20.refs_0_), channel_id=1, source_target_pairs={{0,24},{4,28},{8,16},{12,20},{16,8},{20,12},{24,0},{28,4},{1,25},{... | collective-permute-start | bytes 196616 | tf_op jit(solution)/shard_map/ppermute | solution.py:30
  31.2 2.3 %collective-permute-done.9 = bf16[256,256]{1,0:T(8,128)(2,1)S(1)} collective-permute-done((bf16[256,256]{1,0:T(8,128)(2,1)S(1)}, bf16[256,256]{1,0:T(8,128)(2,1)S(1)}, u32[]{:S(2)}, u32[]{:S(2)}) %collective-permute-start.9) | collective-permute-done | bytes 131104 | tf_op jit(solution)/shard_map/ppermute | solution.py:30
  33.5 0.6 collective-permute-start.10
  34.1 0.7 %collective-permute-done.14.refs_2_ = bf16[128,256]{1,0:T(8,128)(2,1)S(1)} collective-permute-done((bf16[128,256]{1,0:T(8,128)(2,1)S(1)}, bf16[128,256]{1,0:T(8,128)(2,1)S(1)}, u32[]{:S(2)}, u32[]{:S(2)}) %collective-permute-start.14) | collective-permute-done | bytes 65568 | tf_op jit(solution)/shard_map/ppermute | solution.py:30
  34.8 0.0 collective-permute-done.15.refs_3_
  34.8 0.7 %collective-permute-done.16.refs_4_ = bf16[128,256]{1,0:T(8,128)(2,1)S(1)} collective-permute-done((bf16[128,256]{1,0:T(8,128)(2,1)S(1)}, bf16[128,256]{1,0:T(8,128)(2,1)S(1)}, u32[]{:S(2)}, u32[]{:S(2)}) %collective-permute-start.16) | collective-permute-done | bytes 65568 | tf_op jit(solution)/shard_map/ppermute | solution.py:30
  35.6 0.1 collective-permute-start.17
  35.6 2.9 %collective-permute-done.10 = bf16[256,256]{1,0:T(8,128)(2,1)S(1)} collective-permute-done((bf16[256,256]{1,0:T(8,128)(2,1)S(1)}, bf16[256,256]{1,0:T(8,128)(2,1)S(1)}, u32[]{:S(2)}, u32[]{:S(2)}) %collective-permute-start.10) | collective-permute-done | bytes 131104 | tf_op jit(solution)/shard_map/ppermute | solution.py:30
  38.6 0.8 %collective-permute-start.11 = (bf16[256,256]{1,0:T(8,128)(2,1)S(1)}, bf16[256,256]{1,0:T(8,128)(2,1)S(1)}, u32[]{:S(2)}, u32[]{:S(2)}) collective-permute-start(bf16[256,256]{1,0:T(8,128)(2,1)S(1)} %add_convert_fusion.1), channel_id=1, source_target_pairs={{0,1},{1,0},{2,3},{3,2},{4,5},{5,4},{6,7},{7,6},{8,9},{9,8},{10,11... | collective-permute-start | bytes 393224 | tf_op jit(solution)/shard_map/ppermute | solution.py:30
  39.4 0.0 collective-permute-start.13
  39.4 1.3 %collective-permute-done.13.refs_1_ = bf16[128,256]{1,0:T(8,128)(2,1)S(1)} collective-permute-done((bf16[128,256]{1,0:T(8,128)(2,1)S(1)}, bf16[128,256]{1,0:T(8,128)(2,1)S(1)}, u32[]{:S(2)}, u32[]{:S(2)}) %collective-permute-start.13) | collective-permute-done | bytes 65568 | tf_op jit(solution)/shard_map/ppermute | solution.py:30
  40.6 0.0 collective-permute-done.17.refs_5_
  40.6 0.4 shard_map.88
  41.1 1.4 %collective-permute-start.18 = (bf16[128,256]{1,0:T(8,128)(2,1)S(1)}, bf16[128,256]{1,0:T(8,128)(2,1)S(1)}, u32[]{:S(2)}, u32[]{:S(2)}) collective-permute-start(bf16[128,256]{1,0:T(8,128)(2,1)S(1)} %get-tuple-element.22), channel_id=1, source_target_pairs={{0,1},{1,0},{2,3},{3,2},{4,5},{5,4},{6,7},{7,6},{8,9},{9,8},{10,11... | collective-permute-start | bytes 196616 | tf_op jit(solution)/shard_map/ppermute | solution.py:30
  42.5 1.7 %collective-permute-start.19 = (bf16[128,256]{1,0:T(8,128)(2,1)S(1)}, bf16[128,256]{1,0:T(8,128)(2,1)S(1)}, u32[]{:S(2)}, u32[]{:S(2)}) collective-permute-start(bf16[128,256]{1,0:T(8,128)(2,1)S(1)} %get-tuple-element.23), channel_id=1, source_target_pairs={{0,2},{1,3},{2,0},{3,1},{4,6},{5,7},{6,4},{7,5},{8,10},{9,11},{10,... | collective-permute-start | bytes 196616 | tf_op jit(solution)/shard_map/ppermute | solution.py:30
  44.2 1.4 %collective-permute-start.20 = (bf16[128,256]{1,0:T(8,128)(2,1)S(1)}, bf16[128,256]{1,0:T(8,128)(2,1)S(1)}, u32[]{:S(2)}, u32[]{:S(2)}) collective-permute-start(bf16[128,256]{1,0:T(8,128)(2,1)S(1)} %get-tuple-element.24), channel_id=1, source_target_pairs={{0,3},{1,2},{2,1},{3,0},{4,7},{5,6},{6,5},{7,4},{8,11},{9,10},{10,... | collective-permute-start | bytes 196616 | tf_op jit(solution)/shard_map/ppermute | solution.py:30
  45.6 0.0 collective-permute-done.11
  45.6 0.9 %collective-permute-start.12 = (bf16[256,256]{1,0:T(8,128)(2,1)S(1)}, bf16[256,256]{1,0:T(8,128)(2,1)S(1)}, u32[]{:S(2)}, u32[]{:S(2)}) collective-permute-start(bf16[256,256]{1,0:T(8,128)(2,1)S(1)} %add_convert_fusion), channel_id=1, source_target_pairs={{0,2},{1,3},{2,0},{3,1},{4,6},{5,7},{6,4},{7,5},{8,10},{9,11},{10,... | collective-permute-start | bytes 393224 | tf_op jit(solution)/shard_map/ppermute | solution.py:30
  46.5 0.0 collective-permute-done.18
  46.5 7.0 %collective-permute-done.19 = bf16[128,256]{1,0:T(8,128)(2,1)S(1)} collective-permute-done((bf16[128,256]{1,0:T(8,128)(2,1)S(1)}, bf16[128,256]{1,0:T(8,128)(2,1)S(1)}, u32[]{:S(2)}, u32[]{:S(2)}) %collective-permute-start.19) | collective-permute-done | bytes 65568 | tf_op jit(solution)/shard_map/ppermute | solution.py:30
  53.5 0.0 collective-permute-done.20
  53.5 0.7 %add_convert_fusion.4 = bf16[128,256]{1,0:T(8,128)(2,1)} fusion(bf16[128,256]{1,0:T(8,128)(2,1)S(1)} %collective-permute-done.20, bf16[128,256]{1,0:T(8,128)(2,1)S(1)} %collective-permute-done.19, f32[128,256]{1,0:T(8,128)S(1)} %get-tuple-element.21, bf16[128,256]{1,0:T(8,128)(2,1)S(1)} %collective-permute-done.18), kind=kLoop, calls=%fused_computation.7 | loop fusion | flops 229376 | bytes 393216 | tf_op jit(solution)/shard_map/convert_element_type | solution.py:167
  54.2 2.9 %collective-permute-done.12 = bf16[256,256]{1,0:T(8,128)(2,1)S(1)} collective-permute-done((bf16[256,256]{1,0:T(8,128)(2,1)S(1)}, bf16[256,256]{1,0:T(8,128)(2,1)S(1)}, u32[]{:S(2)}, u32[]{:S(2)}) %collective-permute-start.12) | collective-permute-done | bytes 131104 | tf_op jit(solution)/shard_map/ppermute | solution.py:30
  57.1 0.7 %convert_add_fusion = f32[256,256]{1,0:T(8,128)} fusion(bf16[256,256]{1,0:T(8,128)(2,1)S(1)} %collective-permute-done.12, bf16[256,256]{1,0:T(8,128)(2,1)S(1)} %add_convert_fusion), kind=kLoop, calls=%fused_computation | loop fusion | flops 196608 | bytes 524288 | tf_op jit(solution)/shard_map/add | solution.py:149
  (6 shorter events, 0.2 us)
Async XLA Ops:
  0.6 10.0 %copy-start.2 = (bf16[128,256]{1,0:T(8,128)(2,1)S(1)}, bf16[128,256]{1,0:T(8,128)(2,1)}, u32[]{:S(2)}) copy-start(bf16[128,256]{1,0:T(8,128)(2,1)} %refs_0_.1) | copy-start | bytes 196612
  0.6 5.7 %collective-permute-start.1 = (bf16[128,256]{1,0:T(8,128)(2,1)}, bf16[128,256]{1,0:T(8,128)(2,1)S(1)}, u32[]{:S(2)}, u32[]{:S(2)}) collective-permute-start(bf16[128,256]{1,0:T(8,128)(2,1)} %refs_0_.1), channel_id=1, source_target_pairs={{0,8},{4,12},{8,0},{12,4},{16,24},{20,28},{24,16},{28,20},{1,9},{5... | collective-permute-start | bytes 196616 | tf_op jit(solution)/shard_map/ppermute | solution.py:30
  3.6 4.5 %collective-permute-start.2 = (bf16[128,256]{1,0:T(8,128)(2,1)}, bf16[128,256]{1,0:T(8,128)(2,1)S(1)}, u32[]{:S(2)}, u32[]{:S(2)}) collective-permute-start(bf16[128,256]{1,0:T(8,128)(2,1)} %refs_0_.1), channel_id=1, source_target_pairs={{0,16},{4,20},{8,24},{12,28},{16,0},{20,4},{24,8},{28,12},{1,17},{... | collective-permute-start | bytes 196616 | tf_op jit(solution)/shard_map/ppermute | solution.py:30
  5.2 5.4 %collective-permute-start.3 = (bf16[128,256]{1,0:T(8,128)(2,1)}, bf16[128,256]{1,0:T(8,128)(2,1)S(1)}, u32[]{:S(2)}, u32[]{:S(2)}) collective-permute-start(bf16[128,256]{1,0:T(8,128)(2,1)} %refs_0_.1), channel_id=1, source_target_pairs={{0,24},{4,28},{8,16},{12,20},{16,8},{20,12},{24,0},{28,4},{1,25},{... | collective-permute-start | bytes 196616 | tf_op jit(solution)/shard_map/ppermute | solution.py:30
  10.6 0.7 %copy-start.5 = (s32[1,8,1,2]{1,3,2,0:T(2,128)S(1)}, s32[1,8,1,2]{1,3,2,0:T(2,128)}, u32[]{:S(2)}) copy-start(s32[1,8,1,2]{1,3,2,0:T(2,128)} %param.9) | copy-start | bytes 196
  10.6 3.4 %collective-permute-start.4 = (bf16[384,256]{1,0:T(8,128)(2,1)S(1)}, bf16[384,256]{1,0:T(8,128)(2,1)S(1)}, u32[]{:S(2)}, u32[]{:S(2)}) collective-permute-start(bf16[384,256]{1,0:T(8,128)(2,1)S(1)} %pad_maximum_fusion), channel_id=1, source_target_pairs={{0,4},{4,0},{8,12},{12,8},{16,20},{20,16},{24,28},{28,24},{1,5},{5... | collective-permute-start | bytes 589832 | tf_op jit(solution)/shard_map/ppermute | solution.py:30
  10.7 3.3 %collective-permute-start = (bf16[128,256]{1,0:T(8,128)(2,1)S(1)}, bf16[128,256]{1,0:T(8,128)(2,1)S(1)}, u32[]{:S(2)}, u32[]{:S(2)}) collective-permute-start(bf16[128,256]{1,0:T(8,128)(2,1)S(1)} %copy-done.2), channel_id=1, source_target_pairs={{0,4},{4,0},{8,12},{12,8},{16,20},{20,16},{24,28},{28,24},{1,5},{5... | collective-permute-start | bytes 196616 | tf_op jit(solution)/shard_map/ppermute | solution.py:30
  11.3 0.7 %copy-start.4 = (s32[1,8,1]{1,2,0:T(1,128)S(1)}, s32[1,8,1]{1,2,0:T(1,128)}, u32[]{:S(2)}) copy-start(s32[1,8,1]{1,2,0:T(1,128)} %param.10) | copy-start | bytes 100
  12.0 1.0 %copy-start = (bf16[1,8,1,128,256]{4,3,2,1,0:T(8,128)(2,1)S(1)}, bf16[1,8,1,128,256]{4,3,2,1,0:T(8,128)(2,1)}, u32[]{:S(2)}) copy-start(bf16[1,8,1,128,256]{4,3,2,1,0:T(8,128)(2,1)} %param.11) | copy-start | bytes 1572868
  13.9 10.9 %copy-start.1 = (bf16[256,256]{1,0:T(8,128)(2,1)S(1)}, bf16[256,256]{1,0:T(8,128)(2,1)}, u32[]{:S(2)}) copy-start(bf16[256,256]{1,0:T(8,128)(2,1)} %refs_4_.1) | copy-start | bytes 393220
  13.9 10.9 %copy-start.3 = (bf16[128,256]{1,0:T(8,128)(2,1)S(1)}, bf16[128,256]{1,0:T(8,128)(2,1)}, u32[]{:S(2)}) copy-start(bf16[128,256]{1,0:T(8,128)(2,1)} %refs_5_.1) | copy-start | bytes 196612
  14.4 4.5 %collective-permute-start.5 = (bf16[128,256]{1,0:T(8,128)(2,1)S(1)}, bf16[128,256]{1,0:T(8,128)(2,1)S(1)}, u32[]{:S(2)}, u32[]{:S(2)}) collective-permute-start(bf16[128,256]{1,0:T(8,128)(2,1)S(1)} %get-tuple-element.15), channel_id=1, source_target_pairs={{0,1},{1,0},{2,3},{3,2},{4,5},{5,4},{6,7},{7,6},{8,9},{9,8},{10,11... | collective-permute-start | bytes 196616 | tf_op jit(solution)/shard_map/ppermute | solution.py:30
  16.1 7.5 %collective-permute-start.6 = (bf16[128,256]{1,0:T(8,128)(2,1)S(1)}, bf16[128,256]{1,0:T(8,128)(2,1)S(1)}, u32[]{:S(2)}, u32[]{:S(2)}) collective-permute-start(bf16[128,256]{1,0:T(8,128)(2,1)S(1)} %get-tuple-element.16), channel_id=1, source_target_pairs={{0,2},{1,3},{2,0},{3,1},{4,6},{5,7},{6,4},{7,5},{8,10},{9,11},{10,... | collective-permute-start | bytes 196616 | tf_op jit(solution)/shard_map/ppermute | solution.py:30
  18.7 6.2 %collective-permute-start.7 = (bf16[128,256]{1,0:T(8,128)(2,1)S(1)}, bf16[128,256]{1,0:T(8,128)(2,1)S(1)}, u32[]{:S(2)}, u32[]{:S(2)}) collective-permute-start(bf16[128,256]{1,0:T(8,128)(2,1)S(1)} %get-tuple-element.17), channel_id=1, source_target_pairs={{0,3},{1,2},{2,1},{3,0},{4,7},{5,6},{6,5},{7,4},{8,11},{9,10},{10,... | collective-permute-start | bytes 196616 | tf_op jit(solution)/shard_map/ppermute | solution.py:30
  25.7 1.3 %collective-permute-start.8 = (bf16[256,256]{1,0:T(8,128)(2,1)S(1)}, bf16[256,256]{1,0:T(8,128)(2,1)S(1)}, u32[]{:S(2)}, u32[]{:S(2)}) collective-permute-start(bf16[256,256]{1,0:T(8,128)(2,1)S(1)} %get-tuple-element.19), channel_id=1, source_target_pairs={{0,4},{4,0},{8,12},{12,8},{16,20},{20,16},{24,28},{28,24},{1,5},{5... | collective-permute-start | bytes 393224 | tf_op jit(solution)/shard_map/ppermute | solution.py:30
  27.1 6.4 %collective-permute-start.9 = (bf16[256,256]{1,0:T(8,128)(2,1)S(1)}, bf16[256,256]{1,0:T(8,128)(2,1)S(1)}, u32[]{:S(2)}, u32[]{:S(2)}) collective-permute-start(bf16[256,256]{1,0:T(8,128)(2,1)S(1)} %add_convert_fusion.3), channel_id=1, source_target_pairs={{0,8},{4,12},{8,0},{12,4},{16,24},{20,28},{24,16},{28,20},{1,9},{5... | collective-permute-start | bytes 393224 | tf_op jit(solution)/shard_map/ppermute | solution.py:30
  27.7 7.1 %collective-permute-start.14 = (bf16[128,256]{1,0:T(8,128)(2,1)S(1)}, bf16[128,256]{1,0:T(8,128)(2,1)S(1)}, u32[]{:S(2)}, u32[]{:S(2)}) collective-permute-start(bf16[128,256]{1,0:T(8,128)(2,1)S(1)} %get-tuple-element.20.refs_0_), channel_id=1, source_target_pairs={{0,8},{4,12},{8,0},{12,4},{16,24},{20,28},{24,16},{28,20},{1,9},{5... | collective-permute-start | bytes 196616 | tf_op jit(solution)/shard_map/ppermute | solution.py:30
  29.2 5.6 %collective-permute-start.15 = (bf16[128,256]{1,0:T(8,128)(2,1)S(1)}, bf16[128,256]{1,0:T(8,128)(2,1)S(1)}, u32[]{:S(2)}, u32[]{:S(2)}) collective-permute-start(bf16[128,256]{1,0:T(8,128)(2,1)S(1)} %get-tuple-element.20.refs_0_), channel_id=1, source_target_pairs={{0,16},{4,20},{8,24},{12,28},{16,0},{20,4},{24,8},{28,12},{1,17},{... | collective-permute-start | bytes 196616 | tf_op jit(solution)/shard_map/ppermute | solution.py:30
  29.7 5.9 %collective-permute-start.16 = (bf16[128,256]{1,0:T(8,128)(2,1)S(1)}, bf16[128,256]{1,0:T(8,128)(2,1)S(1)}, u32[]{:S(2)}, u32[]{:S(2)}) collective-permute-start(bf16[128,256]{1,0:T(8,128)(2,1)S(1)} %get-tuple-element.20.refs_0_), channel_id=1, source_target_pairs={{0,24},{4,28},{8,16},{12,20},{16,8},{20,12},{24,0},{28,4},{1,25},{... | collective-permute-start | bytes 196616 | tf_op jit(solution)/shard_map/ppermute | solution.py:30
  33.5 5.0 %collective-permute-start.10 = (bf16[256,256]{1,0:T(8,128)(2,1)S(1)}, bf16[256,256]{1,0:T(8,128)(2,1)S(1)}, u32[]{:S(2)}, u32[]{:S(2)}) collective-permute-start(bf16[256,256]{1,0:T(8,128)(2,1)S(1)} %add_convert_fusion.2), channel_id=1, source_target_pairs={{0,16},{4,20},{8,24},{12,28},{16,0},{20,4},{24,8},{28,12},{1,17},{... | collective-permute-start | bytes 393224 | tf_op jit(solution)/shard_map/ppermute | solution.py:30
  35.6 5.1 %collective-permute-start.17 = (bf16[384,256]{1,0:T(8,128)(2,1)S(1)}, bf16[384,256]{1,0:T(8,128)(2,1)S(1)}, u32[]{:S(2)}, u32[]{:S(2)}) collective-permute-start(bf16[384,256]{1,0:T(8,128)(2,1)S(1)} %pad_maximum_fusion.1), channel_id=1, source_target_pairs={{0,4},{4,0},{8,12},{12,8},{16,20},{20,16},{24,28},{28,24},{1,5},{5... | collective-permute-start | bytes 589832 | tf_op jit(solution)/shard_map/ppermute | solution.py:30
  38.6 7.0 %collective-permute-start.11 = (bf16[256,256]{1,0:T(8,128)(2,1)S(1)}, bf16[256,256]{1,0:T(8,128)(2,1)S(1)}, u32[]{:S(2)}, u32[]{:S(2)}) collective-permute-start(bf16[256,256]{1,0:T(8,128)(2,1)S(1)} %add_convert_fusion.1), channel_id=1, source_target_pairs={{0,1},{1,0},{2,3},{3,2},{4,5},{5,4},{6,7},{7,6},{8,9},{9,8},{10,11... | collective-permute-start | bytes 393224 | tf_op jit(solution)/shard_map/ppermute | solution.py:30
  39.4 1.3 %collective-permute-start.13 = (bf16[128,256]{1,0:T(8,128)(2,1)S(1)}, bf16[128,256]{1,0:T(8,128)(2,1)S(1)}, u32[]{:S(2)}, u32[]{:S(2)}) collective-permute-start(bf16[128,256]{1,0:T(8,128)(2,1)S(1)} %get-tuple-element.20.refs_0_), channel_id=1, source_target_pairs={{0,4},{4,0},{8,12},{12,8},{16,20},{20,16},{24,28},{28,24},{1,5},{5... | collective-permute-start | bytes 196616 | tf_op jit(solution)/shard_map/ppermute | solution.py:30
  41.1 5.4 %collective-permute-start.18 = (bf16[128,256]{1,0:T(8,128)(2,1)S(1)}, bf16[128,256]{1,0:T(8,128)(2,1)S(1)}, u32[]{:S(2)}, u32[]{:S(2)}) collective-permute-start(bf16[128,256]{1,0:T(8,128)(2,1)S(1)} %get-tuple-element.22), channel_id=1, source_target_pairs={{0,1},{1,0},{2,3},{3,2},{4,5},{5,4},{6,7},{7,6},{8,9},{9,8},{10,11... | collective-permute-start | bytes 196616 | tf_op jit(solution)/shard_map/ppermute | solution.py:30
  42.5 11.0 %collective-permute-start.19 = (bf16[128,256]{1,0:T(8,128)(2,1)S(1)}, bf16[128,256]{1,0:T(8,128)(2,1)S(1)}, u32[]{:S(2)}, u32[]{:S(2)}) collective-permute-start(bf16[128,256]{1,0:T(8,128)(2,1)S(1)} %get-tuple-element.23), channel_id=1, source_target_pairs={{0,2},{1,3},{2,0},{3,1},{4,6},{5,7},{6,4},{7,5},{8,10},{9,11},{10,... | collective-permute-start | bytes 196616 | tf_op jit(solution)/shard_map/ppermute | solution.py:30
  44.2 9.3 %collective-permute-start.20 = (bf16[128,256]{1,0:T(8,128)(2,1)S(1)}, bf16[128,256]{1,0:T(8,128)(2,1)S(1)}, u32[]{:S(2)}, u32[]{:S(2)}) collective-permute-start(bf16[128,256]{1,0:T(8,128)(2,1)S(1)} %get-tuple-element.24), channel_id=1, source_target_pairs={{0,3},{1,2},{2,1},{3,0},{4,7},{5,6},{6,5},{7,4},{8,11},{9,10},{10,... | collective-permute-start | bytes 196616 | tf_op jit(solution)/shard_map/ppermute | solution.py:30
  45.6 11.5 %collective-permute-start.12 = (bf16[256,256]{1,0:T(8,128)(2,1)S(1)}, bf16[256,256]{1,0:T(8,128)(2,1)S(1)}, u32[]{:S(2)}, u32[]{:S(2)}) collective-permute-start(bf16[256,256]{1,0:T(8,128)(2,1)S(1)} %add_convert_fusion), channel_id=1, source_target_pairs={{0,2},{1,3},{2,0},{3,1},{4,6},{5,7},{6,4},{7,5},{8,10},{9,11},{10,... | collective-permute-start | bytes 393224 | tf_op jit(solution)/shard_map/ppermute | solution.py:30

commit v2 on v1

v2 whole, which is shorter than its diff:
```python
import functools
import math

import jax
import jax.numpy as jnp
from jax import lax
from jax.experimental import pallas as pl
from jax.experimental.pallas import tpu as pltpu
from jax.sharding import PartitionSpec as P

F32 = jnp.float32
BF16 = jnp.bfloat16
VMEM_LIMIT = 8 * 1024 * 1024


def vmem():
    return pl.BlockSpec(memory_space=pltpu.VMEM)


def smem():
    return pl.BlockSpec(memory_space=pltpu.SMEM)


def params():
    return pltpu.CompilerParams(vmem_limit_bytes=VMEM_LIMIT)


def swap(value, axis, distance):
    size = lax.axis_size(axis)
    return lax.ppermute(value, axis, [(i, i ^ distance) for i in range(size)])


def far_order(slabs):
    return sorted(range(2, slabs, 2), key=lambda d: -bin(d).count("1"))


def sub_order(subs):
    return list(range(subs))[:0:-1]


def dense_kernel(order, subs, rows_ref, counts_ref, tiles_ref, out_ref):
    me, mine = lax.axis_index("blk"), lax.axis_index("rep")
    block = tiles_ref.shape[1]
    slots = tiles_ref.shape[2] // block
    for q, distance in enumerate(order):
        slab = me ^ distance
        tile = tiles_ref[slab]
        turned = [tile[:, k * block : (k + 1) * block].T for k in range(slots)]
        places = [
            jnp.where(k < counts_ref[slab], rows_ref[slab, k] ^ mine, -1) for k in range(slots)
        ]
        for b, sub in enumerate(subs):
            value = jnp.zeros((block, block), tile.dtype)
            for k in range(slots):
                value = jnp.where(places[k] == sub, turned[k], value)
            out_ref[q * block : (q + 1) * block, b * block : (b + 1) * block] = value


def dense_adjacency(order, subs, rows, counts, tiles):
    block = tiles.shape[1]
    shape = (len(order) * block, len(subs) * block)
    return pl.pallas_call(
        functools.partial(dense_kernel, order, subs),
        out_shape=jax.ShapeDtypeStruct(shape, tiles.dtype),
        in_specs=[smem(), smem(), vmem()],
        out_specs=vmem(),
        compiler_params=params(),
        cost_estimate=pl.CostEstimate(flops=0, bytes_accessed=4 * tiles.size * 2, transcendentals=0),
    )(rows, counts, tiles)


def apply_kernel(n_pieces, dense_ref, *refs):
    pieces, (odd_ref, even_ref) = refs[:n_pieces], refs[n_pieces:]
    nodes = jnp.concatenate([piece[...] for piece in pieces], axis=0)
    rows = odd_ref.shape[0]
    odd = jnp.dot(dense_ref[rows:, :], nodes, preferred_element_type=F32)
    odd_ref[...] = odd.astype(odd_ref.dtype)
    even_ref[...] = jnp.dot(dense_ref[:rows, :], nodes, preferred_element_type=F32)


def apply_dense(dense, pieces):
    shape = (dense.shape[0] // 2, pieces[0].shape[1])
    return pl.pallas_call(
        functools.partial(apply_kernel, len(pieces)),
        out_shape=[jax.ShapeDtypeStruct(shape, t) for t in (BF16, F32)],
        in_specs=[vmem()] * (1 + len(pieces)),
        out_specs=[vmem()] * 2,
        compiler_params=params(),
        cost_estimate=pl.CostEstimate(
            flops=2 * dense.size * shape[1], bytes_accessed=2 * dense.size, transcendentals=0
        ),
    )(dense, *pieces)


def chip_kernel(n_keep, even_ref, other_ref, *refs):
    keeps, (own_ref, *outs) = refs[:n_keep], refs[n_keep:]
    block, rows = own_ref.shape[0], even_ref.shape[0]
    own_ref[...] = even_ref[:block, :] + other_ref[:block, :].astype(F32)
    if keeps:
        half = (keeps[0][...] + other_ref[rows:, :].astype(F32)).astype(BF16)
        outs[-1][...] = half
        outs = outs[:-1]
    for q, out in enumerate(outs, 1):
        part = slice(q * block, (q + 1) * block)
        out[:block, :] = (even_ref[part, :] + other_ref[part, :].astype(F32)).astype(BF16)
        if keeps:
            out[block:, :] = half


def chip_sums(even, other, n_far, *keeps):
    block, feat = even.shape[0] // (1 + n_far), even.shape[1]
    more = keeps[0].shape[0] if keeps else 0
    shapes = [jax.ShapeDtypeStruct((block, feat), F32)]
    shapes += [jax.ShapeDtypeStruct((block + more, feat), BF16)] * n_far
    shapes += [jax.ShapeDtypeStruct((more, feat), BF16)] if keeps else []
    return pl.pallas_call(
        functools.partial(chip_kernel, len(keeps)),
        out_shape=shapes,
        in_specs=[vmem()] * (2 + len(keeps)),
        out_specs=[vmem()] * len(shapes),
        compiler_params=params(),
        cost_estimate=pl.CostEstimate(flops=4 * even.size, bytes_accessed=4 * even.size, transcendentals=0),
    )(even, other, *keeps)


def tree(order, values):
    values = [value.astype(F32) for _, value in sorted(zip(order, values), key=lambda pair: pair[0])]
    while len(values) > 1:
        values = [values[k] + values[k + 1] for k in range(0, len(values), 2)]
    return values[0]


def layer_kernel(n_parts, *refs):
    parts, (weight_ref, cotangent_ref, pair_ref) = refs[:n_parts], refs[n_parts:]
    block = cotangent_ref.shape[0]
    total = parts[0][...]
    for part in parts[1:]:
        total = total + part[...].astype(F32)
    agg = total.astype(BF16)
    pre = jnp.dot(agg, weight_ref[...], preferred_element_type=F32)
    sig = 1.0 / (1.0 + jnp.exp(-pre))
    dpre = cotangent_ref[...].astype(F32) * sig * (1.0 + pre * (1.0 - sig))
    pair_ref[:block, :] = agg
    pair_ref[block:, :] = dpre.astype(BF16)


def layer(parts, weight, cotangent):
    block, feat = cotangent.shape
    return pl.pallas_call(
        functools.partial(layer_kernel, len(parts)),
        out_shape=jax.ShapeDtypeStruct((2 * block, feat), BF16),
        in_specs=[vmem()] * (len(parts) + 2),
        out_specs=vmem(),
        compiler_params=params(),
        cost_estimate=pl.CostEstimate(
            flops=2 * block * feat * feat, bytes_accessed=block * feat * 16, transcendentals=block * feat
        ),
    )(*parts, weight, cotangent)


def activation_kernel(pair_ref, weight_ref, out_ref):
    pre = jnp.dot(pair_ref[: out_ref.shape[0], :], weight_ref[...], preferred_element_type=F32)
    out_ref[...] = (pre / (1.0 + jnp.exp(-pre))).astype(out_ref.dtype)


def layer_output(pair, weight):
    shape = (pair.shape[0] // 2, pair.shape[1])
    return pl.pallas_call(
        activation_kernel,
        out_shape=jax.ShapeDtypeStruct(shape, BF16),
        in_specs=[vmem()] * 2,
        out_specs=vmem(),
        compiler_params=params(),
        cost_estimate=pl.CostEstimate(
            flops=pair.size * shape[1], bytes_accessed=pair.size * 4, transcendentals=pair.size // 2
        ),
    )(pair, weight)


def back_kernel(scale, n_pairs, dense_ref, weight_ref, *refs):
    pairs, (odd_ref, even_ref, keep_ref) = refs[:n_pairs], refs[n_pairs:]
    block = pairs[0].shape[0] // 2
    dpre = jnp.concatenate([pair[block:, :] for pair in pairs], axis=0)
    back = lax.dot_general(
        dpre, weight_ref[...], (((1,), (1,)), ((), ())), preferred_element_type=F32
    ).astype(BF16)
    rows = even_ref.shape[0]
    odd = jnp.dot(dense_ref[rows:, :], back, preferred_element_type=F32)
    odd_ref[:rows, :] = odd.astype(odd_ref.dtype)
    even_ref[...] = jnp.dot(dense_ref[:rows, :], back, preferred_element_type=F32)
    agg = jnp.concatenate([pair[:block, :] for pair in pairs], axis=0)
    half = agg.shape[1] // 2
    first, second = (
        lax.dot_general(cols, dpre, (((0,), (0,)), ((), ())), preferred_element_type=F32) * scale
        for cols in (agg[:, :half], agg[:, half:])
    )
    is_first = lax.axis_index("blk") % 2 == 0
    odd_ref[rows:, :] = jnp.where(is_first, second, first).astype(odd_ref.dtype)
    keep_ref[...] = jnp.where(is_first, first, second)


def apply_back(dense, weight, pairs, scale):
    rows, feat = dense.shape[0] // 2, weight.shape[0]
    half = feat // 2
    shapes = ((rows + half, BF16), (rows, F32), (half, F32))
    return pl.pallas_call(
        functools.partial(back_kernel, scale, len(pairs)),
        out_shape=[jax.ShapeDtypeStruct((n, feat), t) for n, t in shapes],
        in_specs=[vmem()] * (2 + len(pairs)),
        out_specs=[vmem()] * 3,
        compiler_params=params(),
        cost_estimate=pl.CostEstimate(
            flops=4 * dense.size * feat, bytes_accessed=2 * dense.size, transcendentals=0
        ),
    )(dense, weight, *pairs)


def half_kernel(order, half_ref, *refs):
    parts, out_ref = refs[:-1], refs[-1]
    more = half_ref.shape[0]
    out_ref[...] = tree(order, [half_ref[...]] + [part[-more:, :] for part in parts])


def half_sum(order, half, parts):
    return pl.pallas_call(
        functools.partial(half_kernel, order),
        out_shape=jax.ShapeDtypeStruct(half.shape, F32),
        in_specs=[vmem()] * (1 + len(parts)),
        out_specs=vmem(),
        compiler_params=params(),
        cost_estimate=pl.CostEstimate(flops=half.size * 4, bytes_accessed=half.size * 12, transcendentals=0),
    )(half, *parts)


def last_kernel(own_ref, *refs):
    parts, out_ref = refs[:-1], refs[-1]
    total = own_ref[...]
    for part in parts:
        total = total + part[: own_ref.shape[0], :].astype(F32)
    out_ref[...] = total.astype(out_ref.dtype)


def last_sum(own, parts):
    return pl.pallas_call(
        last_kernel,
        out_shape=jax.ShapeDtypeStruct(own.shape, BF16),
        in_specs=[vmem()] * (1 + len(parts)),
        out_specs=vmem(),
        compiler_params=params(),
        cost_estimate=pl.CostEstimate(flops=own.size * 4, bytes_accessed=own.size * 12, transcendentals=0),
    )(own, *parts)


def exchange(value, axis, distances):
    return [value] + [swap(value, axis, d) for d in distances]


def join(mine):
    other = swap(mine, "blk", 1)
    is_first = lax.axis_index("blk") % 2 == 0
    return jnp.where(
        is_first, jnp.concatenate([mine, other], axis=0), jnp.concatenate([other, mine], axis=0)
    )


def shards_direct(features, weight, cotangent, rows, counts, tiles):
    slabs, subs = lax.axis_size("blk"), lax.axis_size("rep")
    far, near = far_order(slabs), sub_order(subs)
    node_count = features.shape[0] * slabs * subs
    even = [0] + far
    dense = dense_adjacency(even + [d + 1 for d in even], [0] + near, rows, counts, tiles)
    pieces, dense = lax.optimization_barrier((exchange(features, "rep", near), dense))
    odd, mine = apply_dense(dense, pieces)
    own, *sums = chip_sums(mine, swap(odd, "blk", 1), len(far))
    parts = [swap(value, "blk", d) for value, d in zip(sums, far)]
    pair = layer([own] + parts, weight, cotangent)
    pairs = exchange(pair, "rep", near)
    activation = layer_output(pair, weight)
    pairs, activation = lax.optimization_barrier((pairs, activation))
    odd, mine, keep = apply_back(dense, weight, pairs, 1.0 / math.sqrt(node_count))
    own, *sums, half = chip_sums(mine, swap(odd, "blk", 1), len(far), keep)
    parts = [swap(value, "blk", d) for value, d in zip(sums, far)]
    grad = join(half_sum(even, half, parts))
    return activation, grad, last_sum(own, parts)


def add_tile(running, column_block, node_slab, tiles, slot_rows, slot_counts):
    block_size = node_slab.shape[0]
    tile_now = lax.dynamic_index_in_dim(tiles, column_block, 0, keepdims=False)
    rows_now = lax.dynamic_index_in_dim(slot_rows, column_block, 0, keepdims=False)
    count_now = lax.dynamic_index_in_dim(slot_counts, column_block, 0, keepdims=False)

    def one_slot(slot_index, carried):
        weights_now = lax.dynamic_slice_in_dim(tile_now, slot_index * block_size, block_size, 1)
        product = jnp.dot(weights_now, node_slab, preferred_element_type=F32)
        first_row = rows_now[slot_index] * block_size
        current = lax.dynamic_slice_in_dim(carried, first_row, block_size, 0)
        return lax.dynamic_update_slice_in_dim(carried, current + product, first_row, 0)

    return lax.fori_loop(0, count_now, one_slot, running)


def aggregate(node_slab, tiles, slot_rows, slot_counts):
    block_size = node_slab.shape[0]
    running = jnp.zeros((block_size * lax.axis_size("rep"), node_slab.shape[1]), F32)
    piece = lax.all_gather(node_slab, "blk", axis=0, tiled=True)
    piece_count = piece.shape[0] // block_size

    def one_piece(inner, running_now):
        slab_now = lax.dynamic_slice_in_dim(piece, inner * block_size, block_size, 0)
        return add_tile(running_now, inner, slab_now, tiles, slot_rows, slot_counts)

    total = lax.fori_loop(0, piece_count, one_piece, running)
    return lax.psum_scatter(total.astype(BF16), "rep", scatter_dimension=0, tiled=True)


def shards_general(features, weight, cotangent, rows, counts, tiles):
    agg = aggregate(features, tiles, rows, counts)
    pre = jnp.dot(agg, weight, preferred_element_type=F32)
    sig = jax.nn.sigmoid(pre)
    activation = (pre * sig).astype(BF16)
    dpre = (cotangent.astype(F32) * sig * (1.0 + pre * (1.0 - sig))).astype(BF16)
    local_grad = lax.dot_general(agg, dpre, (((0,), (0,)), ((), ())), preferred_element_type=F32)
    node_count = features.shape[0] * lax.axis_size("blk") * lax.axis_size("rep")
    grad_weight = lax.psum(local_grad, ("blk", "rep")) / math.sqrt(node_count)
    back = lax.dot_general(dpre, weight, (((1,), (1,)), ((), ())), preferred_element_type=F32)
    return activation, grad_weight, aggregate(back.astype(BF16), tiles, rows, counts)


def shards(features, weight, cotangent, block_rows, block_counts, block_values):
    tiles = block_values[0, :, 0]
    rows = block_rows[0, :, 0]
    counts = block_counts[0, :, 0]
    sizes = lax.axis_size("blk"), lax.axis_size("rep")
    direct = sizes[0] in (4, 8) and sizes[1] in (2, 4)
    return (shards_direct if direct else shards_general)(
        features, weight, cotangent, rows, counts, tiles
    )


def solution(mesh):
    placed = (
        P(("blk", "rep"), None),
        P(),
        P(("blk", "rep"), None),
        P("blk", None, "rep", None),
        P("blk", None, "rep"),
        P("blk", None, "rep", None, None),
    )
    return jax.shard_map(
        shards,
        mesh=mesh,
        in_specs=placed,
        out_specs=(P(("blk", "rep"), None), P(), P(("blk", "rep"), None)),
        check_vma=False,
    )
```

time: 58 us -> 48.8 us (0.84)
  waiting for transfers between devices: 30.5 us -> 23.9 us
  starting transfers between devices: 20.4 us -> 17.5 us
  Pallas kernels: 2.66 us -> 3.91 us
  other arithmetic: 1.55 us -> 0.73 us
    ppermute x21 -> x15, waiting for transfers between devices: 30.5 us -> 23.9 us  [swap(): return lax.ppermute(value, axis, [(i, i ^ distance) for i in range(size)])]
    ppermute x21 -> x15, starting transfers between devices: 20.4 us -> 17.5 us  [swap(): return lax.ppermute(value, axis, [(i, i ^ distance) for i in range(size)])]
    pallas_call x2 -> x8, Pallas kernels: 1.75 us -> 3.47 us  [the longest x1 0.83 us: dense_adjacency(): pl.pallas_call(functools.partial(dense_kernel, order, subs), out_shape=ja...]
    convert_element_type x5 -> x0, other arithmetic: 0.8 us -> none  [the longest x1 0.66 us: shards_direct(): return (activation, grad_weight.astype(F32), grad_features.astype(BF16))]
    add x1 -> x0, other arithmetic: 0.73 us -> none  [total_direct(): value = value.astype(F32) + other.astype(F32)]
    select_n x0 -> x1, other arithmetic: none -> 0.73 us  [join(): jnp.where(is_first, jnp.concatenate([mine, other], axis=0), jnp.concatena...]
  transfers between devices with their start and end apart: 21 -> 15, of which waited for: 13 -> 12; matrix products, arithmetic and copies ran while one was open for 1% -> 0% of each run, Pallas kernels for 2% -> 5%
where the time goes in v2:
time: 48.8 us; the launch traced here: 48.6 us
  waiting for transfers between devices  23.9 us (49%)
  starting transfers between devices  17.5 us (36%)
  Pallas kernels  3.91 us (8%)
  local copies, waits for them, and re-layouts  1.79 us (4%)
  between operations  0.74 us (2%)
  other arithmetic  0.73 us (1%)
    ppermute x15, waiting for transfers between devices, swap(): return lax.ppermute(value, axis, [(i, i ^ distance) for i in range(size)])  23.9 us
    ppermute x15, starting transfers between devices, swap(): return lax.ppermute(value, axis, [(i, i ^ distance) for i in range(size)])  17.5 us
    unnamed x12, local copies, waits for them, and re-layouts  1.71 us
  transfers between devices with their start and end apart: 15, of which 12 were waited for; matrix products, arithmetic and copies ran while one was open for 0% of the time, Pallas kernels for 5%

profile of v2, /device:TPU:0, one launch (start us, length us, event | category | flops | bytes accessed | tf_op | source)
XLA Modules:
  0.0 48.6 jit_solution(3746293061305209047)
XLA Ops:
  0.6 0.0 copy-start.5
  0.6 5.1 %collective-permute-start = (bf16[128,256]{1,0:T(8,128)(2,1)}, bf16[128,256]{1,0:T(8,128)(2,1)S(1)}, u32[]{:S(2)}, u32[]{:S(2)}) collective-permute-start(bf16[128,256]{1,0:T(8,128)(2,1)} %refs_0_), channel_id=1, source_target_pairs={{0,3},{1,2},{2,1},{3,0},{4,7},{5,6},{6,5},{7,4},{8,11},{9,10},{10,... | collective-permute-start | bytes 196616 | tf_op jit(solution)/shard_map/ppermute | solution.py:30
  5.8 0.0 collective-permute-start.1
  5.8 0.6 %collective-permute-start.2 = (bf16[128,256]{1,0:T(8,128)(2,1)}, bf16[128,256]{1,0:T(8,128)(2,1)S(1)}, u32[]{:S(2)}, u32[]{:S(2)}) collective-permute-start(bf16[128,256]{1,0:T(8,128)(2,1)} %refs_0_), channel_id=1, source_target_pairs={{0,1},{1,0},{2,3},{3,2},{4,5},{5,4},{6,7},{7,6},{8,9},{9,8},{10,11... | collective-permute-start | bytes 196616 | tf_op jit(solution)/shard_map/ppermute | solution.py:30
  6.4 0.0 copy-done.5
  6.4 0.1 copy.9.rows_ref
  6.5 0.0 copy-start.4
  6.5 0.7 %copy-done.4 = s32[1,8,1]{1,2,0:T(1,128)S(1)} copy-done((s32[1,8,1]{1,2,0:T(1,128)S(1)}, s32[1,8,1]{1,2,0:T(1,128)}, u32[]{:S(2)}) %copy-start.4) | copy-done | bytes 56
  7.1 0.0 copy-start.1
  7.1 1.0 %copy-done.1 = bf16[1,8,1,128,256]{4,3,2,1,0:T(8,128)(2,1)S(1)} copy-done((bf16[1,8,1,128,256]{4,3,2,1,0:T(8,128)(2,1)S(1)}, bf16[1,8,1,128,256]{4,3,2,1,0:T(8,128)(2,1)}, u32[]{:S(2)}) %copy-start.1) | copy-done | bytes 524312
  8.2 0.0 copy-start.2
  8.2 0.8 %shard_map.85.dense_ref = bf16[1024,512]{1,0:T(8,128)(2,1)S(1)} custom-call(s32[8,2]{1,0:T(8,128)S(1)} %copy.9.rows_ref, s32[8]{0:T(128)S(1)} %bitcast.4, bf16[8,128,256]{2,1,0:T(8,128)(2,1)S(1)} %bitcast.3), custom_call_target="tpu_custom_call" | custom-call | bytes 2097152 | tf_op jit(solution)/shard_map/pallas_call | solution.py:62
  9.0 0.0 collective-permute-done.refs_1_
  9.0 2.5 %collective-permute-done.1.refs_2_ = bf16[128,256]{1,0:T(8,128)(2,1)S(1)} collective-permute-done((bf16[128,256]{1,0:T(8,128)(2,1)}, bf16[128,256]{1,0:T(8,128)(2,1)S(1)}, u32[]{:S(2)}, u32[]{:S(2)}) %collective-permute-start.1) | collective-permute-done | bytes 65568 | tf_op jit(solution)/shard_map/ppermute | solution.py:30
  11.6 0.0 collective-permute-done.2.refs_3_
  11.6 0.0 copy-done.2
  11.6 0.4 shard_map.86
  12.0 0.1 collective-permute-start.3
  12.1 1.5 %collective-permute-done.3.other_ref = bf16[512,256]{1,0:T(8,128)(2,1)S(1)} collective-permute-done((bf16[512,256]{1,0:T(8,128)(2,1)S(1)}, bf16[512,256]{1,0:T(8,128)(2,1)S(1)}, u32[]{:S(2)}, u32[]{:S(2)}) %collective-permute-start.3) | collective-permute-done | bytes 262176 | tf_op jit(solution)/shard_map/ppermute | solution.py:30
  13.6 0.0 copy-start
  13.6 0.0 copy-start.3
  13.7 2.5 %collective-permute-start.4 = (bf16[128,256]{1,0:T(8,128)(2,1)S(1)}, bf16[128,256]{1,0:T(8,128)(2,1)S(1)}, u32[]{:S(2)}, u32[]{:S(2)}) collective-permute-start(bf16[128,256]{1,0:T(8,128)(2,1)S(1)} %get-tuple-element.35), channel_id=1, source_target_pairs={{0,24},{4,28},{8,16},{12,20},{16,8},{20,12},{24,0},{28,4},{1,25},{... | collective-permute-start | bytes 196616 | tf_op jit(solution)/shard_map/ppermute | solution.py:30
  16.2 0.5 %collective-permute-start.5 = (bf16[128,256]{1,0:T(8,128)(2,1)S(1)}, bf16[128,256]{1,0:T(8,128)(2,1)S(1)}, u32[]{:S(2)}, u32[]{:S(2)}) collective-permute-start(bf16[128,256]{1,0:T(8,128)(2,1)S(1)} %get-tuple-element.36), channel_id=1, source_target_pairs={{0,8},{4,12},{8,0},{12,4},{16,24},{20,28},{24,16},{28,20},{1,9},{5... | collective-permute-start | bytes 196616 | tf_op jit(solution)/shard_map/ppermute | solution.py:30
  16.7 0.5 %collective-permute-start.6 = (bf16[128,256]{1,0:T(8,128)(2,1)S(1)}, bf16[128,256]{1,0:T(8,128)(2,1)S(1)}, u32[]{:S(2)}, u32[]{:S(2)}) collective-permute-start(bf16[128,256]{1,0:T(8,128)(2,1)S(1)} %get-tuple-element.37), channel_id=1, source_target_pairs={{0,16},{4,20},{8,24},{12,28},{16,0},{20,4},{24,8},{28,12},{1,17},{... | collective-permute-start | bytes 196616 | tf_op jit(solution)/shard_map/ppermute | solution.py:30
  17.2 2.1 %collective-permute-done.4.refs_1_ = bf16[128,256]{1,0:T(8,128)(2,1)S(1)} collective-permute-done((bf16[128,256]{1,0:T(8,128)(2,1)S(1)}, bf16[128,256]{1,0:T(8,128)(2,1)S(1)}, u32[]{:S(2)}, u32[]{:S(2)}) %collective-permute-start.4) | collective-permute-done | bytes 65568 | tf_op jit(solution)/shard_map/ppermute | solution.py:30
  19.3 1.1 %collective-permute-done.5.refs_2_ = bf16[128,256]{1,0:T(8,128)(2,1)S(1)} collective-permute-done((bf16[128,256]{1,0:T(8,128)(2,1)S(1)}, bf16[128,256]{1,0:T(8,128)(2,1)S(1)}, u32[]{:S(2)}, u32[]{:S(2)}) %collective-permute-start.5) | collective-permute-done | bytes 65568 | tf_op jit(solution)/shard_map/ppermute | solution.py:30
  20.5 0.5 %collective-permute-done.6.refs_3_ = bf16[128,256]{1,0:T(8,128)(2,1)S(1)} collective-permute-done((bf16[128,256]{1,0:T(8,128)(2,1)S(1)}, bf16[128,256]{1,0:T(8,128)(2,1)S(1)}, u32[]{:S(2)}, u32[]{:S(2)}) %collective-permute-start.6) | collective-permute-done | bytes 65568 | tf_op jit(solution)/shard_map/ppermute | solution.py:30
  21.0 0.0 copy-done
  21.0 0.0 copy-done.3
  21.0 0.2 shard_map.88.pair_ref.refs_0_
  21.2 2.8 %collective-permute-start.7 = (bf16[256,256]{1,0:T(8,128)(2,1)S(1)}, bf16[256,256]{1,0:T(8,128)(2,1)S(1)}, u32[]{:S(2)}, u32[]{:S(2)}) collective-permute-start(bf16[256,256]{1,0:T(8,128)(2,1)S(1)} %shard_map.88.pair_ref.refs_0_), channel_id=1, source_target_pairs={{0,3},{1,2},{2,1},{3,0},{4,7},{5,6},{6,5},{7,4},{8,11},{9,10},{10,... | collective-permute-start | bytes 393224 | tf_op jit(solution)/shard_map/ppermute | solution.py:30
  24.0 0.0 collective-permute-start.8
  24.0 1.7 %collective-permute-start.9 = (bf16[256,256]{1,0:T(8,128)(2,1)S(1)}, bf16[256,256]{1,0:T(8,128)(2,1)S(1)}, u32[]{:S(2)}, u32[]{:S(2)}) collective-permute-start(bf16[256,256]{1,0:T(8,128)(2,1)S(1)} %shard_map.88.pair_ref.refs_0_), channel_id=1, source_target_pairs={{0,1},{1,0},{2,3},{3,2},{4,5},{5,4},{6,7},{7,6},{8,9},{9,8},{10,11... | collective-permute-start | bytes 393224 | tf_op jit(solution)/shard_map/ppermute | solution.py:30
  25.7 0.8 %shard_map.89 = bf16[128,256]{1,0:T(8,128)(2,1)} custom-call(bf16[256,256]{1,0:T(8,128)(2,1)S(1)} %shard_map.88.pair_ref.refs_0_, bf16[256,256]{1,0:T(8,128)(2,1)S(1)} %copy-done), custom_call_target="tpu_custom_call" | custom-call | flops 16777216 | bytes 262144 | tf_op jit(solution)/shard_map/pallas_call | solution.py:168
  26.5 3.0 %collective-permute-done.7.refs_1_ = bf16[256,256]{1,0:T(8,128)(2,1)S(1)} collective-permute-done((bf16[256,256]{1,0:T(8,128)(2,1)S(1)}, bf16[256,256]{1,0:T(8,128)(2,1)S(1)}, u32[]{:S(2)}, u32[]{:S(2)}) %collective-permute-start.7) | collective-permute-done | bytes 131104 | tf_op jit(solution)/shard_map/ppermute | solution.py:30
  29.5 5.0 %collective-permute-done.8.refs_2_ = bf16[256,256]{1,0:T(8,128)(2,1)S(1)} collective-permute-done((bf16[256,256]{1,0:T(8,128)(2,1)S(1)}, bf16[256,256]{1,0:T(8,128)(2,1)S(1)}, u32[]{:S(2)}, u32[]{:S(2)}) %collective-permute-start.8) | collective-permute-done | bytes 131104 | tf_op jit(solution)/shard_map/ppermute | solution.py:30
  34.6 0.0 collective-permute-done.9.refs_3_
  34.6 0.8 %shard_map.90 = (bf16[640,256]{1,0:T(8,128)(2,1)S(1)}, f32[512,256]{1,0:T(8,128)S(1)}, f32[128,256]{1,0:T(8,128)S(1)}) custom-call(bf16[1024,512]{1,0:T(8,128)(2,1)S(1)} %shard_map.85.dense_ref, bf16[256,256]{1,0:T(8,128)(2,1)S(1)} %copy-done, bf16[256,256]{1,0:T(8,128)(2,1)S(1)} %shard_map.88.pair_ref.refs_0_, ...), custom_call_target="tpu_custom_call" | custom-call | flops 536870912 | bytes 1048576 | tf_op jit(solution)/shard_map/pallas_call | solution.py:206
  35.4 0.1 collective-permute-start.10
  35.5 1.6 %collective-permute-done.10.other_ref = bf16[640,256]{1,0:T(8,128)(2,1)S(1)} collective-permute-done((bf16[640,256]{1,0:T(8,128)(2,1)S(1)}, bf16[640,256]{1,0:T(8,128)(2,1)S(1)}, u32[]{:S(2)}, u32[]{:S(2)}) %collective-permute-start.10) | collective-permute-done | bytes 327712 | tf_op jit(solution)/shard_map/ppermute | solution.py:30
  37.1 0.1 shard_map.91
  37.1 2.1 %collective-permute-start.11 = (bf16[256,256]{1,0:T(8,128)(2,1)S(1)}, bf16[256,256]{1,0:T(8,128)(2,1)S(1)}, u32[]{:S(2)}, u32[]{:S(2)}) collective-permute-start(bf16[256,256]{1,0:T(8,128)(2,1)S(1)} %get-tuple-element.47), channel_id=1, source_target_pairs={{0,24},{4,28},{8,16},{12,20},{16,8},{20,12},{24,0},{28,4},{1,25},{... | collective-permute-start | bytes 393224 | tf_op jit(solution)/shard_map/ppermute | solution.py:30
  39.2 0.8 %collective-permute-start.12 = (bf16[256,256]{1,0:T(8,128)(2,1)S(1)}, bf16[256,256]{1,0:T(8,128)(2,1)S(1)}, u32[]{:S(2)}, u32[]{:S(2)}) collective-permute-start(bf16[256,256]{1,0:T(8,128)(2,1)S(1)} %get-tuple-element.48), channel_id=1, source_target_pairs={{0,8},{4,12},{8,0},{12,4},{16,24},{20,28},{24,16},{28,20},{1,9},{5... | collective-permute-start | bytes 393224 | tf_op jit(solution)/shard_map/ppermute | solution.py:30
  40.0 0.7 %collective-permute-start.13 = (bf16[256,256]{1,0:T(8,128)(2,1)S(1)}, bf16[256,256]{1,0:T(8,128)(2,1)S(1)}, u32[]{:S(2)}, u32[]{:S(2)}) collective-permute-start(bf16[256,256]{1,0:T(8,128)(2,1)S(1)} %get-tuple-element.49), channel_id=1, source_target_pairs={{0,16},{4,20},{8,24},{12,28},{16,0},{20,4},{24,8},{28,12},{1,17},{... | collective-permute-start | bytes 393224 | tf_op jit(solution)/shard_map/ppermute | solution.py:30
  40.7 3.7 %collective-permute-done.11.refs_0_ = bf16[256,256]{1,0:T(8,128)(2,1)S(1)} collective-permute-done((bf16[256,256]{1,0:T(8,128)(2,1)S(1)}, bf16[256,256]{1,0:T(8,128)(2,1)S(1)}, u32[]{:S(2)}, u32[]{:S(2)}) %collective-permute-start.11) | collective-permute-done | bytes 131104 | tf_op jit(solution)/shard_map/ppermute | solution.py:30
  44.4 1.9 %collective-permute-done.12.refs_1_ = bf16[256,256]{1,0:T(8,128)(2,1)S(1)} collective-permute-done((bf16[256,256]{1,0:T(8,128)(2,1)S(1)}, bf16[256,256]{1,0:T(8,128)(2,1)S(1)}, u32[]{:S(2)}, u32[]{:S(2)}) %collective-permute-start.12) | collective-permute-done | bytes 131104 | tf_op jit(solution)/shard_map/ppermute | solution.py:30
  46.3 0.2 collective-permute-done.13.refs_2_
  46.5 0.1 collective-permute-start.14
  46.6 0.7 %shard_map.93 = bf16[128,256]{1,0:T(8,128)(2,1)} custom-call(f32[128,256]{1,0:T(8,128)S(1)} %get-tuple-element.50.own_ref, bf16[256,256]{1,0:T(8,128)(2,1)S(1)} %collective-permute-done.11.refs_0_, bf16[256,256]{1,0:T(8,128)(2,1)S(1)} %collective-permute-done.12.refs_1_, bf16[256,256]{1,0:T(8,128)(2,1)S(1)} %collective-permute-done.13.refs_2_), custom_call_target="tpu_custom_call" | custom-call | flops 131072 | bytes 393216 | tf_op jit(solution)/shard_map/pallas_call | solution.py:244
  47.2 0.7 %collective-permute-done.14 = f32[128,256]{1,0:T(8,128)S(1)} collective-permute-done((f32[128,256]{1,0:T(8,128)S(1)}, f32[128,256]{1,0:T(8,128)S(1)}, u32[]{:S(2)}, u32[]{:S(2)}) %collective-permute-start.14) | collective-permute-done | bytes 131104 | tf_op jit(solution)/shard_map/ppermute | solution.py:30
  47.9 0.7 %maximum_select_fusion = f32[256,256]{1,0:T(8,128)} fusion(f32[128,256]{1,0:T(8,128)S(1)} %collective-permute-done.14, f32[128,256]{1,0:T(8,128)S(1)} %shard_map.92, pred[]{:T(512)S(6)} %eq.5), kind=kLoop, calls=%fused_computation | loop fusion | flops 196608 | bytes 524289 | tf_op jit(solution)/shard_map/jit(_where)/select_n | solution.py:261
  (2 shorter events, 0.1 us)
Async XLA Ops:
  0.6 5.8 %copy-start.5 = (s32[1,8,1,2]{1,3,2,0:T(2,128)S(1)}, s32[1,8,1,2]{1,3,2,0:T(2,128)}, u32[]{:S(2)}) copy-start(s32[1,8,1,2]{1,3,2,0:T(2,128)} %param.9) | copy-start | bytes 196
  0.6 8.4 %collective-permute-start = (bf16[128,256]{1,0:T(8,128)(2,1)}, bf16[128,256]{1,0:T(8,128)(2,1)S(1)}, u32[]{:S(2)}, u32[]{:S(2)}) collective-permute-start(bf16[128,256]{1,0:T(8,128)(2,1)} %refs_0_), channel_id=1, source_target_pairs={{0,3},{1,2},{2,1},{3,0},{4,7},{5,6},{6,5},{7,4},{8,11},{9,10},{10,... | collective-permute-start | bytes 196616 | tf_op jit(solution)/shard_map/ppermute | solution.py:30
  5.8 5.8 %collective-permute-start.1 = (bf16[128,256]{1,0:T(8,128)(2,1)}, bf16[128,256]{1,0:T(8,128)(2,1)S(1)}, u32[]{:S(2)}, u32[]{:S(2)}) collective-permute-start(bf16[128,256]{1,0:T(8,128)(2,1)} %refs_0_), channel_id=1, source_target_pairs={{0,2},{1,3},{2,0},{3,1},{4,6},{5,7},{6,4},{7,5},{8,10},{9,11},{10,... | collective-permute-start | bytes 196616 | tf_op jit(solution)/shard_map/ppermute | solution.py:30
  5.8 5.8 %collective-permute-start.2 = (bf16[128,256]{1,0:T(8,128)(2,1)}, bf16[128,256]{1,0:T(8,128)(2,1)S(1)}, u32[]{:S(2)}, u32[]{:S(2)}) collective-permute-start(bf16[128,256]{1,0:T(8,128)(2,1)} %refs_0_), channel_id=1, source_target_pairs={{0,1},{1,0},{2,3},{3,2},{4,5},{5,4},{6,7},{7,6},{8,9},{9,8},{10,11... | collective-permute-start | bytes 196616 | tf_op jit(solution)/shard_map/ppermute | solution.py:30
  6.5 0.7 %copy-start.4 = (s32[1,8,1]{1,2,0:T(1,128)S(1)}, s32[1,8,1]{1,2,0:T(1,128)}, u32[]{:S(2)}) copy-start(s32[1,8,1]{1,2,0:T(1,128)} %param.10) | copy-start | bytes 100
  7.1 1.0 %copy-start.1 = (bf16[1,8,1,128,256]{4,3,2,1,0:T(8,128)(2,1)S(1)}, bf16[1,8,1,128,256]{4,3,2,1,0:T(8,128)(2,1)}, u32[]{:S(2)}) copy-start(bf16[1,8,1,128,256]{4,3,2,1,0:T(8,128)(2,1)} %param.11) | copy-start | bytes 1572868
  8.2 3.4 %copy-start.2 = (bf16[128,256]{1,0:T(8,128)(2,1)S(1)}, bf16[128,256]{1,0:T(8,128)(2,1)}, u32[]{:S(2)}) copy-start(bf16[128,256]{1,0:T(8,128)(2,1)} %refs_0_) | copy-start | bytes 196612
  12.0 1.6 %collective-permute-start.3 = (bf16[512,256]{1,0:T(8,128)(2,1)S(1)}, bf16[512,256]{1,0:T(8,128)(2,1)S(1)}, u32[]{:S(2)}, u32[]{:S(2)}) collective-permute-start(bf16[512,256]{1,0:T(8,128)(2,1)S(1)} %get-tuple-element.33), channel_id=1, source_target_pairs={{0,4},{4,0},{8,12},{12,8},{16,20},{20,16},{24,28},{28,24},{1,5},{5... | collective-permute-start | bytes 786440 | tf_op jit(solution)/shard_map/ppermute | solution.py:30
  13.6 7.4 %copy-start = (bf16[256,256]{1,0:T(8,128)(2,1)S(1)}, bf16[256,256]{1,0:T(8,128)(2,1)}, u32[]{:S(2)}) copy-start(bf16[256,256]{1,0:T(8,128)(2,1)} %weight_ref.3) | copy-start | bytes 393220
  13.6 7.4 %copy-start.3 = (bf16[128,256]{1,0:T(8,128)(2,1)S(1)}, bf16[128,256]{1,0:T(8,128)(2,1)}, u32[]{:S(2)}) copy-start(bf16[128,256]{1,0:T(8,128)(2,1)} %refs_5_.1) | copy-start | bytes 196612
  13.7 5.6 %collective-permute-start.4 = (bf16[128,256]{1,0:T(8,128)(2,1)S(1)}, bf16[128,256]{1,0:T(8,128)(2,1)S(1)}, u32[]{:S(2)}, u32[]{:S(2)}) collective-permute-start(bf16[128,256]{1,0:T(8,128)(2,1)S(1)} %get-tuple-element.35), channel_id=1, source_target_pairs={{0,24},{4,28},{8,16},{12,20},{16,8},{20,12},{24,0},{28,4},{1,25},{... | collective-permute-start | bytes 196616 | tf_op jit(solution)/shard_map/ppermute | solution.py:30
  16.2 4.3 %collective-permute-start.5 = (bf16[128,256]{1,0:T(8,128)(2,1)S(1)}, bf16[128,256]{1,0:T(8,128)(2,1)S(1)}, u32[]{:S(2)}, u32[]{:S(2)}) collective-permute-start(bf16[128,256]{1,0:T(8,128)(2,1)S(1)} %get-tuple-element.36), channel_id=1, source_target_pairs={{0,8},{4,12},{8,0},{12,4},{16,24},{20,28},{24,16},{28,20},{1,9},{5... | collective-permute-start | bytes 196616 | tf_op jit(solution)/shard_map/ppermute | solution.py:30
  16.7 4.3 %collective-permute-start.6 = (bf16[128,256]{1,0:T(8,128)(2,1)S(1)}, bf16[128,256]{1,0:T(8,128)(2,1)S(1)}, u32[]{:S(2)}, u32[]{:S(2)}) collective-permute-start(bf16[128,256]{1,0:T(8,128)(2,1)S(1)} %get-tuple-element.37), channel_id=1, source_target_pairs={{0,16},{4,20},{8,24},{12,28},{16,0},{20,4},{24,8},{28,12},{1,17},{... | collective-permute-start | bytes 196616 | tf_op jit(solution)/shard_map/ppermute | solution.py:30
  21.2 8.3 %collective-permute-start.7 = (bf16[256,256]{1,0:T(8,128)(2,1)S(1)}, bf16[256,256]{1,0:T(8,128)(2,1)S(1)}, u32[]{:S(2)}, u32[]{:S(2)}) collective-permute-start(bf16[256,256]{1,0:T(8,128)(2,1)S(1)} %shard_map.88.pair_ref.refs_0_), channel_id=1, source_target_pairs={{0,3},{1,2},{2,1},{3,0},{4,7},{5,6},{6,5},{7,4},{8,11},{9,10},{10,... | collective-permute-start | bytes 393224 | tf_op jit(solution)/shard_map/ppermute | solution.py:30
  24.0 10.6 %collective-permute-start.8 = (bf16[256,256]{1,0:T(8,128)(2,1)S(1)}, bf16[256,256]{1,0:T(8,128)(2,1)S(1)}, u32[]{:S(2)}, u32[]{:S(2)}) collective-permute-start(bf16[256,256]{1,0:T(8,128)(2,1)S(1)} %shard_map.88.pair_ref.refs_0_), channel_id=1, source_target_pairs={{0,2},{1,3},{2,0},{3,1},{4,6},{5,7},{6,4},{7,5},{8,10},{9,11},{10,... | collective-permute-start | bytes 393224 | tf_op jit(solution)/shard_map/ppermute | solution.py:30
  24.0 10.6 %collective-permute-start.9 = (bf16[256,256]{1,0:T(8,128)(2,1)S(1)}, bf16[256,256]{1,0:T(8,128)(2,1)S(1)}, u32[]{:S(2)}, u32[]{:S(2)}) collective-permute-start(bf16[256,256]{1,0:T(8,128)(2,1)S(1)} %shard_map.88.pair_ref.refs_0_), channel_id=1, source_target_pairs={{0,1},{1,0},{2,3},{3,2},{4,5},{5,4},{6,7},{7,6},{8,9},{9,8},{10,11... | collective-permute-start | bytes 393224 | tf_op jit(solution)/shard_map/ppermute | solution.py:30
  35.4 1.7 %collective-permute-start.10 = (bf16[640,256]{1,0:T(8,128)(2,1)S(1)}, bf16[640,256]{1,0:T(8,128)(2,1)S(1)}, u32[]{:S(2)}, u32[]{:S(2)}) collective-permute-start(bf16[640,256]{1,0:T(8,128)(2,1)S(1)} %get-tuple-element.44), channel_id=1, source_target_pairs={{0,4},{4,0},{8,12},{12,8},{16,20},{20,16},{24,28},{28,24},{1,5},{5... | collective-permute-start | bytes 983048 | tf_op jit(solution)/shard_map/ppermute | solution.py:30
  37.1 7.3 %collective-permute-start.11 = (bf16[256,256]{1,0:T(8,128)(2,1)S(1)}, bf16[256,256]{1,0:T(8,128)(2,1)S(1)}, u32[]{:S(2)}, u32[]{:S(2)}) collective-permute-start(bf16[256,256]{1,0:T(8,128)(2,1)S(1)} %get-tuple-element.47), channel_id=1, source_target_pairs={{0,24},{4,28},{8,16},{12,20},{16,8},{20,12},{24,0},{28,4},{1,25},{... | collective-permute-start | bytes 393224 | tf_op jit(solution)/shard_map/ppermute | solution.py:30
  39.2 7.1 %collective-permute-start.12 = (bf16[256,256]{1,0:T(8,128)(2,1)S(1)}, bf16[256,256]{1,0:T(8,128)(2,1)S(1)}, u32[]{:S(2)}, u32[]{:S(2)}) collective-permute-start(bf16[256,256]{1,0:T(8,128)(2,1)S(1)} %get-tuple-element.48), channel_id=1, source_target_pairs={{0,8},{4,12},{8,0},{12,4},{16,24},{20,28},{24,16},{28,20},{1,9},{5... | collective-permute-start | bytes 393224 | tf_op jit(solution)/shard_map/ppermute | solution.py:30
  40.0 6.5 %collective-permute-start.13 = (bf16[256,256]{1,0:T(8,128)(2,1)S(1)}, bf16[256,256]{1,0:T(8,128)(2,1)S(1)}, u32[]{:S(2)}, u32[]{:S(2)}) collective-permute-start(bf16[256,256]{1,0:T(8,128)(2,1)S(1)} %get-tuple-element.49), channel_id=1, source_target_pairs={{0,16},{4,20},{8,24},{12,28},{16,0},{20,4},{24,8},{28,12},{1,17},{... | collective-permute-start | bytes 393224 | tf_op jit(solution)/shard_map/ppermute | solution.py:30
  46.5 1.4 %collective-permute-start.14 = (f32[128,256]{1,0:T(8,128)S(1)}, f32[128,256]{1,0:T(8,128)S(1)}, u32[]{:S(2)}, u32[]{:S(2)}) collective-permute-start(f32[128,256]{1,0:T(8,128)S(1)} %shard_map.92), channel_id=1, source_target_pairs={{0,4},{4,0},{8,12},{12,8},{16,20},{20,16},{24,28},{28,24},{1,5},{5... | collective-permute-start | bytes 393224 | tf_op jit(solution)/shard_map/ppermute | solution.py:30

commit v3 on v2

--- a/solution.py
+++ b/solution.py
@@ -35,7 +35,7 @@
 
 
 def sub_order(subs):
-    return list(range(subs))[:0:-1]
+    return [2, 3, 1] if subs == 4 else [1]
 
 
 def dense_kernel(order, subs, rows_ref, counts_ref, tiles_ref, out_ref):
@@ -69,58 +69,103 @@
     )(rows, counts, tiles)
 
 
-def apply_kernel(n_pieces, dense_ref, *refs):
-    pieces, (odd_ref, even_ref) = refs[:n_pieces], refs[n_pieces:]
-    nodes = jnp.concatenate([piece[...] for piece in pieces], axis=0)
-    rows = odd_ref.shape[0]
-    odd = jnp.dot(dense_ref[rows:, :], nodes, preferred_element_type=F32)
-    odd_ref[...] = odd.astype(odd_ref.dtype)
-    even_ref[...] = jnp.dot(dense_ref[:rows, :], nodes, preferred_element_type=F32)
-
-
-def apply_dense(dense, pieces):
-    shape = (dense.shape[0] // 2, pieces[0].shape[1])
-    return pl.pallas_call(
-        functools.partial(apply_kernel, len(pieces)),
-        out_shape=[jax.ShapeDtypeStruct(shape, t) for t in (BF16, F32)],
+def first_kernel(n_pieces, dense_ref, *refs):
+    nodes = jnp.concatenate([piece[...] for piece in refs[:n_pieces]], axis=0)
+    out_ref = refs[-1]
+    half = dense_ref.shape[0] // 2
+    rows = dense_ref[half : half + out_ref.shape[0], :]
+    out_ref[...] = jnp.dot(rows, nodes, preferred_element_type=F32).astype(out_ref.dtype)
+
+
+def apply_first(dense, pieces):
+    shape = pieces[0].shape
+    return pl.pallas_call(
+        functools.partial(first_kernel, len(pieces)),
+        out_shape=jax.ShapeDtypeStruct(shape, BF16),
+        in_specs=[vmem()] * (1 + len(pieces)),
+        out_specs=vmem(),
+        compiler_params=params(),
+        cost_estimate=pl.CostEstimate(
+            flops=2 * dense.shape[1] * shape[0] * shape[1], bytes_accessed=dense.size // 4, transcendentals=0
+        ),
+    )(dense, *pieces)
+
+
+def rest_kernel(n_pieces, dense_ref, *refs):
+    nodes = jnp.concatenate([piece[...] for piece in refs[:n_pieces]], axis=0)
+    odd_ref, even_ref = refs[n_pieces:]
+    half = dense_ref.shape[0] // 2
+    rows = dense_ref[dense_ref.shape[0] - odd_ref.shape[0] :, :]
+    odd_ref[...] = jnp.dot(rows, nodes, preferred_element_type=F32).astype(odd_ref.dtype)
+    even_ref[...] = jnp.dot(dense_ref[:half, :], nodes, preferred_element_type=F32)
+
+
+def apply_rest(dense, pieces, block):
+    rows, feat = dense.shape[0] // 2, pieces[0].shape[1]
+    return pl.pallas_call(
+        functools.partial(rest_kernel, len(pieces)),
+        out_shape=[jax.ShapeDtypeStruct((rows - block, feat), BF16), jax.ShapeDtypeStruct((rows, feat), F32)],
         in_specs=[vmem()] * (1 + len(pieces)),
         out_specs=[vmem()] * 2,
         compiler_params=params(),
         cost_estimate=pl.CostEstimate(
-            flops=2 * dense.size * shape[1], bytes_accessed=2 * dense.size, transcendentals=0
+            flops=2 * dense.size * feat, bytes_accessed=2 * dense.size, transcendentals=0
         ),
     )(dense, *pieces)
 
 
-def chip_kernel(n_keep, even_ref, other_ref, *refs):
-    keeps, (own_ref, *outs) = refs[:n_keep], refs[n_keep:]
-    block, rows = own_ref.shape[0], even_ref.shape[0]
-    own_ref[...] = even_ref[:block, :] + other_ref[:block, :].astype(F32)
-    if keeps:
-        half = (keeps[0][...] + other_ref[rows:, :].astype(F32)).astype(BF16)
-        outs[-1][...] = half
-        outs = outs[:-1]
-    for q, out in enumerate(outs, 1):
-        part = slice(q * block, (q + 1) * block)
-        out[:block, :] = (even_ref[part, :] + other_ref[part, :].astype(F32)).astype(BF16)
-        if keeps:
-            out[block:, :] = half
-
-
-def chip_sums(even, other, n_far, *keeps):
-    block, feat = even.shape[0] // (1 + n_far), even.shape[1]
-    more = keeps[0].shape[0] if keeps else 0
+def first_sum_kernel(even_ref, other_ref, *refs):
+    block = even_ref.shape[0]
+    if len(refs) == 1:
+        refs[0][...] = (even_ref[...] + other_ref[...].astype(F32)).astype(BF16)
+        return
+    keep_ref, out_ref, half_ref = refs
+    out_ref[:block, :] = (even_ref[...] + other_ref[:block, :].astype(F32)).astype(BF16)
+    half = (keep_ref[...] + other_ref[block:, :].astype(F32)).astype(BF16)
+    out_ref[block:, :] = half
+    half_ref[...] = half
+
+
+def first_sum(even, other, block, *keep):
+    shapes = [jax.ShapeDtypeStruct(other.shape, BF16)]
+    shapes += [jax.ShapeDtypeStruct(half.shape, BF16) for half in keep]
+    top = pl.BlockSpec((block, even.shape[1]), lambda i: (0, 0))
+    return pl.pallas_call(
+        first_sum_kernel,
+        grid=(1,),
+        out_shape=shapes,
+        in_specs=[top] + [vmem()] * (1 + len(keep)),
+        out_specs=[vmem()] * len(shapes),
+        compiler_params=params(),
+        cost_estimate=pl.CostEstimate(flops=other.size, bytes_accessed=other.size * 8, transcendentals=0),
+    )(even, other, *keep)
+
+
+def rest_sum_kernel(n_half, even_ref, other_ref, *refs):
+    half, (own_ref, *outs) = refs[:n_half], refs[n_half:]
+    block = own_ref.shape[0]
+    for q, out in enumerate([own_ref] + outs):
+        total = even_ref[(q + 1) * block : (q + 2) * block, :]
+        total = total + other_ref[q * block : (q + 1) * block, :].astype(F32)
+        out[:block, :] = total.astype(out.dtype)
+        if half and q:
+            out[block:, :] = half[0][...]
+
+
+def rest_sums(even, other, block, *half):
+    feat = even.shape[1]
+    more = half[0].shape[0] if half else 0
+    n_out = other.shape[0] // block - 1
     shapes = [jax.ShapeDtypeStruct((block, feat), F32)]
-    shapes += [jax.ShapeDtypeStruct((block + more, feat), BF16)] * n_far
-    shapes += [jax.ShapeDtypeStruct((more, feat), BF16)] if keeps else []
-    return pl.pallas_call(
-        functools.partial(chip_kernel, len(keeps)),
+    shapes += [jax.ShapeDtypeStruct((block + more, feat), BF16)] * n_out
+    return pl.pallas_call(
+        functools.partial(rest_sum_kernel, len(half)),
         out_shape=shapes,
-        in_specs=[vmem()] * (2 + len(keeps)),
+        in_specs=[vmem()] * (2 + len(half)),
         out_specs=[vmem()] * len(shapes),
         compiler_params=params(),
-        cost_estimate=pl.CostEstimate(flops=4 * even.size, bytes_accessed=4 * even.size, transcendentals=0),
-    )(even, other, *keeps)
+        cost_estimate=pl.CostEstimate(flops=other.size, bytes_accessed=other.size * 8, transcendentals=0),
+    )(even, other, *half)
 
 
 def tree(order, values):
@@ -178,31 +223,31 @@
 
 
 def back_kernel(scale, n_pairs, dense_ref, weight_ref, *refs):
-    pairs, (odd_ref, even_ref, keep_ref) = refs[:n_pairs], refs[n_pairs:]
+    pairs, (back_ref, first_ref, keep_ref) = refs[:n_pairs], refs[n_pairs:]
     block = pairs[0].shape[0] // 2
     dpre = jnp.concatenate([pair[block:, :] for pair in pairs], axis=0)
     back = lax.dot_general(
         dpre, weight_ref[...], (((1,), (1,)), ((), ())), preferred_element_type=F32
     ).astype(BF16)
-    rows = even_ref.shape[0]
-    odd = jnp.dot(dense_ref[rows:, :], back, preferred_element_type=F32)
-    odd_ref[:rows, :] = odd.astype(odd_ref.dtype)
-    even_ref[...] = jnp.dot(dense_ref[:rows, :], back, preferred_element_type=F32)
+    back_ref[...] = back
+    rows = dense_ref.shape[0] // 2
+    first = jnp.dot(dense_ref[rows : rows + block, :], back, preferred_element_type=F32)
+    first_ref[:block, :] = first.astype(BF16)
     agg = jnp.concatenate([pair[:block, :] for pair in pairs], axis=0)
     half = agg.shape[1] // 2
-    first, second = (
+    upper, lower = (
         lax.dot_general(cols, dpre, (((0,), (0,)), ((), ())), preferred_element_type=F32) * scale
         for cols in (agg[:, :half], agg[:, half:])
     )
     is_first = lax.axis_index("blk") % 2 == 0
-    odd_ref[rows:, :] = jnp.where(is_first, second, first).astype(odd_ref.dtype)
-    keep_ref[...] = jnp.where(is_first, first, second)
+    first_ref[block:, :] = jnp.where(is_first, lower, upper).astype(BF16)
+    keep_ref[...] = jnp.where(is_first, upper, lower)
 
 
 def apply_back(dense, weight, pairs, scale):
-    rows, feat = dense.shape[0] // 2, weight.shape[0]
-    half = feat // 2
-    shapes = ((rows + half, BF16), (rows, F32), (half, F32))
+    feat = weight.shape[0]
+    block, half = pairs[0].shape[0] // 2, feat // 2
+    shapes = ((len(pairs) * block, BF16), (block + half, BF16), (half, F32))
     return pl.pallas_call(
         functools.partial(back_kernel, scale, len(pairs)),
         out_shape=[jax.ShapeDtypeStruct((n, feat), t) for n, t in shapes],
@@ -210,7 +255,7 @@
         out_specs=[vmem()] * 3,
         compiler_params=params(),
         cost_estimate=pl.CostEstimate(
-            flops=4 * dense.size * feat, bytes_accessed=2 * dense.size, transcendentals=0
+            flops=8 * len(pairs) * block * feat * feat, bytes_accessed=dense.size, transcendentals=0
         ),
     )(dense, weight, *pairs)
 
@@ -218,13 +263,14 @@
 def half_kernel(order, half_ref, *refs):
     parts, out_ref = refs[:-1], refs[-1]
     more = half_ref.shape[0]
-    out_ref[...] = tree(order, [half_ref[...]] + [part[-more:, :] for part in parts])
+    total = tree(order, [half_ref[...]] + [part[-more:, :] for part in parts])
+    out_ref[...] = total.astype(out_ref.dtype)
 
 
 def half_sum(order, half, parts):
     return pl.pallas_call(
         functools.partial(half_kernel, order),
-        out_shape=jax.ShapeDtypeStruct(half.shape, F32),
+        out_shape=jax.ShapeDtypeStruct(half.shape, BF16),
         in_specs=[vmem()] * (1 + len(parts)),
         out_specs=vmem(),
         compiler_params=params(),
@@ -264,23 +310,33 @@
 
 
 def shards_direct(features, weight, cotangent, rows, counts, tiles):
+    block = features.shape[0]
     slabs, subs = lax.axis_size("blk"), lax.axis_size("rep")
     far, near = far_order(slabs), sub_order(subs)
-    node_count = features.shape[0] * slabs * subs
-    even = [0] + far
+    node_count = block * slabs * subs
+    even = far[:1] + [0] + far[1:]
     dense = dense_adjacency(even + [d + 1 for d in even], [0] + near, rows, counts, tiles)
+
     pieces, dense = lax.optimization_barrier((exchange(features, "rep", near), dense))
-    odd, mine = apply_dense(dense, pieces)
-    own, *sums = chip_sums(mine, swap(odd, "blk", 1), len(far))
-    parts = [swap(value, "blk", d) for value, d in zip(sums, far)]
+    other = swap(apply_first(dense, pieces), "blk", 1)
+    rest, mine = apply_rest(dense, pieces, block)
+    rest, other = lax.optimization_barrier((rest, other))
+    (first,) = first_sum(mine, other, block)
+    own, *sums = rest_sums(mine, swap(rest, "blk", 1), block)
+    parts = [swap(value, "blk", d) for value, d in zip([first] + sums, far)]
+
     pair = layer([own] + parts, weight, cotangent)
     pairs = exchange(pair, "rep", near)
     activation = layer_output(pair, weight)
     pairs, activation = lax.optimization_barrier((pairs, activation))
-    odd, mine, keep = apply_back(dense, weight, pairs, 1.0 / math.sqrt(node_count))
-    own, *sums, half = chip_sums(mine, swap(odd, "blk", 1), len(far), keep)
-    parts = [swap(value, "blk", d) for value, d in zip(sums, far)]
-    grad = join(half_sum(even, half, parts))
+    back, first, keep = apply_back(dense, weight, pairs, 1.0 / math.sqrt(node_count))
+    other = swap(first, "blk", 1)
+    rest, mine = apply_rest(dense, [back], block)
+    rest, other = lax.optimization_barrier((rest, other))
+    first, half = first_sum(mine, other, block, keep)
+    own, *sums = rest_sums(mine, swap(rest, "blk", 1), block, half)
+    parts = [swap(value, "blk", d) for value, d in zip([first] + sums, far)]
+    grad = join(half_sum([0] + far, half, parts)).astype(F32)
     return activation, grad, last_sum(own, parts)
 
 

time: 48.8 us -> 47 us (0.963)
  waiting for transfers between devices: 23.9 us -> 20.8 us
  starting transfers between devices: 17.5 us -> 18.5 us
    ppermute x15 -> x17, waiting for transfers between devices: 23.9 us -> 20.8 us  [swap(): return lax.ppermute(value, axis, [(i, i ^ distance) for i in range(size)])]
    ppermute x15 -> x17, starting transfers between devices: 17.5 us -> 18.5 us  [swap(): return lax.ppermute(value, axis, [(i, i ^ distance) for i in range(size)])]
    select_n x1 -> x0, other arithmetic: 0.73 us -> none  [join(): jnp.where(is_first, jnp.concatenate([mine, other], axis=0), jnp.concatena...]
    convert_element_type x0 -> x1, other arithmetic: none -> 0.73 us  [shards_direct(): grad = join(half_sum([0] + far, half, parts)).astype(F32)]
    pallas_call x3 -> x7, Pallas kernels: 0.54 us -> 1.11 us  [the longest x2 0.81 us: apply_rest(): pl.pallas_call(functools.partial(rest_kernel, len(pieces)), out_shape=[ja...]
  transfers between devices with their start and end apart: 15 -> 17, of which waited for: 12 -> 13; matrix products, arithmetic and copies ran while one was open for 0% -> 0% of each run, Pallas kernels for 5% -> 7%
where the time goes in v3:
time: 47 us; the launch traced here: 46.8 us
  waiting for transfers between devices  20.8 us (44%)
  starting transfers between devices  18.5 us (39%)
  Pallas kernels  4.27 us (9%)
  local copies, waits for them, and re-layouts  1.8 us (4%)
  between operations  0.78 us (2%)
  other arithmetic  0.73 us (2%)
    ppermute x17, waiting for transfers between devices, swap(): return lax.ppermute(value, axis, [(i, i ^ distance) for i in range(size)])  20.8 us
    ppermute x17, starting transfers between devices, swap(): return lax.ppermute(value, axis, [(i, i ^ distance) for i in range(size)])  18.5 us
    unnamed x12, local copies, waits for them, and re-layouts  1.72 us
  transfers between devices with their start and end apart: 17, of which 13 were waited for; matrix products, arithmetic and copies ran while one was open for 0% of the time, Pallas kernels for 7%

profile of v3, /device:TPU:0, one launch (start us, length us, event | category | flops | bytes accessed | tf_op | source)
XLA Modules:
  0.0 46.8 jit_solution(9372971722333742073)
XLA Ops:
  0.6 0.0 copy-start.5
  0.6 4.1 %collective-permute-start = (bf16[128,256]{1,0:T(8,128)(2,1)}, bf16[128,256]{1,0:T(8,128)(2,1)S(1)}, u32[]{:S(2)}, u32[]{:S(2)}) collective-permute-start(bf16[128,256]{1,0:T(8,128)(2,1)} %refs_0_.1), channel_id=1, source_target_pairs={{0,2},{1,3},{2,0},{3,1},{4,6},{5,7},{6,4},{7,5},{8,10},{9,11},{10,... | collective-permute-start | bytes 196616 | tf_op jit(solution)/shard_map/ppermute | solution.py:30
  4.7 1.3 %collective-permute-start.1 = (bf16[128,256]{1,0:T(8,128)(2,1)}, bf16[128,256]{1,0:T(8,128)(2,1)S(1)}, u32[]{:S(2)}, u32[]{:S(2)}) collective-permute-start(bf16[128,256]{1,0:T(8,128)(2,1)} %refs_0_.1), channel_id=1, source_target_pairs={{0,3},{1,2},{2,1},{3,0},{4,7},{5,6},{6,5},{7,4},{8,11},{9,10},{10,... | collective-permute-start | bytes 196616 | tf_op jit(solution)/shard_map/ppermute | solution.py:30
  6.1 0.2 collective-permute-start.2
  6.3 0.0 copy-done.5
  6.3 0.1 copy.9.rows_ref
  6.4 0.0 copy-start.4
  6.4 0.7 %copy-done.4 = s32[1,8,1]{1,2,0:T(1,128)S(1)} copy-done((s32[1,8,1]{1,2,0:T(1,128)S(1)}, s32[1,8,1]{1,2,0:T(1,128)}, u32[]{:S(2)}) %copy-start.4) | copy-done | bytes 56
  7.1 0.0 copy-start.1
  7.1 1.0 %copy-done.1 = bf16[1,8,1,128,256]{4,3,2,1,0:T(8,128)(2,1)S(1)} copy-done((bf16[1,8,1,128,256]{4,3,2,1,0:T(8,128)(2,1)S(1)}, bf16[1,8,1,128,256]{4,3,2,1,0:T(8,128)(2,1)}, u32[]{:S(2)}) %copy-start.1) | copy-done | bytes 524312
  8.1 0.0 copy-start.2
  8.1 0.8 %shard_map.85.dense_ref = bf16[1024,512]{1,0:T(8,128)(2,1)S(1)} custom-call(s32[8,2]{1,0:T(8,128)S(1)} %copy.9.rows_ref, s32[8]{0:T(128)S(1)} %bitcast.4, bf16[8,128,256]{2,1,0:T(8,128)(2,1)S(1)} %bitcast.3), custom_call_target="tpu_custom_call" | custom-call | bytes 2097152 | tf_op jit(solution)/shard_map/pallas_call | solution.py:62
  8.9 0.0 collective-permute-done.refs_1_
  9.0 2.2 %collective-permute-done.1.refs_2_ = bf16[128,256]{1,0:T(8,128)(2,1)S(1)} collective-permute-done((bf16[128,256]{1,0:T(8,128)(2,1)}, bf16[128,256]{1,0:T(8,128)(2,1)S(1)}, u32[]{:S(2)}, u32[]{:S(2)}) %collective-permute-start.1) | collective-permute-done | bytes 65568 | tf_op jit(solution)/shard_map/ppermute | solution.py:30
  11.2 0.1 collective-permute-done.2.refs_3_
  11.3 0.0 copy-done.2
  11.3 0.2 shard_map.87
  11.5 0.1 collective-permute-start.3
  11.5 0.4 shard_map.86
  12.0 0.8 %collective-permute-done.3.other_ref = bf16[128,256]{1,0:T(8,128)(2,1)S(1)} collective-permute-done((bf16[128,256]{1,0:T(8,128)(2,1)S(1)}, bf16[128,256]{1,0:T(8,128)(2,1)S(1)}, u32[]{:S(2)}, u32[]{:S(2)}) %collective-permute-start.3) | collective-permute-done | bytes 65568 | tf_op jit(solution)/shard_map/ppermute | solution.py:30
  12.8 0.2 collective-permute-start.4
  13.0 0.0 copy-start
  13.0 0.0 copy-start.3
  13.0 2.5 %collective-permute-start.5 = (bf16[128,256]{1,0:T(8,128)(2,1)S(1)}, bf16[128,256]{1,0:T(8,128)(2,1)S(1)}, u32[]{:S(2)}, u32[]{:S(2)}) collective-permute-start(bf16[128,256]{1,0:T(8,128)(2,1)S(1)} %shard_map.89), channel_id=1, source_target_pairs={{0,24},{4,28},{8,16},{12,20},{16,8},{20,12},{24,0},{28,4},{1,25},{... | collective-permute-start | bytes 196616 | tf_op jit(solution)/shard_map/ppermute | solution.py:30
  15.5 0.0 collective-permute-done.4.other_ref
  15.5 0.6 %collective-permute-start.6 = (bf16[128,256]{1,0:T(8,128)(2,1)S(1)}, bf16[128,256]{1,0:T(8,128)(2,1)S(1)}, u32[]{:S(2)}, u32[]{:S(2)}) collective-permute-start(bf16[128,256]{1,0:T(8,128)(2,1)S(1)} %get-tuple-element.42), channel_id=1, source_target_pairs={{0,8},{4,12},{8,0},{12,4},{16,24},{20,28},{24,16},{28,20},{1,9},{5... | collective-permute-start | bytes 196616 | tf_op jit(solution)/shard_map/ppermute | solution.py:30
  16.1 1.2 %collective-permute-start.7 = (bf16[128,256]{1,0:T(8,128)(2,1)S(1)}, bf16[128,256]{1,0:T(8,128)(2,1)S(1)}, u32[]{:S(2)}, u32[]{:S(2)}) collective-permute-start(bf16[128,256]{1,0:T(8,128)(2,1)S(1)} %get-tuple-element.43), channel_id=1, source_target_pairs={{0,16},{4,20},{8,24},{12,28},{16,0},{20,4},{24,8},{28,12},{1,17},{... | collective-permute-start | bytes 196616 | tf_op jit(solution)/shard_map/ppermute | solution.py:30
  17.3 1.1 %collective-permute-done.5.refs_1_ = bf16[128,256]{1,0:T(8,128)(2,1)S(1)} collective-permute-done((bf16[128,256]{1,0:T(8,128)(2,1)S(1)}, bf16[128,256]{1,0:T(8,128)(2,1)S(1)}, u32[]{:S(2)}, u32[]{:S(2)}) %collective-permute-start.5) | collective-permute-done | bytes 65568 | tf_op jit(solution)/shard_map/ppermute | solution.py:30
  18.4 1.5 %collective-permute-done.6.refs_2_ = bf16[128,256]{1,0:T(8,128)(2,1)S(1)} collective-permute-done((bf16[128,256]{1,0:T(8,128)(2,1)S(1)}, bf16[128,256]{1,0:T(8,128)(2,1)S(1)}, u32[]{:S(2)}, u32[]{:S(2)}) %collective-permute-start.6) | collective-permute-done | bytes 65568 | tf_op jit(solution)/shard_map/ppermute | solution.py:30
  19.9 0.5 %collective-permute-done.7.refs_3_ = bf16[128,256]{1,0:T(8,128)(2,1)S(1)} collective-permute-done((bf16[128,256]{1,0:T(8,128)(2,1)S(1)}, bf16[128,256]{1,0:T(8,128)(2,1)S(1)}, u32[]{:S(2)}, u32[]{:S(2)}) %collective-permute-start.7) | collective-permute-done | bytes 65568 | tf_op jit(solution)/shard_map/ppermute | solution.py:30
  20.4 0.0 copy-done
  20.4 0.0 copy-done.3
  20.4 0.2 shard_map.90.pair_ref.refs_0_
  20.6 2.7 %collective-permute-start.8 = (bf16[256,256]{1,0:T(8,128)(2,1)S(1)}, bf16[256,256]{1,0:T(8,128)(2,1)S(1)}, u32[]{:S(2)}, u32[]{:S(2)}) collective-permute-start(bf16[256,256]{1,0:T(8,128)(2,1)S(1)} %shard_map.90.pair_ref.refs_0_), channel_id=1, source_target_pairs={{0,2},{1,3},{2,0},{3,1},{4,6},{5,7},{6,4},{7,5},{8,10},{9,11},{10,... | collective-permute-start | bytes 393224 | tf_op jit(solution)/shard_map/ppermute | solution.py:30
  23.4 0.6 %collective-permute-start.9 = (bf16[256,256]{1,0:T(8,128)(2,1)S(1)}, bf16[256,256]{1,0:T(8,128)(2,1)S(1)}, u32[]{:S(2)}, u32[]{:S(2)}) collective-permute-start(bf16[256,256]{1,0:T(8,128)(2,1)S(1)} %shard_map.90.pair_ref.refs_0_), channel_id=1, source_target_pairs={{0,3},{1,2},{2,1},{3,0},{4,7},{5,6},{6,5},{7,4},{8,11},{9,10},{10,... | collective-permute-start | bytes 393224 | tf_op jit(solution)/shard_map/ppermute | solution.py:30
  24.0 0.3 collective-permute-start.10
  24.3 0.8 %shard_map.91 = bf16[128,256]{1,0:T(8,128)(2,1)} custom-call(bf16[256,256]{1,0:T(8,128)(2,1)S(1)} %shard_map.90.pair_ref.refs_0_, bf16[256,256]{1,0:T(8,128)(2,1)S(1)} %copy-done), custom_call_target="tpu_custom_call" | custom-call | flops 16777216 | bytes 262144 | tf_op jit(solution)/shard_map/pallas_call | solution.py:213
  25.1 7.2 %collective-permute-done.8.refs_1_ = bf16[256,256]{1,0:T(8,128)(2,1)S(1)} collective-permute-done((bf16[256,256]{1,0:T(8,128)(2,1)S(1)}, bf16[256,256]{1,0:T(8,128)(2,1)S(1)}, u32[]{:S(2)}, u32[]{:S(2)}) %collective-permute-start.8) | collective-permute-done | bytes 131104 | tf_op jit(solution)/shard_map/ppermute | solution.py:30
  32.3 0.0 collective-permute-done.9.refs_2_
  32.3 0.7 %collective-permute-done.10.refs_3_ = bf16[256,256]{1,0:T(8,128)(2,1)S(1)} collective-permute-done((bf16[256,256]{1,0:T(8,128)(2,1)S(1)}, bf16[256,256]{1,0:T(8,128)(2,1)S(1)}, u32[]{:S(2)}, u32[]{:S(2)}) %collective-permute-start.10) | collective-permute-done | bytes 131104 | tf_op jit(solution)/shard_map/ppermute | solution.py:30
  33.0 0.6 %shard_map.92 = (bf16[512,256]{1,0:T(8,128)(2,1)S(1)}, bf16[256,256]{1,0:T(8,128)(2,1)S(1)}, f32[128,256]{1,0:T(8,128)S(1)}) custom-call(bf16[1024,512]{1,0:T(8,128)(2,1)S(1)} %shard_map.85.dense_ref, bf16[256,256]{1,0:T(8,128)(2,1)S(1)} %copy-done, bf16[256,256]{1,0:T(8,128)(2,1)S(1)} %shard_map.90.pair_ref.refs_0_, ...), custom_call_target="tpu_custom_call" | custom-call | flops 268435456 | bytes 524288 | tf_op jit(solution)/shard_map/pallas_call | solution.py:251
  33.6 0.1 collective-permute-start.11
  33.7 0.4 shard_map.93
  34.1 0.9 %collective-permute-done.11.other_ref = bf16[256,256]{1,0:T(8,128)(2,1)S(1)} collective-permute-done((bf16[256,256]{1,0:T(8,128)(2,1)S(1)}, bf16[256,256]{1,0:T(8,128)(2,1)S(1)}, u32[]{:S(2)}, u32[]{:S(2)}) %collective-permute-start.11) | collective-permute-done | bytes 131104 | tf_op jit(solution)/shard_map/ppermute | solution.py:30
  35.0 0.1 collective-permute-start.13
  35.2 2.5 %collective-permute-start.12 = (bf16[256,256]{1,0:T(8,128)(2,1)S(1)}, bf16[256,256]{1,0:T(8,128)(2,1)S(1)}, u32[]{:S(2)}, u32[]{:S(2)}) collective-permute-start(bf16[256,256]{1,0:T(8,128)(2,1)S(1)} %get-tuple-element.56), channel_id=1, source_target_pairs={{0,24},{4,28},{8,16},{12,20},{16,8},{20,12},{24,0},{28,4},{1,25},{... | collective-permute-start | bytes 393224 | tf_op jit(solution)/shard_map/ppermute | solution.py:30
  37.7 0.0 collective-permute-done.13.other_ref
  37.8 0.3 collective-permute-start.14
  38.1 1.5 %collective-permute-start.15 = (bf16[256,256]{1,0:T(8,128)(2,1)S(1)}, bf16[256,256]{1,0:T(8,128)(2,1)S(1)}, u32[]{:S(2)}, u32[]{:S(2)}) collective-permute-start(bf16[256,256]{1,0:T(8,128)(2,1)S(1)} %get-tuple-element.59), channel_id=1, source_target_pairs={{0,16},{4,20},{8,24},{12,28},{16,0},{20,4},{24,8},{28,12},{1,17},{... | collective-permute-start | bytes 393224 | tf_op jit(solution)/shard_map/ppermute | solution.py:30
  39.6 2.9 %collective-permute-done.12.refs_0_ = bf16[256,256]{1,0:T(8,128)(2,1)S(1)} collective-permute-done((bf16[256,256]{1,0:T(8,128)(2,1)S(1)}, bf16[256,256]{1,0:T(8,128)(2,1)S(1)}, u32[]{:S(2)}, u32[]{:S(2)}) %collective-permute-start.12) | collective-permute-done | bytes 131104 | tf_op jit(solution)/shard_map/ppermute | solution.py:30
  42.5 1.9 %collective-permute-done.14.refs_1_ = bf16[256,256]{1,0:T(8,128)(2,1)S(1)} collective-permute-done((bf16[256,256]{1,0:T(8,128)(2,1)S(1)}, bf16[256,256]{1,0:T(8,128)(2,1)S(1)}, u32[]{:S(2)}, u32[]{:S(2)}) %collective-permute-start.14) | collective-permute-done | bytes 131104 | tf_op jit(solution)/shard_map/ppermute | solution.py:30
  44.4 0.3 collective-permute-done.15.refs_2_
  44.8 0.1 collective-permute-start.16
  44.9 0.7 %shard_map.97 = bf16[128,256]{1,0:T(8,128)(2,1)} custom-call(f32[128,256]{1,0:T(8,128)S(1)} %get-tuple-element.60.own_ref, bf16[256,256]{1,0:T(8,128)(2,1)S(1)} %collective-permute-done.12.refs_0_, bf16[256,256]{1,0:T(8,128)(2,1)S(1)} %collective-permute-done.14.refs_1_, bf16[256,256]{1,0:T(8,128)(2,1)S(1)} %collective-permute-done.15.refs_2_), custom_call_target="tpu_custom_call" | custom-call | flops 131072 | bytes 393216 | tf_op jit(solution)/shard_map/pallas_call | solution.py:290
  45.5 0.6 %collective-permute-done.16 = bf16[128,256]{1,0:T(8,128)(2,1)S(1)} collective-permute-done((bf16[128,256]{1,0:T(8,128)(2,1)S(1)}, bf16[128,256]{1,0:T(8,128)(2,1)S(1)}, u32[]{:S(2)}, u32[]{:S(2)}) %collective-permute-start.16) | collective-permute-done | bytes 65568 | tf_op jit(solution)/shard_map/ppermute | solution.py:30
  46.1 0.7 %fusion = f32[256,256]{1,0:T(8,128)} fusion(bf16[128,256]{1,0:T(8,128)(2,1)S(1)} %collective-permute-done.16, bf16[128,256]{1,0:T(8,128)(2,1)S(1)} %shard_map.96, pred[]{:T(512)S(6)} %eq.5), kind=kLoop, calls=%fused_computation.1 | loop fusion | flops 655360 | bytes 393217 | tf_op jit(solution)/shard_map/convert_element_type | solution.py:339
  (5 shorter events, 0.2 us)
Async XLA Ops:
  0.6 5.7 %copy-start.5 = (s32[1,8,1,2]{1,3,2,0:T(2,128)S(1)}, s32[1,8,1,2]{1,3,2,0:T(2,128)}, u32[]{:S(2)}) copy-start(s32[1,8,1,2]{1,3,2,0:T(2,128)} %param.9) | copy-start | bytes 196
  0.6 8.3 %collective-permute-start = (bf16[128,256]{1,0:T(8,128)(2,1)}, bf16[128,256]{1,0:T(8,128)(2,1)S(1)}, u32[]{:S(2)}, u32[]{:S(2)}) collective-permute-start(bf16[128,256]{1,0:T(8,128)(2,1)} %refs_0_.1), channel_id=1, source_target_pairs={{0,2},{1,3},{2,0},{3,1},{4,6},{5,7},{6,4},{7,5},{8,10},{9,11},{10,... | collective-permute-start | bytes 196616 | tf_op jit(solution)/shard_map/ppermute | solution.py:30
  4.7 6.4 %collective-permute-start.1 = (bf16[128,256]{1,0:T(8,128)(2,1)}, bf16[128,256]{1,0:T(8,128)(2,1)S(1)}, u32[]{:S(2)}, u32[]{:S(2)}) collective-permute-start(bf16[128,256]{1,0:T(8,128)(2,1)} %refs_0_.1), channel_id=1, source_target_pairs={{0,3},{1,2},{2,1},{3,0},{4,7},{5,6},{6,5},{7,4},{8,11},{9,10},{10,... | collective-permute-start | bytes 196616 | tf_op jit(solution)/shard_map/ppermute | solution.py:30
  6.1 5.2 %collective-permute-start.2 = (bf16[128,256]{1,0:T(8,128)(2,1)}, bf16[128,256]{1,0:T(8,128)(2,1)S(1)}, u32[]{:S(2)}, u32[]{:S(2)}) collective-permute-start(bf16[128,256]{1,0:T(8,128)(2,1)} %refs_0_.1), channel_id=1, source_target_pairs={{0,1},{1,0},{2,3},{3,2},{4,5},{5,4},{6,7},{7,6},{8,9},{9,8},{10,11... | collective-permute-start | bytes 196616 | tf_op jit(solution)/shard_map/ppermute | solution.py:30
  6.4 0.7 %copy-start.4 = (s32[1,8,1]{1,2,0:T(1,128)S(1)}, s32[1,8,1]{1,2,0:T(1,128)}, u32[]{:S(2)}) copy-start(s32[1,8,1]{1,2,0:T(1,128)} %param.10) | copy-start | bytes 100
  7.1 1.0 %copy-start.1 = (bf16[1,8,1,128,256]{4,3,2,1,0:T(8,128)(2,1)S(1)}, bf16[1,8,1,128,256]{4,3,2,1,0:T(8,128)(2,1)}, u32[]{:S(2)}) copy-start(bf16[1,8,1,128,256]{4,3,2,1,0:T(8,128)(2,1)} %param.11) | copy-start | bytes 1572868
  8.1 3.2 %copy-start.2 = (bf16[128,256]{1,0:T(8,128)(2,1)S(1)}, bf16[128,256]{1,0:T(8,128)(2,1)}, u32[]{:S(2)}) copy-start(bf16[128,256]{1,0:T(8,128)(2,1)} %refs_0_.1) | copy-start | bytes 196612
  11.5 1.3 %collective-permute-start.3 = (bf16[128,256]{1,0:T(8,128)(2,1)S(1)}, bf16[128,256]{1,0:T(8,128)(2,1)S(1)}, u32[]{:S(2)}, u32[]{:S(2)}) collective-permute-start(bf16[128,256]{1,0:T(8,128)(2,1)S(1)} %shard_map.87), channel_id=1, source_target_pairs={{0,4},{4,0},{8,12},{12,8},{16,20},{20,16},{24,28},{28,24},{1,5},{5... | collective-permute-start | bytes 196616 | tf_op jit(solution)/shard_map/ppermute | solution.py:30
  12.8 2.7 %collective-permute-start.4 = (bf16[384,256]{1,0:T(8,128)(2,1)S(1)}, bf16[384,256]{1,0:T(8,128)(2,1)S(1)}, u32[]{:S(2)}, u32[]{:S(2)}) collective-permute-start(bf16[384,256]{1,0:T(8,128)(2,1)S(1)} %get-tuple-element.39), channel_id=1, source_target_pairs={{0,4},{4,0},{8,12},{12,8},{16,20},{20,16},{24,28},{28,24},{1,5},{5... | collective-permute-start | bytes 589832 | tf_op jit(solution)/shard_map/ppermute | solution.py:30
  13.0 7.5 %copy-start = (bf16[256,256]{1,0:T(8,128)(2,1)S(1)}, bf16[256,256]{1,0:T(8,128)(2,1)}, u32[]{:S(2)}) copy-start(bf16[256,256]{1,0:T(8,128)(2,1)} %weight_ref.3) | copy-start | bytes 393220
  13.0 7.4 %copy-start.3 = (bf16[128,256]{1,0:T(8,128)(2,1)S(1)}, bf16[128,256]{1,0:T(8,128)(2,1)}, u32[]{:S(2)}) copy-start(bf16[128,256]{1,0:T(8,128)(2,1)} %refs_5_.1) | copy-start | bytes 196612
  13.0 5.4 %collective-permute-start.5 = (bf16[128,256]{1,0:T(8,128)(2,1)S(1)}, bf16[128,256]{1,0:T(8,128)(2,1)S(1)}, u32[]{:S(2)}, u32[]{:S(2)}) collective-permute-start(bf16[128,256]{1,0:T(8,128)(2,1)S(1)} %shard_map.89), channel_id=1, source_target_pairs={{0,24},{4,28},{8,16},{12,20},{16,8},{20,12},{24,0},{28,4},{1,25},{... | collective-permute-start | bytes 196616 | tf_op jit(solution)/shard_map/ppermute | solution.py:30
  15.5 4.3 %collective-permute-start.6 = (bf16[128,256]{1,0:T(8,128)(2,1)S(1)}, bf16[128,256]{1,0:T(8,128)(2,1)S(1)}, u32[]{:S(2)}, u32[]{:S(2)}) collective-permute-start(bf16[128,256]{1,0:T(8,128)(2,1)S(1)} %get-tuple-element.42), channel_id=1, source_target_pairs={{0,8},{4,12},{8,0},{12,4},{16,24},{20,28},{24,16},{28,20},{1,9},{5... | collective-permute-start | bytes 196616 | tf_op jit(solution)/shard_map/ppermute | solution.py:30
  16.1 4.3 %collective-permute-start.7 = (bf16[128,256]{1,0:T(8,128)(2,1)S(1)}, bf16[128,256]{1,0:T(8,128)(2,1)S(1)}, u32[]{:S(2)}, u32[]{:S(2)}) collective-permute-start(bf16[128,256]{1,0:T(8,128)(2,1)S(1)} %get-tuple-element.43), channel_id=1, source_target_pairs={{0,16},{4,20},{8,24},{12,28},{16,0},{20,4},{24,8},{28,12},{1,17},{... | collective-permute-start | bytes 196616 | tf_op jit(solution)/shard_map/ppermute | solution.py:30
  20.6 11.6 %collective-permute-start.8 = (bf16[256,256]{1,0:T(8,128)(2,1)S(1)}, bf16[256,256]{1,0:T(8,128)(2,1)S(1)}, u32[]{:S(2)}, u32[]{:S(2)}) collective-permute-start(bf16[256,256]{1,0:T(8,128)(2,1)S(1)} %shard_map.90.pair_ref.refs_0_), channel_id=1, source_target_pairs={{0,2},{1,3},{2,0},{3,1},{4,6},{5,7},{6,4},{7,5},{8,10},{9,11},{10,... | collective-permute-start | bytes 393224 | tf_op jit(solution)/shard_map/ppermute | solution.py:30
  23.4 8.9 %collective-permute-start.9 = (bf16[256,256]{1,0:T(8,128)(2,1)S(1)}, bf16[256,256]{1,0:T(8,128)(2,1)S(1)}, u32[]{:S(2)}, u32[]{:S(2)}) collective-permute-start(bf16[256,256]{1,0:T(8,128)(2,1)S(1)} %shard_map.90.pair_ref.refs_0_), channel_id=1, source_target_pairs={{0,3},{1,2},{2,1},{3,0},{4,7},{5,6},{6,5},{7,4},{8,11},{9,10},{10,... | collective-permute-start | bytes 393224 | tf_op jit(solution)/shard_map/ppermute | solution.py:30
  24.0 9.0 %collective-permute-start.10 = (bf16[256,256]{1,0:T(8,128)(2,1)S(1)}, bf16[256,256]{1,0:T(8,128)(2,1)S(1)}, u32[]{:S(2)}, u32[]{:S(2)}) collective-permute-start(bf16[256,256]{1,0:T(8,128)(2,1)S(1)} %shard_map.90.pair_ref.refs_0_), channel_id=1, source_target_pairs={{0,1},{1,0},{2,3},{3,2},{4,5},{5,4},{6,7},{7,6},{8,9},{9,8},{10,11... | collective-permute-start | bytes 393224 | tf_op jit(solution)/shard_map/ppermute | solution.py:30
  33.6 1.4 %collective-permute-start.11 = (bf16[256,256]{1,0:T(8,128)(2,1)S(1)}, bf16[256,256]{1,0:T(8,128)(2,1)S(1)}, u32[]{:S(2)}, u32[]{:S(2)}) collective-permute-start(bf16[256,256]{1,0:T(8,128)(2,1)S(1)} %get-tuple-element.52), channel_id=1, source_target_pairs={{0,4},{4,0},{8,12},{12,8},{16,20},{20,16},{24,28},{28,24},{1,5},{5... | collective-permute-start | bytes 393224 | tf_op jit(solution)/shard_map/ppermute | solution.py:30
  35.0 2.7 %collective-permute-start.13 = (bf16[384,256]{1,0:T(8,128)(2,1)S(1)}, bf16[384,256]{1,0:T(8,128)(2,1)S(1)}, u32[]{:S(2)}, u32[]{:S(2)}) collective-permute-start(bf16[384,256]{1,0:T(8,128)(2,1)S(1)} %get-tuple-element.57), channel_id=1, source_target_pairs={{0,4},{4,0},{8,12},{12,8},{16,20},{20,16},{24,28},{28,24},{1,5},{5... | collective-permute-start | bytes 589832 | tf_op jit(solution)/shard_map/ppermute | solution.py:30
  35.2 7.3 %collective-permute-start.12 = (bf16[256,256]{1,0:T(8,128)(2,1)S(1)}, bf16[256,256]{1,0:T(8,128)(2,1)S(1)}, u32[]{:S(2)}, u32[]{:S(2)}) collective-permute-start(bf16[256,256]{1,0:T(8,128)(2,1)S(1)} %get-tuple-element.56), channel_id=1, source_target_pairs={{0,24},{4,28},{8,16},{12,20},{16,8},{20,12},{24,0},{28,4},{1,25},{... | collective-permute-start | bytes 393224 | tf_op jit(solution)/shard_map/ppermute | solution.py:30
  37.8 6.6 %collective-permute-start.14 = (bf16[256,256]{1,0:T(8,128)(2,1)S(1)}, bf16[256,256]{1,0:T(8,128)(2,1)S(1)}, u32[]{:S(2)}, u32[]{:S(2)}) collective-permute-start(bf16[256,256]{1,0:T(8,128)(2,1)S(1)} %get-tuple-element.58), channel_id=1, source_target_pairs={{0,8},{4,12},{8,0},{12,4},{16,24},{20,28},{24,16},{28,20},{1,9},{5... | collective-permute-start | bytes 393224 | tf_op jit(solution)/shard_map/ppermute | solution.py:30
  38.1 6.6 %collective-permute-start.15 = (bf16[256,256]{1,0:T(8,128)(2,1)S(1)}, bf16[256,256]{1,0:T(8,128)(2,1)S(1)}, u32[]{:S(2)}, u32[]{:S(2)}) collective-permute-start(bf16[256,256]{1,0:T(8,128)(2,1)S(1)} %get-tuple-element.59), channel_id=1, source_target_pairs={{0,16},{4,20},{8,24},{12,28},{16,0},{20,4},{24,8},{28,12},{1,17},{... | collective-permute-start | bytes 393224 | tf_op jit(solution)/shard_map/ppermute | solution.py:30
  44.8 1.3 %collective-permute-start.16 = (bf16[128,256]{1,0:T(8,128)(2,1)S(1)}, bf16[128,256]{1,0:T(8,128)(2,1)S(1)}, u32[]{:S(2)}, u32[]{:S(2)}) collective-permute-start(bf16[128,256]{1,0:T(8,128)(2,1)S(1)} %shard_map.96), channel_id=1, source_target_pairs={{0,4},{4,0},{8,12},{12,8},{16,20},{20,16},{24,28},{28,24},{1,5},{5... | collective-permute-start | bytes 196616 | tf_op jit(solution)/shard_map/ppermute | solution.py:30

commit v4 on v3

--- a/solution.py
+++ b/solution.py
@@ -10,6 +10,7 @@
 
 F32 = jnp.float32
 BF16 = jnp.bfloat16
+ROWS = (((0,), (0,)), ((), ()))
 VMEM_LIMIT = 8 * 1024 * 1024
 
 
@@ -25,25 +26,30 @@
     return pltpu.CompilerParams(vmem_limit_bytes=VMEM_LIMIT)
 
 
-def swap(value, axis, distance):
-    size = lax.axis_size(axis)
-    return lax.ppermute(value, axis, [(i, i ^ distance) for i in range(size)])
-
-
-def far_order(slabs):
-    return sorted(range(2, slabs, 2), key=lambda d: -bin(d).count("1"))
+def send(value, axis, step):
+    return lax.ppermute(value, axis, [(i, step(i)) for i in range(lax.axis_size(axis))])
+
+
+def at(distance):
+    return lambda i: i ^ distance
+
+
+def far_steps(slabs):
+    if slabs == 8:
+        return [at(6), at(2), at(4)]
+    return [at(2)]
 
 
 def sub_order(subs):
     return [2, 3, 1] if subs == 4 else [1]
 
 
-def dense_kernel(order, subs, rows_ref, counts_ref, tiles_ref, out_ref):
+def dense_kernel(steps, subs, rows_ref, counts_ref, tiles_ref, out_ref):
     me, mine = lax.axis_index("blk"), lax.axis_index("rep")
     block = tiles_ref.shape[1]
     slots = tiles_ref.shape[2] // block
-    for q, distance in enumerate(order):
-        slab = me ^ distance
+    for q, step in enumerate(steps):
+        slab = step(me)
         tile = tiles_ref[slab]
         turned = [tile[:, k * block : (k + 1) * block].T for k in range(slots)]
         places = [
@@ -56,11 +62,11 @@
             out_ref[q * block : (q + 1) * block, b * block : (b + 1) * block] = value
 
 
-def dense_adjacency(order, subs, rows, counts, tiles):
+def dense_adjacency(steps, subs, rows, counts, tiles):
     block = tiles.shape[1]
-    shape = (len(order) * block, len(subs) * block)
-    return pl.pallas_call(
-        functools.partial(dense_kernel, order, subs),
+    shape = (len(steps) * block, len(subs) * block)
+    return pl.pallas_call(
+        functools.partial(dense_kernel, steps, subs),
         out_shape=jax.ShapeDtypeStruct(shape, tiles.dtype),
         in_specs=[smem(), smem(), vmem()],
         out_specs=vmem(),
@@ -91,8 +97,8 @@
     )(dense, *pieces)
 
 
-def rest_kernel(n_pieces, dense_ref, *refs):
-    nodes = jnp.concatenate([piece[...] for piece in refs[:n_pieces]], axis=0)
+def rest_kernel(block, n_pieces, dense_ref, *refs):
+    nodes = jnp.concatenate([piece[-block:, :] for piece in refs[:n_pieces]], axis=0)
     odd_ref, even_ref = refs[n_pieces:]
     half = dense_ref.shape[0] // 2
     rows = dense_ref[dense_ref.shape[0] - odd_ref.shape[0] :, :]
@@ -103,7 +109,7 @@
 def apply_rest(dense, pieces, block):
     rows, feat = dense.shape[0] // 2, pieces[0].shape[1]
     return pl.pallas_call(
-        functools.partial(rest_kernel, len(pieces)),
+        functools.partial(rest_kernel, block, len(pieces)),
         out_shape=[jax.ShapeDtypeStruct((rows - block, feat), BF16), jax.ShapeDtypeStruct((rows, feat), F32)],
         in_specs=[vmem()] * (1 + len(pieces)),
         out_specs=[vmem()] * 2,
@@ -145,9 +151,9 @@
     half, (own_ref, *outs) = refs[:n_half], refs[n_half:]
     block = own_ref.shape[0]
     for q, out in enumerate([own_ref] + outs):
-        total = even_ref[(q + 1) * block : (q + 2) * block, :]
-        total = total + other_ref[q * block : (q + 1) * block, :].astype(F32)
-        out[:block, :] = total.astype(out.dtype)
+        both = even_ref[(q + 1) * block : (q + 2) * block, :]
+        both = both + other_ref[q * block : (q + 1) * block, :].astype(F32)
+        out[:block, :] = both.astype(out.dtype)
         if half and q:
             out[block:, :] = half[0][...]
 
@@ -168,20 +174,18 @@
     )(even, other, *half)
 
 
-def tree(order, values):
-    values = [value.astype(F32) for _, value in sorted(zip(order, values), key=lambda pair: pair[0])]
-    while len(values) > 1:
-        values = [values[k] + values[k + 1] for k in range(0, len(values), 2)]
-    return values[0]
+def total(values):
+    values = [value.astype(F32) for value in values]
+    if len(values) == 2:
+        return values[0] + values[1]
+    mine, across, one, other = values
+    return (mine + across) + (one + other)
 
 
 def layer_kernel(n_parts, *refs):
     parts, (weight_ref, cotangent_ref, pair_ref) = refs[:n_parts], refs[n_parts:]
     block = cotangent_ref.shape[0]
-    total = parts[0][...]
-    for part in parts[1:]:
-        total = total + part[...].astype(F32)
-    agg = total.astype(BF16)
+    agg = total([part[...] for part in parts]).astype(BF16)
     pre = jnp.dot(agg, weight_ref[...], preferred_element_type=F32)
     sig = 1.0 / (1.0 + jnp.exp(-pre))
     dpre = cotangent_ref[...].astype(F32) * sig * (1.0 + pre * (1.0 - sig))
@@ -222,54 +226,61 @@
     )(pair, weight)
 
 
-def back_kernel(scale, n_pairs, dense_ref, weight_ref, *refs):
-    pairs, (back_ref, first_ref, keep_ref) = refs[:n_pairs], refs[n_pairs:]
+def in_order(pairs, one, two):
+    mine = lax.axis_index("rep")
+    flip = (mine ^ one) > (mine ^ two)
+    first, second = pairs[one][...], pairs[two][...]
+    return jnp.where(flip, second, first), jnp.where(flip, first, second)
+
+
+def pair_kernel(scale, order, groups, dense_ref, *refs):
+    pairs = dict(zip(order, refs))
+    first_ref, keep_ref = refs[len(order) :]
     block = pairs[0].shape[0] // 2
-    dpre = jnp.concatenate([pair[block:, :] for pair in pairs], axis=0)
-    back = lax.dot_general(
-        dpre, weight_ref[...], (((1,), (1,)), ((), ())), preferred_element_type=F32
-    ).astype(BF16)
-    back_ref[...] = back
+    dpre = jnp.concatenate([pairs[d][block:, :] for d in order], axis=0)
     rows = dense_ref.shape[0] // 2
-    first = jnp.dot(dense_ref[rows : rows + block, :], back, preferred_element_type=F32)
+    first = jnp.dot(dense_ref[rows : rows + block, :], dpre, preferred_element_type=F32)
     first_ref[:block, :] = first.astype(BF16)
-    agg = jnp.concatenate([pair[:block, :] for pair in pairs], axis=0)
-    half = agg.shape[1] // 2
-    upper, lower = (
-        lax.dot_general(cols, dpre, (((0,), (0,)), ((), ())), preferred_element_type=F32) * scale
-        for cols in (agg[:, :half], agg[:, half:])
-    )
+    half = first_ref.shape[1] // 2
+    upper = lower = 0.0
+    for one, two in groups:
+        low, high = in_order(pairs, one, two)
+        agg = jnp.concatenate([low[:block, :], high[:block, :]], axis=0)
+        dpre = jnp.concatenate([low[block:, :], high[block:, :]], axis=0)
+        upper = upper + lax.dot_general(agg[:, :half], dpre, ROWS, preferred_element_type=F32)
+        lower = lower + lax.dot_general(agg[:, half:], dpre, ROWS, preferred_element_type=F32)
+    upper, lower = upper * scale, lower * scale
     is_first = lax.axis_index("blk") % 2 == 0
     first_ref[block:, :] = jnp.where(is_first, lower, upper).astype(BF16)
     keep_ref[...] = jnp.where(is_first, upper, lower)
 
 
-def apply_back(dense, weight, pairs, scale):
-    feat = weight.shape[0]
+def apply_pairs(dense, pairs, order, scale):
+    feat = pairs[0].shape[1]
     block, half = pairs[0].shape[0] // 2, feat // 2
-    shapes = ((len(pairs) * block, BF16), (block + half, BF16), (half, F32))
-    return pl.pallas_call(
-        functools.partial(back_kernel, scale, len(pairs)),
+    groups = [(d, d + len(order) // 2) for d in range(len(order) // 2)]
+    shapes = ((block + half, BF16), (half, F32))
+    return pl.pallas_call(
+        functools.partial(pair_kernel, scale, order, groups),
         out_shape=[jax.ShapeDtypeStruct((n, feat), t) for n, t in shapes],
-        in_specs=[vmem()] * (2 + len(pairs)),
-        out_specs=[vmem()] * 3,
+        in_specs=[vmem()] * (1 + len(pairs)),
+        out_specs=[vmem()] * 2,
         compiler_params=params(),
         cost_estimate=pl.CostEstimate(
-            flops=8 * len(pairs) * block * feat * feat, bytes_accessed=dense.size, transcendentals=0
+            flops=6 * len(pairs) * block * feat * feat, bytes_accessed=dense.size, transcendentals=0
         ),
-    )(dense, weight, *pairs)
-
-
-def half_kernel(order, half_ref, *refs):
+    )(dense, *pairs)
+
+
+def half_kernel(half_ref, *refs):
     parts, out_ref = refs[:-1], refs[-1]
     more = half_ref.shape[0]
-    total = tree(order, [half_ref[...]] + [part[-more:, :] for part in parts])
-    out_ref[...] = total.astype(out_ref.dtype)
-
-
-def half_sum(order, half, parts):
-    return pl.pallas_call(
-        functools.partial(half_kernel, order),
+    out_ref[...] = total([half_ref[...]] + [part[-more:, :] for part in parts]).astype(out_ref.dtype)
+
+
+def half_sum(half, parts):
+    return pl.pallas_call(
+        half_kernel,
         out_shape=jax.ShapeDtypeStruct(half.shape, BF16),
         in_specs=[vmem()] * (1 + len(parts)),
         out_specs=vmem(),
@@ -278,31 +289,32 @@
     )(half, *parts)
 
 
-def last_kernel(own_ref, *refs):
+def last_kernel(weight_ref, own_ref, *refs):
     parts, out_ref = refs[:-1], refs[-1]
-    total = own_ref[...]
-    for part in parts:
-        total = total + part[: own_ref.shape[0], :].astype(F32)
-    out_ref[...] = total.astype(out_ref.dtype)
-
-
-def last_sum(own, parts):
+    block = own_ref.shape[0]
+    rows = total([own_ref[...]] + [part[:block, :] for part in parts]).astype(BF16)
+    out_ref[...] = lax.dot_general(
+        rows, weight_ref[...], (((1,), (1,)), ((), ())), preferred_element_type=F32
+    ).astype(out_ref.dtype)
+
+
+def last_product(weight, own, parts):
     return pl.pallas_call(
         last_kernel,
         out_shape=jax.ShapeDtypeStruct(own.shape, BF16),
-        in_specs=[vmem()] * (1 + len(parts)),
-        out_specs=vmem(),
-        compiler_params=params(),
-        cost_estimate=pl.CostEstimate(flops=own.size * 4, bytes_accessed=own.size * 12, transcendentals=0),
-    )(own, *parts)
-
-
-def exchange(value, axis, distances):
-    return [value] + [swap(value, axis, d) for d in distances]
+        in_specs=[vmem()] * (2 + len(parts)),
+        out_specs=vmem(),
+        compiler_params=params(),
+        cost_estimate=pl.CostEstimate(flops=2 * own.size * own.shape[1], bytes_accessed=own.size * 12, transcendentals=0),
+    )(weight, own, *parts)
+
+
+def gather(value, order):
+    return [value] + [send(value, "rep", at(d)) for d in order]
 
 
 def join(mine):
-    other = swap(mine, "blk", 1)
+    other = send(mine, "blk", at(1))
     is_first = lax.axis_index("blk") % 2 == 0
     return jnp.where(
         is_first, jnp.concatenate([mine, other], axis=0), jnp.concatenate([other, mine], axis=0)
@@ -312,32 +324,33 @@
 def shards_direct(features, weight, cotangent, rows, counts, tiles):
     block = features.shape[0]
     slabs, subs = lax.axis_size("blk"), lax.axis_size("rep")
-    far, near = far_order(slabs), sub_order(subs)
+    far, near = far_steps(slabs), sub_order(subs)
     node_count = block * slabs * subs
-    even = far[:1] + [0] + far[1:]
-    dense = dense_adjacency(even + [d + 1 for d in even], [0] + near, rows, counts, tiles)
-
-    pieces, dense = lax.optimization_barrier((exchange(features, "rep", near), dense))
-    other = swap(apply_first(dense, pieces), "blk", 1)
+    even = far[:1] + [at(0)] + far[1:]
+    odd = [lambda i, step=step: step(i) ^ 1 for step in even]
+    dense = dense_adjacency(even + odd, [0] + near, rows, counts, tiles)
+
+    pieces, dense = lax.optimization_barrier((gather(features, near), dense))
+    other = send(apply_first(dense, pieces), "blk", at(1))
     rest, mine = apply_rest(dense, pieces, block)
     rest, other = lax.optimization_barrier((rest, other))
     (first,) = first_sum(mine, other, block)
-    own, *sums = rest_sums(mine, swap(rest, "blk", 1), block)
-    parts = [swap(value, "blk", d) for value, d in zip([first] + sums, far)]
+    own, *sums = rest_sums(mine, send(rest, "blk", at(1)), block)
+    parts = [send(value, "blk", step) for value, step in zip([first] + sums, far)]
 
     pair = layer([own] + parts, weight, cotangent)
-    pairs = exchange(pair, "rep", near)
+    pairs = gather(pair, near)
     activation = layer_output(pair, weight)
     pairs, activation = lax.optimization_barrier((pairs, activation))
-    back, first, keep = apply_back(dense, weight, pairs, 1.0 / math.sqrt(node_count))
-    other = swap(first, "blk", 1)
-    rest, mine = apply_rest(dense, [back], block)
+    first, keep = apply_pairs(dense, pairs, [0] + near, 1.0 / math.sqrt(node_count))
+    other = send(first, "blk", at(1))
+    rest, mine = apply_rest(dense, pairs, block)
     rest, other = lax.optimization_barrier((rest, other))
     first, half = first_sum(mine, other, block, keep)
-    own, *sums = rest_sums(mine, swap(rest, "blk", 1), block, half)
-    parts = [swap(value, "blk", d) for value, d in zip([first] + sums, far)]
-    grad = join(half_sum([0] + far, half, parts)).astype(F32)
-    return activation, grad, last_sum(own, parts)
+    own, *sums = rest_sums(mine, send(rest, "blk", at(1)), block, half)
+    parts = [send(value, "blk", step) for value, step in zip([first] + sums, far)]
+    grad = join(half_sum(half, parts)).astype(F32)
+    return activation, grad, last_product(weight, own, parts)
 
 
 def add_tile(running, column_block, node_slab, tiles, slot_rows, slot_counts):

time: 47 us -> 46.7 us (level)
  no operation moved by 1% of the time
where the time goes in v4:
time: 46.7 us; the launch traced here: 46.5 us
  waiting for transfers between devices  20.6 us (44%)
  starting transfers between devices  18.5 us (40%)
  Pallas kernels  4.15 us (9%)
  local copies, waits for them, and re-layouts  1.8 us (4%)
  between operations  0.77 us (2%)
  other arithmetic  0.73 us (2%)
    ppermute x17, waiting for transfers between devices, send(): lax.ppermute(value, axis, [(i, step(i)) for i in range(lax.axis_size(axis...  20.6 us
    ppermute x17, starting transfers between devices, send(): lax.ppermute(value, axis, [(i, step(i)) for i in range(lax.axis_size(axis...  18.5 us
    unnamed x12, local copies, waits for them, and re-layouts  1.72 us
  transfers between devices with their start and end apart: 17, of which 13 were waited for; matrix products, arithmetic and copies ran while one was open for 0% of the time, Pallas kernels for 7%

profile of v4, /device:TPU:0, one launch (start us, length us, event | category | flops | bytes accessed | tf_op | source)
XLA Modules:
  0.0 46.5 jit_solution(15077011157297389084)
XLA Ops:
  0.6 0.0 copy-start.5
  0.6 4.1 %collective-permute-start = (bf16[128,256]{1,0:T(8,128)(2,1)}, bf16[128,256]{1,0:T(8,128)(2,1)S(1)}, u32[]{:S(2)}, u32[]{:S(2)}) collective-permute-start(bf16[128,256]{1,0:T(8,128)(2,1)} %refs_0_.1), channel_id=1, source_target_pairs={{0,2},{1,3},{2,0},{3,1},{4,6},{5,7},{6,4},{7,5},{8,10},{9,11},{10,... | collective-permute-start | bytes 196616 | tf_op jit(solution)/shard_map/ppermute | solution.py:30
  4.7 1.3 %collective-permute-start.1 = (bf16[128,256]{1,0:T(8,128)(2,1)}, bf16[128,256]{1,0:T(8,128)(2,1)S(1)}, u32[]{:S(2)}, u32[]{:S(2)}) collective-permute-start(bf16[128,256]{1,0:T(8,128)(2,1)} %refs_0_.1), channel_id=1, source_target_pairs={{0,3},{1,2},{2,1},{3,0},{4,7},{5,6},{6,5},{7,4},{8,11},{9,10},{10,... | collective-permute-start | bytes 196616 | tf_op jit(solution)/shard_map/ppermute | solution.py:30
  6.1 0.2 collective-permute-start.2
  6.3 0.0 copy-done.5
  6.3 0.1 copy.9.rows_ref
  6.4 0.0 copy-start.4
  6.4 0.7 %copy-done.4 = s32[1,8,1]{1,2,0:T(1,128)S(1)} copy-done((s32[1,8,1]{1,2,0:T(1,128)S(1)}, s32[1,8,1]{1,2,0:T(1,128)}, u32[]{:S(2)}) %copy-start.4) | copy-done | bytes 56
  7.1 0.0 copy-start.1
  7.1 1.0 %copy-done.1 = bf16[1,8,1,128,256]{4,3,2,1,0:T(8,128)(2,1)S(1)} copy-done((bf16[1,8,1,128,256]{4,3,2,1,0:T(8,128)(2,1)S(1)}, bf16[1,8,1,128,256]{4,3,2,1,0:T(8,128)(2,1)}, u32[]{:S(2)}) %copy-start.1) | copy-done | bytes 524312
  8.1 0.0 copy-start.2
  8.1 0.8 %shard_map.85.dense_ref = bf16[1024,512]{1,0:T(8,128)(2,1)S(1)} custom-call(s32[8,2]{1,0:T(8,128)S(1)} %copy.9.rows_ref, s32[8]{0:T(128)S(1)} %bitcast.4, bf16[8,128,256]{2,1,0:T(8,128)(2,1)S(1)} %bitcast.3), custom_call_target="tpu_custom_call" | custom-call | bytes 2097152 | tf_op jit(solution)/shard_map/pallas_call | solution.py:68
  8.9 0.0 collective-permute-done.refs_1_
  9.0 2.2 %collective-permute-done.1.refs_2_ = bf16[128,256]{1,0:T(8,128)(2,1)S(1)} collective-permute-done((bf16[128,256]{1,0:T(8,128)(2,1)}, bf16[128,256]{1,0:T(8,128)(2,1)S(1)}, u32[]{:S(2)}, u32[]{:S(2)}) %collective-permute-start.1) | collective-permute-done | bytes 65568 | tf_op jit(solution)/shard_map/ppermute | solution.py:30
  11.2 0.1 collective-permute-done.2.refs_3_
  11.3 0.0 copy-done.2
  11.3 0.2 shard_map.87
  11.5 0.1 collective-permute-start.3
  11.5 0.4 shard_map.86
  12.0 0.8 %collective-permute-done.3.other_ref = bf16[128,256]{1,0:T(8,128)(2,1)S(1)} collective-permute-done((bf16[128,256]{1,0:T(8,128)(2,1)S(1)}, bf16[128,256]{1,0:T(8,128)(2,1)S(1)}, u32[]{:S(2)}, u32[]{:S(2)}) %collective-permute-start.3) | collective-permute-done | bytes 65568 | tf_op jit(solution)/shard_map/ppermute | solution.py:30
  12.8 0.2 collective-permute-start.4
  13.0 0.0 copy-start
  13.0 0.0 copy-start.3
  13.0 2.5 %collective-permute-start.5 = (bf16[128,256]{1,0:T(8,128)(2,1)S(1)}, bf16[128,256]{1,0:T(8,128)(2,1)S(1)}, u32[]{:S(2)}, u32[]{:S(2)}) collective-permute-start(bf16[128,256]{1,0:T(8,128)(2,1)S(1)} %shard_map.89), channel_id=1, source_target_pairs={{0,24},{4,28},{8,16},{12,20},{16,8},{20,12},{24,0},{28,4},{1,25},{... | collective-permute-start | bytes 196616 | tf_op jit(solution)/shard_map/ppermute | solution.py:30
  15.5 0.0 collective-permute-done.4.other_ref
  15.5 0.6 %collective-permute-start.6 = (bf16[128,256]{1,0:T(8,128)(2,1)S(1)}, bf16[128,256]{1,0:T(8,128)(2,1)S(1)}, u32[]{:S(2)}, u32[]{:S(2)}) collective-permute-start(bf16[128,256]{1,0:T(8,128)(2,1)S(1)} %get-tuple-element.41), channel_id=1, source_target_pairs={{0,8},{4,12},{8,0},{12,4},{16,24},{20,28},{24,16},{28,20},{1,9},{5... | collective-permute-start | bytes 196616 | tf_op jit(solution)/shard_map/ppermute | solution.py:30
  16.1 1.2 %collective-permute-start.7 = (bf16[128,256]{1,0:T(8,128)(2,1)S(1)}, bf16[128,256]{1,0:T(8,128)(2,1)S(1)}, u32[]{:S(2)}, u32[]{:S(2)}) collective-permute-start(bf16[128,256]{1,0:T(8,128)(2,1)S(1)} %get-tuple-element.42), channel_id=1, source_target_pairs={{0,16},{4,20},{8,24},{12,28},{16,0},{20,4},{24,8},{28,12},{1,17},{... | collective-permute-start | bytes 196616 | tf_op jit(solution)/shard_map/ppermute | solution.py:30
  17.3 1.1 %collective-permute-done.5.refs_1_ = bf16[128,256]{1,0:T(8,128)(2,1)S(1)} collective-permute-done((bf16[128,256]{1,0:T(8,128)(2,1)S(1)}, bf16[128,256]{1,0:T(8,128)(2,1)S(1)}, u32[]{:S(2)}, u32[]{:S(2)}) %collective-permute-start.5) | collective-permute-done | bytes 65568 | tf_op jit(solution)/shard_map/ppermute | solution.py:30
  18.4 1.5 %collective-permute-done.6.refs_2_ = bf16[128,256]{1,0:T(8,128)(2,1)S(1)} collective-permute-done((bf16[128,256]{1,0:T(8,128)(2,1)S(1)}, bf16[128,256]{1,0:T(8,128)(2,1)S(1)}, u32[]{:S(2)}, u32[]{:S(2)}) %collective-permute-start.6) | collective-permute-done | bytes 65568 | tf_op jit(solution)/shard_map/ppermute | solution.py:30
  19.9 0.5 %collective-permute-done.7.refs_3_ = bf16[128,256]{1,0:T(8,128)(2,1)S(1)} collective-permute-done((bf16[128,256]{1,0:T(8,128)(2,1)S(1)}, bf16[128,256]{1,0:T(8,128)(2,1)S(1)}, u32[]{:S(2)}, u32[]{:S(2)}) %collective-permute-start.7) | collective-permute-done | bytes 65568 | tf_op jit(solution)/shard_map/ppermute | solution.py:30
  20.4 0.0 copy-done
  20.4 0.0 copy-done.3
  20.4 0.2 shard_map.90.pair_ref.refs_0_
  20.6 2.7 %collective-permute-start.8 = (bf16[256,256]{1,0:T(8,128)(2,1)S(1)}, bf16[256,256]{1,0:T(8,128)(2,1)S(1)}, u32[]{:S(2)}, u32[]{:S(2)}) collective-permute-start(bf16[256,256]{1,0:T(8,128)(2,1)S(1)} %shard_map.90.pair_ref.refs_0_), channel_id=1, source_target_pairs={{0,2},{1,3},{2,0},{3,1},{4,6},{5,7},{6,4},{7,5},{8,10},{9,11},{10,... | collective-permute-start | bytes 393224 | tf_op jit(solution)/shard_map/ppermute | solution.py:30
  23.4 0.6 %collective-permute-start.9 = (bf16[256,256]{1,0:T(8,128)(2,1)S(1)}, bf16[256,256]{1,0:T(8,128)(2,1)S(1)}, u32[]{:S(2)}, u32[]{:S(2)}) collective-permute-start(bf16[256,256]{1,0:T(8,128)(2,1)S(1)} %shard_map.90.pair_ref.refs_0_), channel_id=1, source_target_pairs={{0,3},{1,2},{2,1},{3,0},{4,7},{5,6},{6,5},{7,4},{8,11},{9,10},{10,... | collective-permute-start | bytes 393224 | tf_op jit(solution)/shard_map/ppermute | solution.py:30
  24.0 0.3 collective-permute-start.10
  24.3 0.8 %shard_map.91 = bf16[128,256]{1,0:T(8,128)(2,1)} custom-call(bf16[256,256]{1,0:T(8,128)(2,1)S(1)} %shard_map.90.pair_ref.refs_0_, bf16[256,256]{1,0:T(8,128)(2,1)S(1)} %copy-done), custom_call_target="tpu_custom_call" | custom-call | flops 16777216 | bytes 262144 | tf_op jit(solution)/shard_map/pallas_call | solution.py:217
  25.1 7.2 %collective-permute-done.8.refs_1_ = bf16[256,256]{1,0:T(8,128)(2,1)S(1)} collective-permute-done((bf16[256,256]{1,0:T(8,128)(2,1)S(1)}, bf16[256,256]{1,0:T(8,128)(2,1)S(1)}, u32[]{:S(2)}, u32[]{:S(2)}) %collective-permute-start.8) | collective-permute-done | bytes 131104 | tf_op jit(solution)/shard_map/ppermute | solution.py:30
  32.3 0.0 collective-permute-done.9.refs_2_
  32.3 0.7 %collective-permute-done.10.refs_3_ = bf16[256,256]{1,0:T(8,128)(2,1)S(1)} collective-permute-done((bf16[256,256]{1,0:T(8,128)(2,1)S(1)}, bf16[256,256]{1,0:T(8,128)(2,1)S(1)}, u32[]{:S(2)}, u32[]{:S(2)}) %collective-permute-start.10) | collective-permute-done | bytes 131104 | tf_op jit(solution)/shard_map/ppermute | solution.py:30
  33.0 0.3 shard_map.93
  33.3 0.1 collective-permute-start.11
  33.4 0.4 shard_map.92
  33.8 0.9 %collective-permute-done.11.other_ref = bf16[256,256]{1,0:T(8,128)(2,1)S(1)} collective-permute-done((bf16[256,256]{1,0:T(8,128)(2,1)S(1)}, bf16[256,256]{1,0:T(8,128)(2,1)S(1)}, u32[]{:S(2)}, u32[]{:S(2)}) %collective-permute-start.11) | collective-permute-done | bytes 131104 | tf_op jit(solution)/shard_map/ppermute | solution.py:30
  34.7 0.1 collective-permute-start.13
  34.9 2.5 %collective-permute-start.12 = (bf16[256,256]{1,0:T(8,128)(2,1)S(1)}, bf16[256,256]{1,0:T(8,128)(2,1)S(1)}, u32[]{:S(2)}, u32[]{:S(2)}) collective-permute-start(bf16[256,256]{1,0:T(8,128)(2,1)S(1)} %get-tuple-element.54), channel_id=1, source_target_pairs={{0,24},{4,28},{8,16},{12,20},{16,8},{20,12},{24,0},{28,4},{1,25},{... | collective-permute-start | bytes 393224 | tf_op jit(solution)/shard_map/ppermute | solution.py:30
  37.4 0.0 collective-permute-done.13.other_ref
  37.5 0.3 collective-permute-start.14
  37.8 1.5 %collective-permute-start.15 = (bf16[256,256]{1,0:T(8,128)(2,1)S(1)}, bf16[256,256]{1,0:T(8,128)(2,1)S(1)}, u32[]{:S(2)}, u32[]{:S(2)}) collective-permute-start(bf16[256,256]{1,0:T(8,128)(2,1)S(1)} %get-tuple-element.57), channel_id=1, source_target_pairs={{0,16},{4,20},{8,24},{12,28},{16,0},{20,4},{24,8},{28,12},{1,17},{... | collective-permute-start | bytes 393224 | tf_op jit(solution)/shard_map/ppermute | solution.py:30
  39.3 2.9 %collective-permute-done.12.refs_0_ = bf16[256,256]{1,0:T(8,128)(2,1)S(1)} collective-permute-done((bf16[256,256]{1,0:T(8,128)(2,1)S(1)}, bf16[256,256]{1,0:T(8,128)(2,1)S(1)}, u32[]{:S(2)}, u32[]{:S(2)}) %collective-permute-start.12) | collective-permute-done | bytes 131104 | tf_op jit(solution)/shard_map/ppermute | solution.py:30
  42.2 1.9 %collective-permute-done.14.refs_1_ = bf16[256,256]{1,0:T(8,128)(2,1)S(1)} collective-permute-done((bf16[256,256]{1,0:T(8,128)(2,1)S(1)}, bf16[256,256]{1,0:T(8,128)(2,1)S(1)}, u32[]{:S(2)}, u32[]{:S(2)}) %collective-permute-start.14) | collective-permute-done | bytes 131104 | tf_op jit(solution)/shard_map/ppermute | solution.py:30
  44.1 0.3 collective-permute-done.15.refs_2_
  44.5 0.1 collective-permute-start.16
  44.6 0.8 %shard_map.97 = bf16[128,256]{1,0:T(8,128)(2,1)} custom-call(bf16[256,256]{1,0:T(8,128)(2,1)S(1)} %copy-done, f32[128,256]{1,0:T(8,128)S(1)} %get-tuple-element.58.own_ref, bf16[256,256]{1,0:T(8,128)(2,1)S(1)} %collective-permute-done.12.refs_0_, bf16[256,256]{1,0:T(8,128)(2,1)S(1)} %collective-permute-done.14.refs_1_, ...), custom_call_target="tpu_custom_call" | custom-call | flops 16777216 | bytes 393216 | tf_op jit(solution)/shard_map/pallas_call | solution.py:302
  45.4 0.4 collective-permute-done.16
  45.8 0.7 %fusion = f32[256,256]{1,0:T(8,128)} fusion(bf16[128,256]{1,0:T(8,128)(2,1)S(1)} %collective-permute-done.16, bf16[128,256]{1,0:T(8,128)(2,1)S(1)} %shard_map.96, pred[]{:T(512)S(6)} %eq.5), kind=kLoop, calls=%fused_computation.1 | loop fusion | flops 655360 | bytes 393217 | tf_op jit(solution)/shard_map/convert_element_type | solution.py:352
  (5 shorter events, 0.2 us)
Async XLA Ops:
  0.6 5.7 %copy-start.5 = (s32[1,8,1,2]{1,3,2,0:T(2,128)S(1)}, s32[1,8,1,2]{1,3,2,0:T(2,128)}, u32[]{:S(2)}) copy-start(s32[1,8,1,2]{1,3,2,0:T(2,128)} %param.9) | copy-start | bytes 196
  0.6 8.3 %collective-permute-start = (bf16[128,256]{1,0:T(8,128)(2,1)}, bf16[128,256]{1,0:T(8,128)(2,1)S(1)}, u32[]{:S(2)}, u32[]{:S(2)}) collective-permute-start(bf16[128,256]{1,0:T(8,128)(2,1)} %refs_0_.1), channel_id=1, source_target_pairs={{0,2},{1,3},{2,0},{3,1},{4,6},{5,7},{6,4},{7,5},{8,10},{9,11},{10,... | collective-permute-start | bytes 196616 | tf_op jit(solution)/shard_map/ppermute | solution.py:30
  4.7 6.4 %collective-permute-start.1 = (bf16[128,256]{1,0:T(8,128)(2,1)}, bf16[128,256]{1,0:T(8,128)(2,1)S(1)}, u32[]{:S(2)}, u32[]{:S(2)}) collective-permute-start(bf16[128,256]{1,0:T(8,128)(2,1)} %refs_0_.1), channel_id=1, source_target_pairs={{0,3},{1,2},{2,1},{3,0},{4,7},{5,6},{6,5},{7,4},{8,11},{9,10},{10,... | collective-permute-start | bytes 196616 | tf_op jit(solution)/shard_map/ppermute | solution.py:30
  6.1 5.2 %collective-permute-start.2 = (bf16[128,256]{1,0:T(8,128)(2,1)}, bf16[128,256]{1,0:T(8,128)(2,1)S(1)}, u32[]{:S(2)}, u32[]{:S(2)}) collective-permute-start(bf16[128,256]{1,0:T(8,128)(2,1)} %refs_0_.1), channel_id=1, source_target_pairs={{0,1},{1,0},{2,3},{3,2},{4,5},{5,4},{6,7},{7,6},{8,9},{9,8},{10,11... | collective-permute-start | bytes 196616 | tf_op jit(solution)/shard_map/ppermute | solution.py:30
  6.4 0.7 %copy-start.4 = (s32[1,8,1]{1,2,0:T(1,128)S(1)}, s32[1,8,1]{1,2,0:T(1,128)}, u32[]{:S(2)}) copy-start(s32[1,8,1]{1,2,0:T(1,128)} %param.10) | copy-start | bytes 100
  7.1 1.0 %copy-start.1 = (bf16[1,8,1,128,256]{4,3,2,1,0:T(8,128)(2,1)S(1)}, bf16[1,8,1,128,256]{4,3,2,1,0:T(8,128)(2,1)}, u32[]{:S(2)}) copy-start(bf16[1,8,1,128,256]{4,3,2,1,0:T(8,128)(2,1)} %param.11) | copy-start | bytes 1572868
  8.1 3.2 %copy-start.2 = (bf16[128,256]{1,0:T(8,128)(2,1)S(1)}, bf16[128,256]{1,0:T(8,128)(2,1)}, u32[]{:S(2)}) copy-start(bf16[128,256]{1,0:T(8,128)(2,1)} %refs_0_.1) | copy-start | bytes 196612
  11.5 1.3 %collective-permute-start.3 = (bf16[128,256]{1,0:T(8,128)(2,1)S(1)}, bf16[128,256]{1,0:T(8,128)(2,1)S(1)}, u32[]{:S(2)}, u32[]{:S(2)}) collective-permute-start(bf16[128,256]{1,0:T(8,128)(2,1)S(1)} %shard_map.87), channel_id=1, source_target_pairs={{0,4},{4,0},{8,12},{12,8},{16,20},{20,16},{24,28},{28,24},{1,5},{5... | collective-permute-start | bytes 196616 | tf_op jit(solution)/shard_map/ppermute | solution.py:30
  12.8 2.7 %collective-permute-start.4 = (bf16[384,256]{1,0:T(8,128)(2,1)S(1)}, bf16[384,256]{1,0:T(8,128)(2,1)S(1)}, u32[]{:S(2)}, u32[]{:S(2)}) collective-permute-start(bf16[384,256]{1,0:T(8,128)(2,1)S(1)} %get-tuple-element.38), channel_id=1, source_target_pairs={{0,4},{4,0},{8,12},{12,8},{16,20},{20,16},{24,28},{28,24},{1,5},{5... | collective-permute-start | bytes 589832 | tf_op jit(solution)/shard_map/ppermute | solution.py:30
  13.0 7.5 %copy-start = (bf16[256,256]{1,0:T(8,128)(2,1)S(1)}, bf16[256,256]{1,0:T(8,128)(2,1)}, u32[]{:S(2)}) copy-start(bf16[256,256]{1,0:T(8,128)(2,1)} %weight_ref.3) | copy-start | bytes 393220
  13.0 7.4 %copy-start.3 = (bf16[128,256]{1,0:T(8,128)(2,1)S(1)}, bf16[128,256]{1,0:T(8,128)(2,1)}, u32[]{:S(2)}) copy-start(bf16[128,256]{1,0:T(8,128)(2,1)} %refs_5_.1) | copy-start | bytes 196612
  13.0 5.4 %collective-permute-start.5 = (bf16[128,256]{1,0:T(8,128)(2,1)S(1)}, bf16[128,256]{1,0:T(8,128)(2,1)S(1)}, u32[]{:S(2)}, u32[]{:S(2)}) collective-permute-start(bf16[128,256]{1,0:T(8,128)(2,1)S(1)} %shard_map.89), channel_id=1, source_target_pairs={{0,24},{4,28},{8,16},{12,20},{16,8},{20,12},{24,0},{28,4},{1,25},{... | collective-permute-start | bytes 196616 | tf_op jit(solution)/shard_map/ppermute | solution.py:30
  15.5 4.3 %collective-permute-start.6 = (bf16[128,256]{1,0:T(8,128)(2,1)S(1)}, bf16[128,256]{1,0:T(8,128)(2,1)S(1)}, u32[]{:S(2)}, u32[]{:S(2)}) collective-permute-start(bf16[128,256]{1,0:T(8,128)(2,1)S(1)} %get-tuple-element.41), channel_id=1, source_target_pairs={{0,8},{4,12},{8,0},{12,4},{16,24},{20,28},{24,16},{28,20},{1,9},{5... | collective-permute-start | bytes 196616 | tf_op jit(solution)/shard_map/ppermute | solution.py:30
  16.1 4.3 %collective-permute-start.7 = (bf16[128,256]{1,0:T(8,128)(2,1)S(1)}, bf16[128,256]{1,0:T(8,128)(2,1)S(1)}, u32[]{:S(2)}, u32[]{:S(2)}) collective-permute-start(bf16[128,256]{1,0:T(8,128)(2,1)S(1)} %get-tuple-element.42), channel_id=1, source_target_pairs={{0,16},{4,20},{8,24},{12,28},{16,0},{20,4},{24,8},{28,12},{1,17},{... | collective-permute-start | bytes 196616 | tf_op jit(solution)/shard_map/ppermute | solution.py:30
  20.6 11.6 %collective-permute-start.8 = (bf16[256,256]{1,0:T(8,128)(2,1)S(1)}, bf16[256,256]{1,0:T(8,128)(2,1)S(1)}, u32[]{:S(2)}, u32[]{:S(2)}) collective-permute-start(bf16[256,256]{1,0:T(8,128)(2,1)S(1)} %shard_map.90.pair_ref.refs_0_), channel_id=1, source_target_pairs={{0,2},{1,3},{2,0},{3,1},{4,6},{5,7},{6,4},{7,5},{8,10},{9,11},{10,... | collective-permute-start | bytes 393224 | tf_op jit(solution)/shard_map/ppermute | solution.py:30
  23.4 8.9 %collective-permute-start.9 = (bf16[256,256]{1,0:T(8,128)(2,1)S(1)}, bf16[256,256]{1,0:T(8,128)(2,1)S(1)}, u32[]{:S(2)}, u32[]{:S(2)}) collective-permute-start(bf16[256,256]{1,0:T(8,128)(2,1)S(1)} %shard_map.90.pair_ref.refs_0_), channel_id=1, source_target_pairs={{0,3},{1,2},{2,1},{3,0},{4,7},{5,6},{6,5},{7,4},{8,11},{9,10},{10,... | collective-permute-start | bytes 393224 | tf_op jit(solution)/shard_map/ppermute | solution.py:30
  24.0 9.0 %collective-permute-start.10 = (bf16[256,256]{1,0:T(8,128)(2,1)S(1)}, bf16[256,256]{1,0:T(8,128)(2,1)S(1)}, u32[]{:S(2)}, u32[]{:S(2)}) collective-permute-start(bf16[256,256]{1,0:T(8,128)(2,1)S(1)} %shard_map.90.pair_ref.refs_0_), channel_id=1, source_target_pairs={{0,1},{1,0},{2,3},{3,2},{4,5},{5,4},{6,7},{7,6},{8,9},{9,8},{10,11... | collective-permute-start | bytes 393224 | tf_op jit(solution)/shard_map/ppermute | solution.py:30
  33.3 1.4 %collective-permute-start.11 = (bf16[256,256]{1,0:T(8,128)(2,1)S(1)}, bf16[256,256]{1,0:T(8,128)(2,1)S(1)}, u32[]{:S(2)}, u32[]{:S(2)}) collective-permute-start(bf16[256,256]{1,0:T(8,128)(2,1)S(1)} %get-tuple-element.50), channel_id=1, source_target_pairs={{0,4},{4,0},{8,12},{12,8},{16,20},{20,16},{24,28},{28,24},{1,5},{5... | collective-permute-start | bytes 393224 | tf_op jit(solution)/shard_map/ppermute | solution.py:30
  34.7 2.7 %collective-permute-start.13 = (bf16[384,256]{1,0:T(8,128)(2,1)S(1)}, bf16[384,256]{1,0:T(8,128)(2,1)S(1)}, u32[]{:S(2)}, u32[]{:S(2)}) collective-permute-start(bf16[384,256]{1,0:T(8,128)(2,1)S(1)} %get-tuple-element.55), channel_id=1, source_target_pairs={{0,4},{4,0},{8,12},{12,8},{16,20},{20,16},{24,28},{28,24},{1,5},{5... | collective-permute-start | bytes 589832 | tf_op jit(solution)/shard_map/ppermute | solution.py:30
  34.9 7.3 %collective-permute-start.12 = (bf16[256,256]{1,0:T(8,128)(2,1)S(1)}, bf16[256,256]{1,0:T(8,128)(2,1)S(1)}, u32[]{:S(2)}, u32[]{:S(2)}) collective-permute-start(bf16[256,256]{1,0:T(8,128)(2,1)S(1)} %get-tuple-element.54), channel_id=1, source_target_pairs={{0,24},{4,28},{8,16},{12,20},{16,8},{20,12},{24,0},{28,4},{1,25},{... | collective-permute-start | bytes 393224 | tf_op jit(solution)/shard_map/ppermute | solution.py:30
  37.5 6.6 %collective-permute-start.14 = (bf16[256,256]{1,0:T(8,128)(2,1)S(1)}, bf16[256,256]{1,0:T(8,128)(2,1)S(1)}, u32[]{:S(2)}, u32[]{:S(2)}) collective-permute-start(bf16[256,256]{1,0:T(8,128)(2,1)S(1)} %get-tuple-element.56), channel_id=1, source_target_pairs={{0,8},{4,12},{8,0},{12,4},{16,24},{20,28},{24,16},{28,20},{1,9},{5... | collective-permute-start | bytes 393224 | tf_op jit(solution)/shard_map/ppermute | solution.py:30
  37.8 6.6 %collective-permute-start.15 = (bf16[256,256]{1,0:T(8,128)(2,1)S(1)}, bf16[256,256]{1,0:T(8,128)(2,1)S(1)}, u32[]{:S(2)}, u32[]{:S(2)}) collective-permute-start(bf16[256,256]{1,0:T(8,128)(2,1)S(1)} %get-tuple-element.57), channel_id=1, source_target_pairs={{0,16},{4,20},{8,24},{12,28},{16,0},{20,4},{24,8},{28,12},{1,17},{... | collective-permute-start | bytes 393224 | tf_op jit(solution)/shard_map/ppermute | solution.py:30
  44.5 1.3 %collective-permute-start.16 = (bf16[128,256]{1,0:T(8,128)(2,1)S(1)}, bf16[128,256]{1,0:T(8,128)(2,1)S(1)}, u32[]{:S(2)}, u32[]{:S(2)}) collective-permute-start(bf16[128,256]{1,0:T(8,128)(2,1)S(1)} %shard_map.96), channel_id=1, source_target_pairs={{0,4},{4,0},{8,12},{12,8},{16,20},{20,16},{24,28},{28,24},{1,5},{5... | collective-permute-start | bytes 196616 | tf_op jit(solution)/shard_map/ppermute | solution.py:30

commit v5 on v4

--- a/solution.py
+++ b/solution.py
@@ -41,7 +41,7 @@
 
 
 def sub_order(subs):
-    return [2, 3, 1] if subs == 4 else [1]
+    return [2, 1, 3] if subs == 4 else [1]
 
 
 def dense_kernel(steps, subs, rows_ref, counts_ref, tiles_ref, out_ref):
@@ -75,18 +75,18 @@
     )(rows, counts, tiles)
 
 
-def first_kernel(n_pieces, dense_ref, *refs):
-    nodes = jnp.concatenate([piece[...] for piece in refs[:n_pieces]], axis=0)
+def first_kernel(order, dense_ref, *refs):
+    nodes = jnp.concatenate([refs[k][...] for k in order], axis=0)
     out_ref = refs[-1]
     half = dense_ref.shape[0] // 2
     rows = dense_ref[half : half + out_ref.shape[0], :]
     out_ref[...] = jnp.dot(rows, nodes, preferred_element_type=F32).astype(out_ref.dtype)
 
 
-def apply_first(dense, pieces):
+def apply_first(dense, pieces, order):
     shape = pieces[0].shape
     return pl.pallas_call(
-        functools.partial(first_kernel, len(pieces)),
+        functools.partial(first_kernel, order),
         out_shape=jax.ShapeDtypeStruct(shape, BF16),
         in_specs=[vmem()] * (1 + len(pieces)),
         out_specs=vmem(),
@@ -97,19 +97,19 @@
     )(dense, *pieces)
 
 
-def rest_kernel(block, n_pieces, dense_ref, *refs):
-    nodes = jnp.concatenate([piece[-block:, :] for piece in refs[:n_pieces]], axis=0)
-    odd_ref, even_ref = refs[n_pieces:]
+def rest_kernel(block, order, dense_ref, *refs):
+    nodes = jnp.concatenate([refs[k][-block:, :] for k in order], axis=0)
+    odd_ref, even_ref = refs[len(order) :]
     half = dense_ref.shape[0] // 2
     rows = dense_ref[dense_ref.shape[0] - odd_ref.shape[0] :, :]
     odd_ref[...] = jnp.dot(rows, nodes, preferred_element_type=F32).astype(odd_ref.dtype)
     even_ref[...] = jnp.dot(dense_ref[:half, :], nodes, preferred_element_type=F32)
 
 
-def apply_rest(dense, pieces, block):
+def apply_rest(dense, pieces, order, block):
     rows, feat = dense.shape[0] // 2, pieces[0].shape[1]
     return pl.pallas_call(
-        functools.partial(rest_kernel, block, len(pieces)),
+        functools.partial(rest_kernel, block, order),
         out_shape=[jax.ShapeDtypeStruct((rows - block, feat), BF16), jax.ShapeDtypeStruct((rows, feat), F32)],
         in_specs=[vmem()] * (1 + len(pieces)),
         out_specs=[vmem()] * 2,
@@ -324,15 +324,17 @@
 def shards_direct(features, weight, cotangent, rows, counts, tiles):
     block = features.shape[0]
     slabs, subs = lax.axis_size("blk"), lax.axis_size("rep")
-    far, near = far_steps(slabs), sub_order(subs)
+    far, near, early = far_steps(slabs), sub_order(subs), [3, 2, 1] if subs == 4 else [1]
+    straight = list(range(subs))
+    order = [([0] + early).index(d) for d in [0] + near]
     node_count = block * slabs * subs
     even = far[:1] + [at(0)] + far[1:]
     odd = [lambda i, step=step: step(i) ^ 1 for step in even]
     dense = dense_adjacency(even + odd, [0] + near, rows, counts, tiles)
 
-    pieces, dense = lax.optimization_barrier((gather(features, near), dense))
-    other = send(apply_first(dense, pieces), "blk", at(1))
-    rest, mine = apply_rest(dense, pieces, block)
+    pieces, dense = lax.optimization_barrier((gather(features, early), dense))
+    other = send(apply_first(dense, pieces, order), "blk", at(1))
+    rest, mine = apply_rest(dense, pieces, order, block)
     rest, other = lax.optimization_barrier((rest, other))
     (first,) = first_sum(mine, other, block)
     own, *sums = rest_sums(mine, send(rest, "blk", at(1)), block)
@@ -344,7 +346,7 @@
     pairs, activation = lax.optimization_barrier((pairs, activation))
     first, keep = apply_pairs(dense, pairs, [0] + near, 1.0 / math.sqrt(node_count))
     other = send(first, "blk", at(1))
-    rest, mine = apply_rest(dense, pairs, block)
+    rest, mine = apply_rest(dense, pairs, straight, block)
     rest, other = lax.optimization_barrier((rest, other))
     first, half = first_sum(mine, other, block, keep)
     own, *sums = rest_sums(mine, send(rest, "blk", at(1)), block, half)

time: 46.7 us -> 46.3 us (level)
  waiting for transfers between devices: 20.6 us -> 19.3 us
  starting transfers between devices: 18.5 us -> 19.3 us
    ppermute x17, waiting for transfers between devices: 20.6 us -> 19.3 us  [send(): lax.ppermute(value, axis, [(i, step(i)) for i in range(lax.axis_size(axis...]
    ppermute x17, starting transfers between devices: 18.5 us -> 19.3 us  [send(): lax.ppermute(value, axis, [(i, step(i)) for i in range(lax.axis_size(axis...]
  transfers between devices with their start and end apart: 17 -> 17, of which waited for: 13 -> 12; matrix products, arithmetic and copies ran while one was open for 0% -> 0% of each run, Pallas kernels for 7% -> 7%
where the time goes in v5:
time: 46.3 us; the launch traced here: 46.1 us
  starting transfers between devices  19.3 us (42%)
  waiting for transfers between devices  19.3 us (42%)
  Pallas kernels  4.15 us (9%)
  local copies, waits for them, and re-layouts  1.8 us (4%)
  between operations  0.77 us (2%)
  other arithmetic  0.73 us (2%)
    ppermute x17, waiting for transfers between devices, send(): lax.ppermute(value, axis, [(i, step(i)) for i in range(lax.axis_size(axis...  19.3 us
    ppermute x17, starting transfers between devices, send(): lax.ppermute(value, axis, [(i, step(i)) for i in range(lax.axis_size(axis...  19.3 us
    unnamed x12, local copies, waits for them, and re-layouts  1.72 us
  transfers between devices with their start and end apart: 17, of which 12 were waited for; matrix products, arithmetic and copies ran while one was open for 0% of the time, Pallas kernels for 7%

profile of v5, /device:TPU:0, one launch (start us, length us, event | category | flops | bytes accessed | tf_op | source)
XLA Modules:
  0.0 46.1 jit_solution(1782899248968988535)
XLA Ops:
  0.6 0.0 copy-start.5
  0.6 5.1 %collective-permute-start = (bf16[128,256]{1,0:T(8,128)(2,1)}, bf16[128,256]{1,0:T(8,128)(2,1)S(1)}, u32[]{:S(2)}, u32[]{:S(2)}) collective-permute-start(bf16[128,256]{1,0:T(8,128)(2,1)} %refs_0_.1), channel_id=1, source_target_pairs={{0,3},{1,2},{2,1},{3,0},{4,7},{5,6},{6,5},{7,4},{8,11},{9,10},{10,... | collective-permute-start | bytes 196616 | tf_op jit(solution)/shard_map/ppermute | solution.py:30
  5.8 0.0 collective-permute-start.1
  5.8 0.6 %collective-permute-start.2 = (bf16[128,256]{1,0:T(8,128)(2,1)}, bf16[128,256]{1,0:T(8,128)(2,1)S(1)}, u32[]{:S(2)}, u32[]{:S(2)}) collective-permute-start(bf16[128,256]{1,0:T(8,128)(2,1)} %refs_0_.1), channel_id=1, source_target_pairs={{0,1},{1,0},{2,3},{3,2},{4,5},{5,4},{6,7},{7,6},{8,9},{9,8},{10,11... | collective-permute-start | bytes 196616 | tf_op jit(solution)/shard_map/ppermute | solution.py:30
  6.4 0.0 copy-done.5
  6.4 0.1 copy.9.rows_ref
  6.5 0.0 copy-start.4
  6.5 0.7 %copy-done.4 = s32[1,8,1]{1,2,0:T(1,128)S(1)} copy-done((s32[1,8,1]{1,2,0:T(1,128)S(1)}, s32[1,8,1]{1,2,0:T(1,128)}, u32[]{:S(2)}) %copy-start.4) | copy-done | bytes 56
  7.1 0.0 copy-start.1
  7.1 1.0 %copy-done.1 = bf16[1,8,1,128,256]{4,3,2,1,0:T(8,128)(2,1)S(1)} copy-done((bf16[1,8,1,128,256]{4,3,2,1,0:T(8,128)(2,1)S(1)}, bf16[1,8,1,128,256]{4,3,2,1,0:T(8,128)(2,1)}, u32[]{:S(2)}) %copy-start.1) | copy-done | bytes 524312
  8.2 0.0 copy-start.2
  8.2 0.8 %shard_map.85.dense_ref = bf16[1024,512]{1,0:T(8,128)(2,1)S(1)} custom-call(s32[8,2]{1,0:T(8,128)S(1)} %copy.9.rows_ref, s32[8]{0:T(128)S(1)} %bitcast.4, bf16[8,128,256]{2,1,0:T(8,128)(2,1)S(1)} %bitcast.3), custom_call_target="tpu_custom_call" | custom-call | bytes 2097152 | tf_op jit(solution)/shard_map/pallas_call | solution.py:68
  9.0 0.0 collective-permute-done.refs_1_
  9.0 2.5 %collective-permute-done.1.refs_2_ = bf16[128,256]{1,0:T(8,128)(2,1)S(1)} collective-permute-done((bf16[128,256]{1,0:T(8,128)(2,1)}, bf16[128,256]{1,0:T(8,128)(2,1)S(1)}, u32[]{:S(2)}, u32[]{:S(2)}) %collective-permute-start.1) | collective-permute-done | bytes 65568 | tf_op jit(solution)/shard_map/ppermute | solution.py:30
  11.6 0.0 collective-permute-done.2.refs_3_
  11.6 0.0 copy-done.2
  11.6 0.2 shard_map.87
  11.8 0.1 collective-permute-start.3
  11.9 0.4 shard_map.86
  12.3 0.8 %collective-permute-done.3.other_ref = bf16[128,256]{1,0:T(8,128)(2,1)S(1)} collective-permute-done((bf16[128,256]{1,0:T(8,128)(2,1)S(1)}, bf16[128,256]{1,0:T(8,128)(2,1)S(1)}, u32[]{:S(2)}, u32[]{:S(2)}) %collective-permute-start.3) | collective-permute-done | bytes 65568 | tf_op jit(solution)/shard_map/ppermute | solution.py:30
  13.1 0.2 collective-permute-start.4
  13.3 0.0 copy-start
  13.3 0.0 copy-start.3
  13.3 2.5 %collective-permute-start.5 = (bf16[128,256]{1,0:T(8,128)(2,1)S(1)}, bf16[128,256]{1,0:T(8,128)(2,1)S(1)}, u32[]{:S(2)}, u32[]{:S(2)}) collective-permute-start(bf16[128,256]{1,0:T(8,128)(2,1)S(1)} %shard_map.89), channel_id=1, source_target_pairs={{0,24},{4,28},{8,16},{12,20},{16,8},{20,12},{24,0},{28,4},{1,25},{... | collective-permute-start | bytes 196616 | tf_op jit(solution)/shard_map/ppermute | solution.py:30
  15.8 0.0 collective-permute-done.4.other_ref
  15.8 0.6 %collective-permute-start.6 = (bf16[128,256]{1,0:T(8,128)(2,1)S(1)}, bf16[128,256]{1,0:T(8,128)(2,1)S(1)}, u32[]{:S(2)}, u32[]{:S(2)}) collective-permute-start(bf16[128,256]{1,0:T(8,128)(2,1)S(1)} %get-tuple-element.41), channel_id=1, source_target_pairs={{0,8},{4,12},{8,0},{12,4},{16,24},{20,28},{24,16},{28,20},{1,9},{5... | collective-permute-start | bytes 196616 | tf_op jit(solution)/shard_map/ppermute | solution.py:30
  16.5 1.2 %collective-permute-start.7 = (bf16[128,256]{1,0:T(8,128)(2,1)S(1)}, bf16[128,256]{1,0:T(8,128)(2,1)S(1)}, u32[]{:S(2)}, u32[]{:S(2)}) collective-permute-start(bf16[128,256]{1,0:T(8,128)(2,1)S(1)} %get-tuple-element.42), channel_id=1, source_target_pairs={{0,16},{4,20},{8,24},{12,28},{16,0},{20,4},{24,8},{28,12},{1,17},{... | collective-permute-start | bytes 196616 | tf_op jit(solution)/shard_map/ppermute | solution.py:30
  17.7 1.1 %collective-permute-done.5.refs_1_ = bf16[128,256]{1,0:T(8,128)(2,1)S(1)} collective-permute-done((bf16[128,256]{1,0:T(8,128)(2,1)S(1)}, bf16[128,256]{1,0:T(8,128)(2,1)S(1)}, u32[]{:S(2)}, u32[]{:S(2)}) %collective-permute-start.5) | collective-permute-done | bytes 65568 | tf_op jit(solution)/shard_map/ppermute | solution.py:30
  18.7 1.4 %collective-permute-done.6.refs_2_ = bf16[128,256]{1,0:T(8,128)(2,1)S(1)} collective-permute-done((bf16[128,256]{1,0:T(8,128)(2,1)S(1)}, bf16[128,256]{1,0:T(8,128)(2,1)S(1)}, u32[]{:S(2)}, u32[]{:S(2)}) %collective-permute-start.6) | collective-permute-done | bytes 65568 | tf_op jit(solution)/shard_map/ppermute | solution.py:30
  20.2 0.5 %collective-permute-done.7.refs_3_ = bf16[128,256]{1,0:T(8,128)(2,1)S(1)} collective-permute-done((bf16[128,256]{1,0:T(8,128)(2,1)S(1)}, bf16[128,256]{1,0:T(8,128)(2,1)S(1)}, u32[]{:S(2)}, u32[]{:S(2)}) %collective-permute-start.7) | collective-permute-done | bytes 65568 | tf_op jit(solution)/shard_map/ppermute | solution.py:30
  20.7 0.0 copy-done
  20.7 0.0 copy-done.3
  20.7 0.2 shard_map.90.pair_ref.refs_0_
  20.9 1.6 %collective-permute-start.8 = (bf16[256,256]{1,0:T(8,128)(2,1)S(1)}, bf16[256,256]{1,0:T(8,128)(2,1)S(1)}, u32[]{:S(2)}, u32[]{:S(2)}) collective-permute-start(bf16[256,256]{1,0:T(8,128)(2,1)S(1)} %shard_map.90.pair_ref.refs_0_), channel_id=1, source_target_pairs={{0,2},{1,3},{2,0},{3,1},{4,6},{5,7},{6,4},{7,5},{8,10},{9,11},{10,... | collective-permute-start | bytes 393224 | tf_op jit(solution)/shard_map/ppermute | solution.py:30
  22.6 1.7 %collective-permute-start.9 = (bf16[256,256]{1,0:T(8,128)(2,1)S(1)}, bf16[256,256]{1,0:T(8,128)(2,1)S(1)}, u32[]{:S(2)}, u32[]{:S(2)}) collective-permute-start(bf16[256,256]{1,0:T(8,128)(2,1)S(1)} %shard_map.90.pair_ref.refs_0_), channel_id=1, source_target_pairs={{0,1},{1,0},{2,3},{3,2},{4,5},{5,4},{6,7},{7,6},{8,9},{9,8},{10,11... | collective-permute-start | bytes 393224 | tf_op jit(solution)/shard_map/ppermute | solution.py:30
  24.3 1.1 %collective-permute-start.10 = (bf16[256,256]{1,0:T(8,128)(2,1)S(1)}, bf16[256,256]{1,0:T(8,128)(2,1)S(1)}, u32[]{:S(2)}, u32[]{:S(2)}) collective-permute-start(bf16[256,256]{1,0:T(8,128)(2,1)S(1)} %shard_map.90.pair_ref.refs_0_), channel_id=1, source_target_pairs={{0,3},{1,2},{2,1},{3,0},{4,7},{5,6},{6,5},{7,4},{8,11},{9,10},{10,... | collective-permute-start | bytes 393224 | tf_op jit(solution)/shard_map/ppermute | solution.py:30
  25.4 0.8 %shard_map.91 = bf16[128,256]{1,0:T(8,128)(2,1)} custom-call(bf16[256,256]{1,0:T(8,128)(2,1)S(1)} %shard_map.90.pair_ref.refs_0_, bf16[256,256]{1,0:T(8,128)(2,1)S(1)} %copy-done), custom_call_target="tpu_custom_call" | custom-call | flops 16777216 | bytes 262144 | tf_op jit(solution)/shard_map/pallas_call | solution.py:217
  26.2 4.9 %collective-permute-done.8.refs_1_ = bf16[256,256]{1,0:T(8,128)(2,1)S(1)} collective-permute-done((bf16[256,256]{1,0:T(8,128)(2,1)S(1)}, bf16[256,256]{1,0:T(8,128)(2,1)S(1)}, u32[]{:S(2)}, u32[]{:S(2)}) %collective-permute-start.8) | collective-permute-done | bytes 131104 | tf_op jit(solution)/shard_map/ppermute | solution.py:30
  31.2 0.0 collective-permute-done.9.refs_2_
  31.2 1.4 %collective-permute-done.10.refs_3_ = bf16[256,256]{1,0:T(8,128)(2,1)S(1)} collective-permute-done((bf16[256,256]{1,0:T(8,128)(2,1)S(1)}, bf16[256,256]{1,0:T(8,128)(2,1)S(1)}, u32[]{:S(2)}, u32[]{:S(2)}) %collective-permute-start.10) | collective-permute-done | bytes 131104 | tf_op jit(solution)/shard_map/ppermute | solution.py:30
  32.6 0.3 shard_map.93
  32.9 0.1 collective-permute-start.11
  33.0 0.4 shard_map.92
  33.4 0.9 %collective-permute-done.11.other_ref = bf16[256,256]{1,0:T(8,128)(2,1)S(1)} collective-permute-done((bf16[256,256]{1,0:T(8,128)(2,1)S(1)}, bf16[256,256]{1,0:T(8,128)(2,1)S(1)}, u32[]{:S(2)}, u32[]{:S(2)}) %collective-permute-start.11) | collective-permute-done | bytes 131104 | tf_op jit(solution)/shard_map/ppermute | solution.py:30
  34.3 0.1 collective-permute-start.13
  34.5 2.5 %collective-permute-start.12 = (bf16[256,256]{1,0:T(8,128)(2,1)S(1)}, bf16[256,256]{1,0:T(8,128)(2,1)S(1)}, u32[]{:S(2)}, u32[]{:S(2)}) collective-permute-start(bf16[256,256]{1,0:T(8,128)(2,1)S(1)} %get-tuple-element.54), channel_id=1, source_target_pairs={{0,24},{4,28},{8,16},{12,20},{16,8},{20,12},{24,0},{28,4},{1,25},{... | collective-permute-start | bytes 393224 | tf_op jit(solution)/shard_map/ppermute | solution.py:30
  36.9 0.0 collective-permute-done.13.other_ref
  37.0 0.4 collective-permute-start.14
  37.4 1.4 %collective-permute-start.15 = (bf16[256,256]{1,0:T(8,128)(2,1)S(1)}, bf16[256,256]{1,0:T(8,128)(2,1)S(1)}, u32[]{:S(2)}, u32[]{:S(2)}) collective-permute-start(bf16[256,256]{1,0:T(8,128)(2,1)S(1)} %get-tuple-element.57), channel_id=1, source_target_pairs={{0,16},{4,20},{8,24},{12,28},{16,0},{20,4},{24,8},{28,12},{1,17},{... | collective-permute-start | bytes 393224 | tf_op jit(solution)/shard_map/ppermute | solution.py:30
  38.8 3.0 %collective-permute-done.12.refs_0_ = bf16[256,256]{1,0:T(8,128)(2,1)S(1)} collective-permute-done((bf16[256,256]{1,0:T(8,128)(2,1)S(1)}, bf16[256,256]{1,0:T(8,128)(2,1)S(1)}, u32[]{:S(2)}, u32[]{:S(2)}) %collective-permute-start.12) | collective-permute-done | bytes 131104 | tf_op jit(solution)/shard_map/ppermute | solution.py:30
  41.8 2.0 %collective-permute-done.14.refs_1_ = bf16[256,256]{1,0:T(8,128)(2,1)S(1)} collective-permute-done((bf16[256,256]{1,0:T(8,128)(2,1)S(1)}, bf16[256,256]{1,0:T(8,128)(2,1)S(1)}, u32[]{:S(2)}, u32[]{:S(2)}) %collective-permute-start.14) | collective-permute-done | bytes 131104 | tf_op jit(solution)/shard_map/ppermute | solution.py:30
  43.7 0.3 collective-permute-done.15.refs_2_
  44.1 0.1 collective-permute-start.16
  44.1 0.8 %shard_map.97 = bf16[128,256]{1,0:T(8,128)(2,1)} custom-call(bf16[256,256]{1,0:T(8,128)(2,1)S(1)} %copy-done, f32[128,256]{1,0:T(8,128)S(1)} %get-tuple-element.58.own_ref, bf16[256,256]{1,0:T(8,128)(2,1)S(1)} %collective-permute-done.12.refs_0_, bf16[256,256]{1,0:T(8,128)(2,1)S(1)} %collective-permute-done.14.refs_1_, ...), custom_call_target="tpu_custom_call" | custom-call | flops 16777216 | bytes 393216 | tf_op jit(solution)/shard_map/pallas_call | solution.py:302
  45.0 0.4 collective-permute-done.16
  45.4 0.7 %fusion = f32[256,256]{1,0:T(8,128)} fusion(bf16[128,256]{1,0:T(8,128)(2,1)S(1)} %collective-permute-done.16, bf16[128,256]{1,0:T(8,128)(2,1)S(1)} %shard_map.96, pred[]{:T(512)S(6)} %eq.5), kind=kLoop, calls=%fused_computation.1 | loop fusion | flops 655360 | bytes 393217 | tf_op jit(solution)/shard_map/convert_element_type | solution.py:354
  (5 shorter events, 0.2 us)
Async XLA Ops:
  0.6 5.8 %copy-start.5 = (s32[1,8,1,2]{1,3,2,0:T(2,128)S(1)}, s32[1,8,1,2]{1,3,2,0:T(2,128)}, u32[]{:S(2)}) copy-start(s32[1,8,1,2]{1,3,2,0:T(2,128)} %param.9) | copy-start | bytes 196
  0.6 8.4 %collective-permute-start = (bf16[128,256]{1,0:T(8,128)(2,1)}, bf16[128,256]{1,0:T(8,128)(2,1)S(1)}, u32[]{:S(2)}, u32[]{:S(2)}) collective-permute-start(bf16[128,256]{1,0:T(8,128)(2,1)} %refs_0_.1), channel_id=1, source_target_pairs={{0,3},{1,2},{2,1},{3,0},{4,7},{5,6},{6,5},{7,4},{8,11},{9,10},{10,... | collective-permute-start | bytes 196616 | tf_op jit(solution)/shard_map/ppermute | solution.py:30
  5.8 5.8 %collective-permute-start.1 = (bf16[128,256]{1,0:T(8,128)(2,1)}, bf16[128,256]{1,0:T(8,128)(2,1)S(1)}, u32[]{:S(2)}, u32[]{:S(2)}) collective-permute-start(bf16[128,256]{1,0:T(8,128)(2,1)} %refs_0_.1), channel_id=1, source_target_pairs={{0,2},{1,3},{2,0},{3,1},{4,6},{5,7},{6,4},{7,5},{8,10},{9,11},{10,... | collective-permute-start | bytes 196616 | tf_op jit(solution)/shard_map/ppermute | solution.py:30
  5.8 5.8 %collective-permute-start.2 = (bf16[128,256]{1,0:T(8,128)(2,1)}, bf16[128,256]{1,0:T(8,128)(2,1)S(1)}, u32[]{:S(2)}, u32[]{:S(2)}) collective-permute-start(bf16[128,256]{1,0:T(8,128)(2,1)} %refs_0_.1), channel_id=1, source_target_pairs={{0,1},{1,0},{2,3},{3,2},{4,5},{5,4},{6,7},{7,6},{8,9},{9,8},{10,11... | collective-permute-start | bytes 196616 | tf_op jit(solution)/shard_map/ppermute | solution.py:30
  6.5 0.7 %copy-start.4 = (s32[1,8,1]{1,2,0:T(1,128)S(1)}, s32[1,8,1]{1,2,0:T(1,128)}, u32[]{:S(2)}) copy-start(s32[1,8,1]{1,2,0:T(1,128)} %param.10) | copy-start | bytes 100
  7.1 1.0 %copy-start.1 = (bf16[1,8,1,128,256]{4,3,2,1,0:T(8,128)(2,1)S(1)}, bf16[1,8,1,128,256]{4,3,2,1,0:T(8,128)(2,1)}, u32[]{:S(2)}) copy-start(bf16[1,8,1,128,256]{4,3,2,1,0:T(8,128)(2,1)} %param.11) | copy-start | bytes 1572868
  8.2 3.4 %copy-start.2 = (bf16[128,256]{1,0:T(8,128)(2,1)S(1)}, bf16[128,256]{1,0:T(8,128)(2,1)}, u32[]{:S(2)}) copy-start(bf16[128,256]{1,0:T(8,128)(2,1)} %refs_0_.1) | copy-start | bytes 196612
  11.8 1.3 %collective-permute-start.3 = (bf16[128,256]{1,0:T(8,128)(2,1)S(1)}, bf16[128,256]{1,0:T(8,128)(2,1)S(1)}, u32[]{:S(2)}, u32[]{:S(2)}) collective-permute-start(bf16[128,256]{1,0:T(8,128)(2,1)S(1)} %shard_map.87), channel_id=1, source_target_pairs={{0,4},{4,0},{8,12},{12,8},{16,20},{20,16},{24,28},{28,24},{1,5},{5... | collective-permute-start | bytes 196616 | tf_op jit(solution)/shard_map/ppermute | solution.py:30
  13.1 2.7 %collective-permute-start.4 = (bf16[384,256]{1,0:T(8,128)(2,1)S(1)}, bf16[384,256]{1,0:T(8,128)(2,1)S(1)}, u32[]{:S(2)}, u32[]{:S(2)}) collective-permute-start(bf16[384,256]{1,0:T(8,128)(2,1)S(1)} %get-tuple-element.38), channel_id=1, source_target_pairs={{0,4},{4,0},{8,12},{12,8},{16,20},{20,16},{24,28},{28,24},{1,5},{5... | collective-permute-start | bytes 589832 | tf_op jit(solution)/shard_map/ppermute | solution.py:30
  13.3 7.4 %copy-start = (bf16[256,256]{1,0:T(8,128)(2,1)S(1)}, bf16[256,256]{1,0:T(8,128)(2,1)}, u32[]{:S(2)}) copy-start(bf16[256,256]{1,0:T(8,128)(2,1)} %weight_ref.3) | copy-start | bytes 393220
  13.3 7.4 %copy-start.3 = (bf16[128,256]{1,0:T(8,128)(2,1)S(1)}, bf16[128,256]{1,0:T(8,128)(2,1)}, u32[]{:S(2)}) copy-start(bf16[128,256]{1,0:T(8,128)(2,1)} %refs_5_.1) | copy-start | bytes 196612
  13.3 5.4 %collective-permute-start.5 = (bf16[128,256]{1,0:T(8,128)(2,1)S(1)}, bf16[128,256]{1,0:T(8,128)(2,1)S(1)}, u32[]{:S(2)}, u32[]{:S(2)}) collective-permute-start(bf16[128,256]{1,0:T(8,128)(2,1)S(1)} %shard_map.89), channel_id=1, source_target_pairs={{0,24},{4,28},{8,16},{12,20},{16,8},{20,12},{24,0},{28,4},{1,25},{... | collective-permute-start | bytes 196616 | tf_op jit(solution)/shard_map/ppermute | solution.py:30
  15.8 4.3 %collective-permute-start.6 = (bf16[128,256]{1,0:T(8,128)(2,1)S(1)}, bf16[128,256]{1,0:T(8,128)(2,1)S(1)}, u32[]{:S(2)}, u32[]{:S(2)}) collective-permute-start(bf16[128,256]{1,0:T(8,128)(2,1)S(1)} %get-tuple-element.41), channel_id=1, source_target_pairs={{0,8},{4,12},{8,0},{12,4},{16,24},{20,28},{24,16},{28,20},{1,9},{5... | collective-permute-start | bytes 196616 | tf_op jit(solution)/shard_map/ppermute | solution.py:30
  16.5 4.3 %collective-permute-start.7 = (bf16[128,256]{1,0:T(8,128)(2,1)S(1)}, bf16[128,256]{1,0:T(8,128)(2,1)S(1)}, u32[]{:S(2)}, u32[]{:S(2)}) collective-permute-start(bf16[128,256]{1,0:T(8,128)(2,1)S(1)} %get-tuple-element.42), channel_id=1, source_target_pairs={{0,16},{4,20},{8,24},{12,28},{16,0},{20,4},{24,8},{28,12},{1,17},{... | collective-permute-start | bytes 196616 | tf_op jit(solution)/shard_map/ppermute | solution.py:30
  20.9 10.2 %collective-permute-start.8 = (bf16[256,256]{1,0:T(8,128)(2,1)S(1)}, bf16[256,256]{1,0:T(8,128)(2,1)S(1)}, u32[]{:S(2)}, u32[]{:S(2)}) collective-permute-start(bf16[256,256]{1,0:T(8,128)(2,1)S(1)} %shard_map.90.pair_ref.refs_0_), channel_id=1, source_target_pairs={{0,2},{1,3},{2,0},{3,1},{4,6},{5,7},{6,4},{7,5},{8,10},{9,11},{10,... | collective-permute-start | bytes 393224 | tf_op jit(solution)/shard_map/ppermute | solution.py:30
  22.6 8.6 %collective-permute-start.9 = (bf16[256,256]{1,0:T(8,128)(2,1)S(1)}, bf16[256,256]{1,0:T(8,128)(2,1)S(1)}, u32[]{:S(2)}, u32[]{:S(2)}) collective-permute-start(bf16[256,256]{1,0:T(8,128)(2,1)S(1)} %shard_map.90.pair_ref.refs_0_), channel_id=1, source_target_pairs={{0,1},{1,0},{2,3},{3,2},{4,5},{5,4},{6,7},{7,6},{8,9},{9,8},{10,11... | collective-permute-start | bytes 393224 | tf_op jit(solution)/shard_map/ppermute | solution.py:30
  24.3 8.3 %collective-permute-start.10 = (bf16[256,256]{1,0:T(8,128)(2,1)S(1)}, bf16[256,256]{1,0:T(8,128)(2,1)S(1)}, u32[]{:S(2)}, u32[]{:S(2)}) collective-permute-start(bf16[256,256]{1,0:T(8,128)(2,1)S(1)} %shard_map.90.pair_ref.refs_0_), channel_id=1, source_target_pairs={{0,3},{1,2},{2,1},{3,0},{4,7},{5,6},{6,5},{7,4},{8,11},{9,10},{10,... | collective-permute-start | bytes 393224 | tf_op jit(solution)/shard_map/ppermute | solution.py:30
  32.9 1.4 %collective-permute-start.11 = (bf16[256,256]{1,0:T(8,128)(2,1)S(1)}, bf16[256,256]{1,0:T(8,128)(2,1)S(1)}, u32[]{:S(2)}, u32[]{:S(2)}) collective-permute-start(bf16[256,256]{1,0:T(8,128)(2,1)S(1)} %get-tuple-element.50), channel_id=1, source_target_pairs={{0,4},{4,0},{8,12},{12,8},{16,20},{20,16},{24,28},{28,24},{1,5},{5... | collective-permute-start | bytes 393224 | tf_op jit(solution)/shard_map/ppermute | solution.py:30
  34.3 2.6 %collective-permute-start.13 = (bf16[384,256]{1,0:T(8,128)(2,1)S(1)}, bf16[384,256]{1,0:T(8,128)(2,1)S(1)}, u32[]{:S(2)}, u32[]{:S(2)}) collective-permute-start(bf16[384,256]{1,0:T(8,128)(2,1)S(1)} %get-tuple-element.55), channel_id=1, source_target_pairs={{0,4},{4,0},{8,12},{12,8},{16,20},{20,16},{24,28},{28,24},{1,5},{5... | collective-permute-start | bytes 589832 | tf_op jit(solution)/shard_map/ppermute | solution.py:30
  34.5 7.3 %collective-permute-start.12 = (bf16[256,256]{1,0:T(8,128)(2,1)S(1)}, bf16[256,256]{1,0:T(8,128)(2,1)S(1)}, u32[]{:S(2)}, u32[]{:S(2)}) collective-permute-start(bf16[256,256]{1,0:T(8,128)(2,1)S(1)} %get-tuple-element.54), channel_id=1, source_target_pairs={{0,24},{4,28},{8,16},{12,20},{16,8},{20,12},{24,0},{28,4},{1,25},{... | collective-permute-start | bytes 393224 | tf_op jit(solution)/shard_map/ppermute | solution.py:30
  37.0 6.8 %collective-permute-start.14 = (bf16[256,256]{1,0:T(8,128)(2,1)S(1)}, bf16[256,256]{1,0:T(8,128)(2,1)S(1)}, u32[]{:S(2)}, u32[]{:S(2)}) collective-permute-start(bf16[256,256]{1,0:T(8,128)(2,1)S(1)} %get-tuple-element.56), channel_id=1, source_target_pairs={{0,8},{4,12},{8,0},{12,4},{16,24},{20,28},{24,16},{28,20},{1,9},{5... | collective-permute-start | bytes 393224 | tf_op jit(solution)/shard_map/ppermute | solution.py:30
  37.4 6.6 %collective-permute-start.15 = (bf16[256,256]{1,0:T(8,128)(2,1)S(1)}, bf16[256,256]{1,0:T(8,128)(2,1)S(1)}, u32[]{:S(2)}, u32[]{:S(2)}) collective-permute-start(bf16[256,256]{1,0:T(8,128)(2,1)S(1)} %get-tuple-element.57), channel_id=1, source_target_pairs={{0,16},{4,20},{8,24},{12,28},{16,0},{20,4},{24,8},{28,12},{1,17},{... | collective-permute-start | bytes 393224 | tf_op jit(solution)/shard_map/ppermute | solution.py:30
  44.1 1.3 %collective-permute-start.16 = (bf16[128,256]{1,0:T(8,128)(2,1)S(1)}, bf16[128,256]{1,0:T(8,128)(2,1)S(1)}, u32[]{:S(2)}, u32[]{:S(2)}) collective-permute-start(bf16[128,256]{1,0:T(8,128)(2,1)S(1)} %shard_map.96), channel_id=1, source_target_pairs={{0,4},{4,0},{8,12},{12,8},{16,20},{20,16},{24,28},{28,24},{1,5},{5... | collective-permute-start | bytes 196616 | tf_op jit(solution)/shard_map/ppermute | solution.py:30

commit v6 on v5

--- a/solution.py
+++ b/solution.py
@@ -41,7 +41,7 @@
 
 
 def sub_order(subs):
-    return [2, 1, 3] if subs == 4 else [1]
+    return [1, 3, 2] if subs == 4 else [1]
 
 
 def dense_kernel(steps, subs, rows_ref, counts_ref, tiles_ref, out_ref):
@@ -226,50 +226,72 @@
     )(pair, weight)
 
 
-def in_order(pairs, one, two):
-    mine = lax.axis_index("rep")
-    flip = (mine ^ one) > (mine ^ two)
-    first, second = pairs[one][...], pairs[two][...]
-    return jnp.where(flip, second, first), jnp.where(flip, first, second)
-
-
-def pair_kernel(scale, order, groups, dense_ref, *refs):
-    pairs = dict(zip(order, refs))
-    first_ref, keep_ref = refs[len(order) :]
+def pair_terms(dense, distances, pairs):
     block = pairs[0].shape[0] // 2
-    dpre = jnp.concatenate([pairs[d][block:, :] for d in order], axis=0)
+    first = jnp.dot(
+        dense, jnp.concatenate([pair[block:, :] for pair in pairs], axis=0), preferred_element_type=F32
+    )
+    if len(pairs) == 2:
+        mine = lax.axis_index("rep")
+        flip = (mine ^ distances[0]) > (mine ^ distances[1])
+        one, two = pairs
+        pairs = [jnp.where(flip, two, one), jnp.where(flip, one, two)]
+    agg = jnp.concatenate([pair[:block, :] for pair in pairs], axis=0)
+    dpre = jnp.concatenate([pair[block:, :] for pair in pairs], axis=0)
+    return first, lax.dot_general(agg, dpre, ROWS, preferred_element_type=F32)
+
+
+def early_kernel(distances, dense_ref, *refs):
+    pairs, (first_ref, grad_ref) = refs[: len(distances)], refs[len(distances) :]
+    block = first_ref.shape[0]
     rows = dense_ref.shape[0] // 2
-    first = jnp.dot(dense_ref[rows : rows + block, :], dpre, preferred_element_type=F32)
-    first_ref[:block, :] = first.astype(BF16)
-    half = first_ref.shape[1] // 2
-    upper = lower = 0.0
-    for one, two in groups:
-        low, high = in_order(pairs, one, two)
-        agg = jnp.concatenate([low[:block, :], high[:block, :]], axis=0)
-        dpre = jnp.concatenate([low[block:, :], high[block:, :]], axis=0)
-        upper = upper + lax.dot_general(agg[:, :half], dpre, ROWS, preferred_element_type=F32)
-        lower = lower + lax.dot_general(agg[:, half:], dpre, ROWS, preferred_element_type=F32)
-    upper, lower = upper * scale, lower * scale
+    part = dense_ref[rows : rows + block, : len(pairs) * block]
+    first_ref[...], grad_ref[...] = pair_terms(part, distances, [pair[...] for pair in pairs])
+
+
+def late_kernel(scale, distances, dense_ref, early_ref, grad_ref, *refs):
+    pairs, (first_ref, keep_ref) = refs[: len(distances)], refs[len(distances) :]
+    block = early_ref.shape[0]
+    rows, columns = dense_ref.shape[0] // 2, dense_ref.shape[1] - len(pairs) * block
+    part = dense_ref[rows : rows + block, columns:]
+    first, grad = pair_terms(part, distances, [pair[...] for pair in pairs])
+    first_ref[:block, :] = (early_ref[...] + first).astype(BF16)
+    grad = (grad_ref[...] + grad) * scale
+    half = grad.shape[0] // 2
+    upper, lower = grad[:half, :], grad[half:, :]
     is_first = lax.axis_index("blk") % 2 == 0
     first_ref[block:, :] = jnp.where(is_first, lower, upper).astype(BF16)
     keep_ref[...] = jnp.where(is_first, upper, lower)
 
 
-def apply_pairs(dense, pairs, order, scale):
+def apply_early(dense, pairs, distances):
+    block, feat = pairs[0].shape[0] // 2, pairs[0].shape[1]
+    return pl.pallas_call(
+        functools.partial(early_kernel, distances),
+        out_shape=[jax.ShapeDtypeStruct((n, feat), F32) for n in (block, feat)],
+        in_specs=[vmem()] * (1 + len(pairs)),
+        out_specs=[vmem()] * 2,
+        compiler_params=params(),
+        cost_estimate=pl.CostEstimate(
+            flops=6 * len(pairs) * block * feat * feat, bytes_accessed=dense.size, transcendentals=0
+        ),
+    )(dense, *pairs)
+
+
+def apply_late(dense, early, pairs, distances, scale):
     feat = pairs[0].shape[1]
     block, half = pairs[0].shape[0] // 2, feat // 2
-    groups = [(d, d + len(order) // 2) for d in range(len(order) // 2)]
     shapes = ((block + half, BF16), (half, F32))
     return pl.pallas_call(
-        functools.partial(pair_kernel, scale, order, groups),
+        functools.partial(late_kernel, scale, distances),
         out_shape=[jax.ShapeDtypeStruct((n, feat), t) for n, t in shapes],
-        in_specs=[vmem()] * (1 + len(pairs)),
+        in_specs=[vmem()] * (3 + len(pairs)),
         out_specs=[vmem()] * 2,
         compiler_params=params(),
         cost_estimate=pl.CostEstimate(
             flops=6 * len(pairs) * block * feat * feat, bytes_accessed=dense.size, transcendentals=0
         ),
-    )(dense, *pairs)
+    )(dense, *early, *pairs)
 
 
 def half_kernel(half_ref, *refs):
@@ -343,8 +365,12 @@
     pair = layer([own] + parts, weight, cotangent)
     pairs = gather(pair, near)
     activation = layer_output(pair, weight)
-    pairs, activation = lax.optimization_barrier((pairs, activation))
-    first, keep = apply_pairs(dense, pairs, [0] + near, 1.0 / math.sqrt(node_count))
+    pairs[-1], activation = lax.optimization_barrier((pairs[-1], activation))
+    cut, distances = subs // 2, [0] + near
+    early_terms = apply_early(dense, pairs[:cut], distances[:cut])
+    first, keep = apply_late(
+        dense, early_terms, pairs[cut:], distances[cut:], 1.0 / math.sqrt(node_count)
+    )
     other = send(first, "blk", at(1))
     rest, mine = apply_rest(dense, pairs, straight, block)
     rest, other = lax.optimization_barrier((rest, other))

time: 46.3 us -> 46.2 us (level)
  waiting for transfers between devices: 19.3 us -> 18.8 us
    ppermute x17, waiting for transfers between devices: 19.3 us -> 18.8 us  [send(): lax.ppermute(value, axis, [(i, step(i)) for i in range(lax.axis_size(axis...]
  transfers between devices with their start and end apart: 17 -> 17, of which waited for: 12 -> 11; matrix products, arithmetic and copies ran while one was open for 0% -> 0% of each run, Pallas kernels for 7% -> 8%
where the time goes in v6:
time: 46.2 us; the launch traced here: 46 us
  starting transfers between devices  19.6 us (42%)
  waiting for transfers between devices  18.8 us (41%)
  Pallas kernels  4.34 us (9%)
  local copies, waits for them, and re-layouts  1.8 us (4%)
  between operations  0.78 us (2%)
  other arithmetic  0.73 us (2%)
    ppermute x17, starting transfers between devices, send(): lax.ppermute(value, axis, [(i, step(i)) for i in range(lax.axis_size(axis...  19.6 us
    ppermute x17, waiting for transfers between devices, send(): lax.ppermute(value, axis, [(i, step(i)) for i in range(lax.axis_size(axis...  18.8 us
    unnamed x12, local copies, waits for them, and re-layouts  1.72 us
  transfers between devices with their start and end apart: 17, of which 11 were waited for; matrix products, arithmetic and copies ran while one was open for 0% of the time, Pallas kernels for 8%

profile of v6, /device:TPU:0, one launch (start us, length us, event | category | flops | bytes accessed | tf_op | source)
XLA Modules:
  0.0 46.0 jit_solution(15053245869993353682)
XLA Ops:
  0.6 0.0 copy-start.5
  0.6 5.1 %collective-permute-start = (bf16[128,256]{1,0:T(8,128)(2,1)}, bf16[128,256]{1,0:T(8,128)(2,1)S(1)}, u32[]{:S(2)}, u32[]{:S(2)}) collective-permute-start(bf16[128,256]{1,0:T(8,128)(2,1)} %refs_0_.1), channel_id=1, source_target_pairs={{0,3},{1,2},{2,1},{3,0},{4,7},{5,6},{6,5},{7,4},{8,11},{9,10},{10,... | collective-permute-start | bytes 196616 | tf_op jit(solution)/shard_map/ppermute | solution.py:30
  5.8 0.0 collective-permute-start.1
  5.8 0.6 %collective-permute-start.2 = (bf16[128,256]{1,0:T(8,128)(2,1)}, bf16[128,256]{1,0:T(8,128)(2,1)S(1)}, u32[]{:S(2)}, u32[]{:S(2)}) collective-permute-start(bf16[128,256]{1,0:T(8,128)(2,1)} %refs_0_.1), channel_id=1, source_target_pairs={{0,1},{1,0},{2,3},{3,2},{4,5},{5,4},{6,7},{7,6},{8,9},{9,8},{10,11... | collective-permute-start | bytes 196616 | tf_op jit(solution)/shard_map/ppermute | solution.py:30
  6.4 0.0 copy-done.5
  6.4 0.1 copy.9.rows_ref
  6.5 0.0 copy-start.4
  6.5 0.7 %copy-done.4 = s32[1,8,1]{1,2,0:T(1,128)S(1)} copy-done((s32[1,8,1]{1,2,0:T(1,128)S(1)}, s32[1,8,1]{1,2,0:T(1,128)}, u32[]{:S(2)}) %copy-start.4) | copy-done | bytes 56
  7.1 0.0 copy-start.1
  7.1 1.0 %copy-done.1 = bf16[1,8,1,128,256]{4,3,2,1,0:T(8,128)(2,1)S(1)} copy-done((bf16[1,8,1,128,256]{4,3,2,1,0:T(8,128)(2,1)S(1)}, bf16[1,8,1,128,256]{4,3,2,1,0:T(8,128)(2,1)}, u32[]{:S(2)}) %copy-start.1) | copy-done | bytes 524312
  8.2 0.0 copy-start.2
  8.2 0.8 %shard_map.85.dense_ref = bf16[1024,512]{1,0:T(8,128)(2,1)S(1)} custom-call(s32[8,2]{1,0:T(8,128)S(1)} %copy.9.rows_ref, s32[8]{0:T(128)S(1)} %bitcast.4, bf16[8,128,256]{2,1,0:T(8,128)(2,1)S(1)} %bitcast.3), custom_call_target="tpu_custom_call" | custom-call | bytes 2097152 | tf_op jit(solution)/shard_map/pallas_call | solution.py:68
  9.0 0.0 collective-permute-done.refs_1_
  9.0 2.5 %collective-permute-done.1.refs_2_ = bf16[128,256]{1,0:T(8,128)(2,1)S(1)} collective-permute-done((bf16[128,256]{1,0:T(8,128)(2,1)}, bf16[128,256]{1,0:T(8,128)(2,1)S(1)}, u32[]{:S(2)}, u32[]{:S(2)}) %collective-permute-start.1) | collective-permute-done | bytes 65568 | tf_op jit(solution)/shard_map/ppermute | solution.py:30
  11.6 0.0 collective-permute-done.2.refs_3_
  11.6 0.0 copy-done.2
  11.6 0.2 shard_map.87
  11.8 0.1 collective-permute-start.3
  11.9 0.4 shard_map.86
  12.3 0.8 %collective-permute-done.3.other_ref = bf16[128,256]{1,0:T(8,128)(2,1)S(1)} collective-permute-done((bf16[128,256]{1,0:T(8,128)(2,1)S(1)}, bf16[128,256]{1,0:T(8,128)(2,1)S(1)}, u32[]{:S(2)}, u32[]{:S(2)}) %collective-permute-start.3) | collective-permute-done | bytes 65568 | tf_op jit(solution)/shard_map/ppermute | solution.py:30
  13.1 0.2 collective-permute-start.4
  13.3 0.0 copy-start
  13.3 0.0 copy-start.3
  13.3 2.5 %collective-permute-start.5 = (bf16[128,256]{1,0:T(8,128)(2,1)S(1)}, bf16[128,256]{1,0:T(8,128)(2,1)S(1)}, u32[]{:S(2)}, u32[]{:S(2)}) collective-permute-start(bf16[128,256]{1,0:T(8,128)(2,1)S(1)} %shard_map.89), channel_id=1, source_target_pairs={{0,24},{4,28},{8,16},{12,20},{16,8},{20,12},{24,0},{28,4},{1,25},{... | collective-permute-start | bytes 196616 | tf_op jit(solution)/shard_map/ppermute | solution.py:30
  15.8 0.0 collective-permute-done.4.other_ref
  15.8 0.6 %collective-permute-start.6 = (bf16[128,256]{1,0:T(8,128)(2,1)S(1)}, bf16[128,256]{1,0:T(8,128)(2,1)S(1)}, u32[]{:S(2)}, u32[]{:S(2)}) collective-permute-start(bf16[128,256]{1,0:T(8,128)(2,1)S(1)} %get-tuple-element.40), channel_id=1, source_target_pairs={{0,8},{4,12},{8,0},{12,4},{16,24},{20,28},{24,16},{28,20},{1,9},{5... | collective-permute-start | bytes 196616 | tf_op jit(solution)/shard_map/ppermute | solution.py:30
  16.5 1.2 %collective-permute-start.7 = (bf16[128,256]{1,0:T(8,128)(2,1)S(1)}, bf16[128,256]{1,0:T(8,128)(2,1)S(1)}, u32[]{:S(2)}, u32[]{:S(2)}) collective-permute-start(bf16[128,256]{1,0:T(8,128)(2,1)S(1)} %get-tuple-element.41), channel_id=1, source_target_pairs={{0,16},{4,20},{8,24},{12,28},{16,0},{20,4},{24,8},{28,12},{1,17},{... | collective-permute-start | bytes 196616 | tf_op jit(solution)/shard_map/ppermute | solution.py:30
  17.7 1.1 %collective-permute-done.5.refs_1_ = bf16[128,256]{1,0:T(8,128)(2,1)S(1)} collective-permute-done((bf16[128,256]{1,0:T(8,128)(2,1)S(1)}, bf16[128,256]{1,0:T(8,128)(2,1)S(1)}, u32[]{:S(2)}, u32[]{:S(2)}) %collective-permute-start.5) | collective-permute-done | bytes 65568 | tf_op jit(solution)/shard_map/ppermute | solution.py:30
  18.7 1.4 %collective-permute-done.6.refs_2_ = bf16[128,256]{1,0:T(8,128)(2,1)S(1)} collective-permute-done((bf16[128,256]{1,0:T(8,128)(2,1)S(1)}, bf16[128,256]{1,0:T(8,128)(2,1)S(1)}, u32[]{:S(2)}, u32[]{:S(2)}) %collective-permute-start.6) | collective-permute-done | bytes 65568 | tf_op jit(solution)/shard_map/ppermute | solution.py:30
  20.2 0.5 %collective-permute-done.7.refs_3_ = bf16[128,256]{1,0:T(8,128)(2,1)S(1)} collective-permute-done((bf16[128,256]{1,0:T(8,128)(2,1)S(1)}, bf16[128,256]{1,0:T(8,128)(2,1)S(1)}, u32[]{:S(2)}, u32[]{:S(2)}) %collective-permute-start.7) | collective-permute-done | bytes 65568 | tf_op jit(solution)/shard_map/ppermute | solution.py:30
  20.7 0.0 copy-done
  20.7 0.0 copy-done.3
  20.7 0.2 shard_map.90.pair_ref.refs_0_
  20.9 1.6 %collective-permute-start.8 = (bf16[256,256]{1,0:T(8,128)(2,1)S(1)}, bf16[256,256]{1,0:T(8,128)(2,1)S(1)}, u32[]{:S(2)}, u32[]{:S(2)}) collective-permute-start(bf16[256,256]{1,0:T(8,128)(2,1)S(1)} %shard_map.90.pair_ref.refs_0_), channel_id=1, source_target_pairs={{0,2},{1,3},{2,0},{3,1},{4,6},{5,7},{6,4},{7,5},{8,10},{9,11},{10,... | collective-permute-start | bytes 393224 | tf_op jit(solution)/shard_map/ppermute | solution.py:30
  22.6 1.7 %collective-permute-start.9 = (bf16[256,256]{1,0:T(8,128)(2,1)S(1)}, bf16[256,256]{1,0:T(8,128)(2,1)S(1)}, u32[]{:S(2)}, u32[]{:S(2)}) collective-permute-start(bf16[256,256]{1,0:T(8,128)(2,1)S(1)} %shard_map.90.pair_ref.refs_0_), channel_id=1, source_target_pairs={{0,1},{1,0},{2,3},{3,2},{4,5},{5,4},{6,7},{7,6},{8,9},{9,8},{10,11... | collective-permute-start | bytes 393224 | tf_op jit(solution)/shard_map/ppermute | solution.py:30
  24.3 1.1 %collective-permute-start.10 = (bf16[256,256]{1,0:T(8,128)(2,1)S(1)}, bf16[256,256]{1,0:T(8,128)(2,1)S(1)}, u32[]{:S(2)}, u32[]{:S(2)}) collective-permute-start(bf16[256,256]{1,0:T(8,128)(2,1)S(1)} %shard_map.90.pair_ref.refs_0_), channel_id=1, source_target_pairs={{0,3},{1,2},{2,1},{3,0},{4,7},{5,6},{6,5},{7,4},{8,11},{9,10},{10,... | collective-permute-start | bytes 393224 | tf_op jit(solution)/shard_map/ppermute | solution.py:30
  25.4 0.8 %shard_map.91 = bf16[128,256]{1,0:T(8,128)(2,1)} custom-call(bf16[256,256]{1,0:T(8,128)(2,1)S(1)} %shard_map.90.pair_ref.refs_0_, bf16[256,256]{1,0:T(8,128)(2,1)S(1)} %copy-done), custom_call_target="tpu_custom_call" | custom-call | flops 16777216 | bytes 262144 | tf_op jit(solution)/shard_map/pallas_call | solution.py:217
  26.2 4.9 %collective-permute-done.8.refs_3_.refs_1_ = bf16[256,256]{1,0:T(8,128)(2,1)S(1)} collective-permute-done((bf16[256,256]{1,0:T(8,128)(2,1)S(1)}, bf16[256,256]{1,0:T(8,128)(2,1)S(1)}, u32[]{:S(2)}, u32[]{:S(2)}) %collective-permute-start.8) | collective-permute-done | bytes 131104 | tf_op jit(solution)/shard_map/ppermute | solution.py:30
  31.2 0.0 collective-permute-done.9.refs_1_
  31.2 0.2 shard_map.93
  31.4 1.2 %collective-permute-done.10.refs_2_.refs_0_ = bf16[256,256]{1,0:T(8,128)(2,1)S(1)} collective-permute-done((bf16[256,256]{1,0:T(8,128)(2,1)S(1)}, bf16[256,256]{1,0:T(8,128)(2,1)S(1)}, u32[]{:S(2)}, u32[]{:S(2)}) %collective-permute-start.10) | collective-permute-done | bytes 131104 | tf_op jit(solution)/shard_map/ppermute | solution.py:30
  32.6 0.2 shard_map.94
  32.8 0.1 collective-permute-start.11
  32.9 0.4 shard_map.92
  33.3 0.9 %collective-permute-done.11.other_ref = bf16[256,256]{1,0:T(8,128)(2,1)S(1)} collective-permute-done((bf16[256,256]{1,0:T(8,128)(2,1)S(1)}, bf16[256,256]{1,0:T(8,128)(2,1)S(1)}, u32[]{:S(2)}, u32[]{:S(2)}) %collective-permute-start.11) | collective-permute-done | bytes 131104 | tf_op jit(solution)/shard_map/ppermute | solution.py:30
  34.2 0.1 collective-permute-start.13
  34.4 2.7 %collective-permute-start.12 = (bf16[256,256]{1,0:T(8,128)(2,1)S(1)}, bf16[256,256]{1,0:T(8,128)(2,1)S(1)}, u32[]{:S(2)}, u32[]{:S(2)}) collective-permute-start(bf16[256,256]{1,0:T(8,128)(2,1)S(1)} %get-tuple-element.52), channel_id=1, source_target_pairs={{0,24},{4,28},{8,16},{12,20},{16,8},{20,12},{24,0},{28,4},{1,25},{... | collective-permute-start | bytes 393224 | tf_op jit(solution)/shard_map/ppermute | solution.py:30
  37.1 0.0 collective-permute-done.13.other_ref
  37.2 0.3 collective-permute-start.14
  37.5 1.5 %collective-permute-start.15 = (bf16[256,256]{1,0:T(8,128)(2,1)S(1)}, bf16[256,256]{1,0:T(8,128)(2,1)S(1)}, u32[]{:S(2)}, u32[]{:S(2)}) collective-permute-start(bf16[256,256]{1,0:T(8,128)(2,1)S(1)} %get-tuple-element.55), channel_id=1, source_target_pairs={{0,16},{4,20},{8,24},{12,28},{16,0},{20,4},{24,8},{28,12},{1,17},{... | collective-permute-start | bytes 393224 | tf_op jit(solution)/shard_map/ppermute | solution.py:30
  39.0 2.7 %collective-permute-done.12.refs_0_ = bf16[256,256]{1,0:T(8,128)(2,1)S(1)} collective-permute-done((bf16[256,256]{1,0:T(8,128)(2,1)S(1)}, bf16[256,256]{1,0:T(8,128)(2,1)S(1)}, u32[]{:S(2)}, u32[]{:S(2)}) %collective-permute-start.12) | collective-permute-done | bytes 131104 | tf_op jit(solution)/shard_map/ppermute | solution.py:30
  41.7 2.2 %collective-permute-done.14.refs_1_ = bf16[256,256]{1,0:T(8,128)(2,1)S(1)} collective-permute-done((bf16[256,256]{1,0:T(8,128)(2,1)S(1)}, bf16[256,256]{1,0:T(8,128)(2,1)S(1)}, u32[]{:S(2)}, u32[]{:S(2)}) %collective-permute-start.14) | collective-permute-done | bytes 131104 | tf_op jit(solution)/shard_map/ppermute | solution.py:30
  43.9 0.0 collective-permute-done.15.refs_2_
  44.0 0.1 collective-permute-start.16
  44.1 0.8 %shard_map.98 = bf16[128,256]{1,0:T(8,128)(2,1)} custom-call(bf16[256,256]{1,0:T(8,128)(2,1)S(1)} %copy-done, f32[128,256]{1,0:T(8,128)S(1)} %get-tuple-element.56.own_ref, bf16[256,256]{1,0:T(8,128)(2,1)S(1)} %collective-permute-done.12.refs_0_, bf16[256,256]{1,0:T(8,128)(2,1)S(1)} %collective-permute-done.14.refs_1_, ...), custom_call_target="tpu_custom_call" | custom-call | flops 16777216 | bytes 393216 | tf_op jit(solution)/shard_map/pallas_call | solution.py:324
  44.9 0.4 collective-permute-done.16
  45.3 0.7 %fusion = f32[256,256]{1,0:T(8,128)} fusion(bf16[128,256]{1,0:T(8,128)(2,1)S(1)} %collective-permute-done.16, bf16[128,256]{1,0:T(8,128)(2,1)S(1)} %shard_map.97, pred[]{:T(512)S(6)} %eq.5), kind=kLoop, calls=%fused_computation.1 | loop fusion | flops 655360 | bytes 393217 | tf_op jit(solution)/shard_map/convert_element_type | solution.py:380
  (5 shorter events, 0.2 us)
Async XLA Ops:
  0.6 5.8 %copy-start.5 = (s32[1,8,1,2]{1,3,2,0:T(2,128)S(1)}, s32[1,8,1,2]{1,3,2,0:T(2,128)}, u32[]{:S(2)}) copy-start(s32[1,8,1,2]{1,3,2,0:T(2,128)} %param.9) | copy-start | bytes 196
  0.6 8.4 %collective-permute-start = (bf16[128,256]{1,0:T(8,128)(2,1)}, bf16[128,256]{1,0:T(8,128)(2,1)S(1)}, u32[]{:S(2)}, u32[]{:S(2)}) collective-permute-start(bf16[128,256]{1,0:T(8,128)(2,1)} %refs_0_.1), channel_id=1, source_target_pairs={{0,3},{1,2},{2,1},{3,0},{4,7},{5,6},{6,5},{7,4},{8,11},{9,10},{10,... | collective-permute-start | bytes 196616 | tf_op jit(solution)/shard_map/ppermute | solution.py:30
  5.8 5.8 %collective-permute-start.1 = (bf16[128,256]{1,0:T(8,128)(2,1)}, bf16[128,256]{1,0:T(8,128)(2,1)S(1)}, u32[]{:S(2)}, u32[]{:S(2)}) collective-permute-start(bf16[128,256]{1,0:T(8,128)(2,1)} %refs_0_.1), channel_id=1, source_target_pairs={{0,2},{1,3},{2,0},{3,1},{4,6},{5,7},{6,4},{7,5},{8,10},{9,11},{10,... | collective-permute-start | bytes 196616 | tf_op jit(solution)/shard_map/ppermute | solution.py:30
  5.8 5.8 %collective-permute-start.2 = (bf16[128,256]{1,0:T(8,128)(2,1)}, bf16[128,256]{1,0:T(8,128)(2,1)S(1)}, u32[]{:S(2)}, u32[]{:S(2)}) collective-permute-start(bf16[128,256]{1,0:T(8,128)(2,1)} %refs_0_.1), channel_id=1, source_target_pairs={{0,1},{1,0},{2,3},{3,2},{4,5},{5,4},{6,7},{7,6},{8,9},{9,8},{10,11... | collective-permute-start | bytes 196616 | tf_op jit(solution)/shard_map/ppermute | solution.py:30
  6.5 0.7 %copy-start.4 = (s32[1,8,1]{1,2,0:T(1,128)S(1)}, s32[1,8,1]{1,2,0:T(1,128)}, u32[]{:S(2)}) copy-start(s32[1,8,1]{1,2,0:T(1,128)} %param.10) | copy-start | bytes 100
  7.1 1.0 %copy-start.1 = (bf16[1,8,1,128,256]{4,3,2,1,0:T(8,128)(2,1)S(1)}, bf16[1,8,1,128,256]{4,3,2,1,0:T(8,128)(2,1)}, u32[]{:S(2)}) copy-start(bf16[1,8,1,128,256]{4,3,2,1,0:T(8,128)(2,1)} %param.11) | copy-start | bytes 1572868
  8.2 3.4 %copy-start.2 = (bf16[128,256]{1,0:T(8,128)(2,1)S(1)}, bf16[128,256]{1,0:T(8,128)(2,1)}, u32[]{:S(2)}) copy-start(bf16[128,256]{1,0:T(8,128)(2,1)} %refs_0_.1) | copy-start | bytes 196612
  11.8 1.3 %collective-permute-start.3 = (bf16[128,256]{1,0:T(8,128)(2,1)S(1)}, bf16[128,256]{1,0:T(8,128)(2,1)S(1)}, u32[]{:S(2)}, u32[]{:S(2)}) collective-permute-start(bf16[128,256]{1,0:T(8,128)(2,1)S(1)} %shard_map.87), channel_id=1, source_target_pairs={{0,4},{4,0},{8,12},{12,8},{16,20},{20,16},{24,28},{28,24},{1,5},{5... | collective-permute-start | bytes 196616 | tf_op jit(solution)/shard_map/ppermute | solution.py:30
  13.1 2.7 %collective-permute-start.4 = (bf16[384,256]{1,0:T(8,128)(2,1)S(1)}, bf16[384,256]{1,0:T(8,128)(2,1)S(1)}, u32[]{:S(2)}, u32[]{:S(2)}) collective-permute-start(bf16[384,256]{1,0:T(8,128)(2,1)S(1)} %get-tuple-element.37), channel_id=1, source_target_pairs={{0,4},{4,0},{8,12},{12,8},{16,20},{20,16},{24,28},{28,24},{1,5},{5... | collective-permute-start | bytes 589832 | tf_op jit(solution)/shard_map/ppermute | solution.py:30
  13.3 7.4 %copy-start = (bf16[256,256]{1,0:T(8,128)(2,1)S(1)}, bf16[256,256]{1,0:T(8,128)(2,1)}, u32[]{:S(2)}) copy-start(bf16[256,256]{1,0:T(8,128)(2,1)} %weight_ref.3) | copy-start | bytes 393220
  13.3 7.4 %copy-start.3 = (bf16[128,256]{1,0:T(8,128)(2,1)S(1)}, bf16[128,256]{1,0:T(8,128)(2,1)}, u32[]{:S(2)}) copy-start(bf16[128,256]{1,0:T(8,128)(2,1)} %refs_5_.1) | copy-start | bytes 196612
  13.3 5.4 %collective-permute-start.5 = (bf16[128,256]{1,0:T(8,128)(2,1)S(1)}, bf16[128,256]{1,0:T(8,128)(2,1)S(1)}, u32[]{:S(2)}, u32[]{:S(2)}) collective-permute-start(bf16[128,256]{1,0:T(8,128)(2,1)S(1)} %shard_map.89), channel_id=1, source_target_pairs={{0,24},{4,28},{8,16},{12,20},{16,8},{20,12},{24,0},{28,4},{1,25},{... | collective-permute-start | bytes 196616 | tf_op jit(solution)/shard_map/ppermute | solution.py:30
  15.8 4.3 %collective-permute-start.6 = (bf16[128,256]{1,0:T(8,128)(2,1)S(1)}, bf16[128,256]{1,0:T(8,128)(2,1)S(1)}, u32[]{:S(2)}, u32[]{:S(2)}) collective-permute-start(bf16[128,256]{1,0:T(8,128)(2,1)S(1)} %get-tuple-element.40), channel_id=1, source_target_pairs={{0,8},{4,12},{8,0},{12,4},{16,24},{20,28},{24,16},{28,20},{1,9},{5... | collective-permute-start | bytes 196616 | tf_op jit(solution)/shard_map/ppermute | solution.py:30
  16.5 4.3 %collective-permute-start.7 = (bf16[128,256]{1,0:T(8,128)(2,1)S(1)}, bf16[128,256]{1,0:T(8,128)(2,1)S(1)}, u32[]{:S(2)}, u32[]{:S(2)}) collective-permute-start(bf16[128,256]{1,0:T(8,128)(2,1)S(1)} %get-tuple-element.41), channel_id=1, source_target_pairs={{0,16},{4,20},{8,24},{12,28},{16,0},{20,4},{24,8},{28,12},{1,17},{... | collective-permute-start | bytes 196616 | tf_op jit(solution)/shard_map/ppermute | solution.py:30
  20.9 10.2 %collective-permute-start.8 = (bf16[256,256]{1,0:T(8,128)(2,1)S(1)}, bf16[256,256]{1,0:T(8,128)(2,1)S(1)}, u32[]{:S(2)}, u32[]{:S(2)}) collective-permute-start(bf16[256,256]{1,0:T(8,128)(2,1)S(1)} %shard_map.90.pair_ref.refs_0_), channel_id=1, source_target_pairs={{0,2},{1,3},{2,0},{3,1},{4,6},{5,7},{6,4},{7,5},{8,10},{9,11},{10,... | collective-permute-start | bytes 393224 | tf_op jit(solution)/shard_map/ppermute | solution.py:30
  22.6 8.6 %collective-permute-start.9 = (bf16[256,256]{1,0:T(8,128)(2,1)S(1)}, bf16[256,256]{1,0:T(8,128)(2,1)S(1)}, u32[]{:S(2)}, u32[]{:S(2)}) collective-permute-start(bf16[256,256]{1,0:T(8,128)(2,1)S(1)} %shard_map.90.pair_ref.refs_0_), channel_id=1, source_target_pairs={{0,1},{1,0},{2,3},{3,2},{4,5},{5,4},{6,7},{7,6},{8,9},{9,8},{10,11... | collective-permute-start | bytes 393224 | tf_op jit(solution)/shard_map/ppermute | solution.py:30
  24.3 8.3 %collective-permute-start.10 = (bf16[256,256]{1,0:T(8,128)(2,1)S(1)}, bf16[256,256]{1,0:T(8,128)(2,1)S(1)}, u32[]{:S(2)}, u32[]{:S(2)}) collective-permute-start(bf16[256,256]{1,0:T(8,128)(2,1)S(1)} %shard_map.90.pair_ref.refs_0_), channel_id=1, source_target_pairs={{0,3},{1,2},{2,1},{3,0},{4,7},{5,6},{6,5},{7,4},{8,11},{9,10},{10,... | collective-permute-start | bytes 393224 | tf_op jit(solution)/shard_map/ppermute | solution.py:30
  32.8 1.4 %collective-permute-start.11 = (bf16[256,256]{1,0:T(8,128)(2,1)S(1)}, bf16[256,256]{1,0:T(8,128)(2,1)S(1)}, u32[]{:S(2)}, u32[]{:S(2)}) collective-permute-start(bf16[256,256]{1,0:T(8,128)(2,1)S(1)} %get-tuple-element.48), channel_id=1, source_target_pairs={{0,4},{4,0},{8,12},{12,8},{16,20},{20,16},{24,28},{28,24},{1,5},{5... | collective-permute-start | bytes 393224 | tf_op jit(solution)/shard_map/ppermute | solution.py:30
  34.2 2.9 %collective-permute-start.13 = (bf16[384,256]{1,0:T(8,128)(2,1)S(1)}, bf16[384,256]{1,0:T(8,128)(2,1)S(1)}, u32[]{:S(2)}, u32[]{:S(2)}) collective-permute-start(bf16[384,256]{1,0:T(8,128)(2,1)S(1)} %get-tuple-element.53), channel_id=1, source_target_pairs={{0,4},{4,0},{8,12},{12,8},{16,20},{20,16},{24,28},{28,24},{1,5},{5... | collective-permute-start | bytes 589832 | tf_op jit(solution)/shard_map/ppermute | solution.py:30
  34.4 7.3 %collective-permute-start.12 = (bf16[256,256]{1,0:T(8,128)(2,1)S(1)}, bf16[256,256]{1,0:T(8,128)(2,1)S(1)}, u32[]{:S(2)}, u32[]{:S(2)}) collective-permute-start(bf16[256,256]{1,0:T(8,128)(2,1)S(1)} %get-tuple-element.52), channel_id=1, source_target_pairs={{0,24},{4,28},{8,16},{12,20},{16,8},{20,12},{24,0},{28,4},{1,25},{... | collective-permute-start | bytes 393224 | tf_op jit(solution)/shard_map/ppermute | solution.py:30
  37.2 6.8 %collective-permute-start.14 = (bf16[256,256]{1,0:T(8,128)(2,1)S(1)}, bf16[256,256]{1,0:T(8,128)(2,1)S(1)}, u32[]{:S(2)}, u32[]{:S(2)}) collective-permute-start(bf16[256,256]{1,0:T(8,128)(2,1)S(1)} %get-tuple-element.54), channel_id=1, source_target_pairs={{0,8},{4,12},{8,0},{12,4},{16,24},{20,28},{24,16},{28,20},{1,9},{5... | collective-permute-start | bytes 393224 | tf_op jit(solution)/shard_map/ppermute | solution.py:30
  37.5 6.4 %collective-permute-start.15 = (bf16[256,256]{1,0:T(8,128)(2,1)S(1)}, bf16[256,256]{1,0:T(8,128)(2,1)S(1)}, u32[]{:S(2)}, u32[]{:S(2)}) collective-permute-start(bf16[256,256]{1,0:T(8,128)(2,1)S(1)} %get-tuple-element.55), channel_id=1, source_target_pairs={{0,16},{4,20},{8,24},{12,28},{16,0},{20,4},{24,8},{28,12},{1,17},{... | collective-permute-start | bytes 393224 | tf_op jit(solution)/shard_map/ppermute | solution.py:30
  44.0 1.3 %collective-permute-start.16 = (bf16[128,256]{1,0:T(8,128)(2,1)S(1)}, bf16[128,256]{1,0:T(8,128)(2,1)S(1)}, u32[]{:S(2)}, u32[]{:S(2)}) collective-permute-start(bf16[128,256]{1,0:T(8,128)(2,1)S(1)} %shard_map.97), channel_id=1, source_target_pairs={{0,4},{4,0},{8,12},{12,8},{16,20},{20,16},{24,28},{28,24},{1,5},{5... | collective-permute-start | bytes 196616 | tf_op jit(solution)/shard_map/ppermute | solution.py:30

commit v7 on v6

--- a/solution.py
+++ b/solution.py
@@ -75,26 +75,30 @@
     )(rows, counts, tiles)
 
 
-def first_kernel(order, dense_ref, *refs):
-    nodes = jnp.concatenate([refs[k][...] for k in order], axis=0)
-    out_ref = refs[-1]
-    half = dense_ref.shape[0] // 2
-    rows = dense_ref[half : half + out_ref.shape[0], :]
-    out_ref[...] = jnp.dot(rows, nodes, preferred_element_type=F32).astype(out_ref.dtype)
-
-
-def apply_first(dense, pieces, order):
+def first_kernel(blocks, n_added, dense_ref, *refs):
+    added, pieces, out_ref = refs[:n_added], refs[n_added:-1], refs[-1]
+    block = out_ref.shape[0]
+    rows = dense_ref.shape[0] // 2
+    nodes = jnp.concatenate([piece[...] for piece in pieces], axis=0)
+    columns = [dense_ref[rows : rows + block, k * block : (k + 1) * block] for k in blocks]
+    product = jnp.dot(jnp.concatenate(columns, axis=1), nodes, preferred_element_type=F32)
+    for more in added:
+        product = more[...] + product
+    out_ref[...] = product.astype(out_ref.dtype)
+
+
+def apply_first(dense, pieces, order, kind, *added):
     shape = pieces[0].shape
     return pl.pallas_call(
-        functools.partial(first_kernel, order),
-        out_shape=jax.ShapeDtypeStruct(shape, BF16),
-        in_specs=[vmem()] * (1 + len(pieces)),
-        out_specs=vmem(),
-        compiler_params=params(),
-        cost_estimate=pl.CostEstimate(
-            flops=2 * dense.shape[1] * shape[0] * shape[1], bytes_accessed=dense.size // 4, transcendentals=0
-        ),
-    )(dense, *pieces)
+        functools.partial(first_kernel, order, len(added)),
+        out_shape=jax.ShapeDtypeStruct(shape, kind),
+        in_specs=[vmem()] * (1 + len(added) + len(pieces)),
+        out_specs=vmem(),
+        compiler_params=params(),
+        cost_estimate=pl.CostEstimate(
+            flops=2 * len(pieces) * shape[0] * shape[0] * shape[1], bytes_accessed=dense.size // 4, transcendentals=0
+        ),
+    )(dense, *added, *pieces)
 
 
 def rest_kernel(block, order, dense_ref, *refs):
@@ -354,8 +358,12 @@
     odd = [lambda i, step=step: step(i) ^ 1 for step in even]
     dense = dense_adjacency(even + odd, [0] + near, rows, counts, tiles)
 
-    pieces, dense = lax.optimization_barrier((gather(features, early), dense))
-    other = send(apply_first(dense, pieces, order), "blk", at(1))
+    pieces = gather(features, early)
+    places = [([0] + near).index(d) for d in [0] + early]
+    cut = subs // 2
+    first = apply_first(dense, pieces[:cut], places[:cut], F32)
+    first = apply_first(dense, pieces[cut:], places[cut:], BF16, first)
+    other = send(first, "blk", at(1))
     rest, mine = apply_rest(dense, pieces, order, block)
     rest, other = lax.optimization_barrier((rest, other))
     (first,) = first_sum(mine, other, block)
@@ -366,7 +374,7 @@
     pairs = gather(pair, near)
     activation = layer_output(pair, weight)
     pairs[-1], activation = lax.optimization_barrier((pairs[-1], activation))
-    cut, distances = subs // 2, [0] + near
+    distances = [0] + near
     early_terms = apply_early(dense, pairs[:cut], distances[:cut])
     first, keep = apply_late(
         dense, early_terms, pairs[cut:], distances[cut:], 1.0 / math.sqrt(node_count)

time: 46.2 us -> 46.2 us (level)
  no operation moved by 1% of the time
where the time goes in v7:
time: 46.2 us; the launch traced here: 46 us
  starting transfers between devices  19.6 us (42%)
  waiting for transfers between devices  18.7 us (40%)
  Pallas kernels  4.46 us (10%)
  local copies, waits for them, and re-layouts  1.8 us (4%)
  between operations  0.8 us (2%)
  other arithmetic  0.73 us (2%)
    ppermute x17, starting transfers between devices, send(): lax.ppermute(value, axis, [(i, step(i)) for i in range(lax.axis_size(axis...  19.6 us
    ppermute x17, waiting for transfers between devices, send(): lax.ppermute(value, axis, [(i, step(i)) for i in range(lax.axis_size(axis...  18.7 us
    unnamed x12, local copies, waits for them, and re-layouts  1.72 us
  transfers between devices with their start and end apart: 17, of which 11 were waited for; matrix products, arithmetic and copies ran while one was open for 0% of the time, Pallas kernels for 8%

profile of v7, /device:TPU:0, one launch (start us, length us, event | category | flops | bytes accessed | tf_op | source)
XLA Modules:
  0.0 46.0 jit_solution(9631989452791729688)
XLA Ops:
  0.6 0.0 copy-start.5
  0.6 5.1 %collective-permute-start = (bf16[128,256]{1,0:T(8,128)(2,1)}, bf16[128,256]{1,0:T(8,128)(2,1)S(1)}, u32[]{:S(2)}, u32[]{:S(2)}) collective-permute-start(bf16[128,256]{1,0:T(8,128)(2,1)} %refs_0_.3), channel_id=1, source_target_pairs={{0,3},{1,2},{2,1},{3,0},{4,7},{5,6},{6,5},{7,4},{8,11},{9,10},{10,... | collective-permute-start | bytes 196616 | tf_op jit(solution)/shard_map/ppermute | solution.py:30
  5.8 0.0 collective-permute-start.1
  5.8 0.6 %collective-permute-start.2 = (bf16[128,256]{1,0:T(8,128)(2,1)}, bf16[128,256]{1,0:T(8,128)(2,1)S(1)}, u32[]{:S(2)}, u32[]{:S(2)}) collective-permute-start(bf16[128,256]{1,0:T(8,128)(2,1)} %refs_0_.3), channel_id=1, source_target_pairs={{0,1},{1,0},{2,3},{3,2},{4,5},{5,4},{6,7},{7,6},{8,9},{9,8},{10,11... | collective-permute-start | bytes 196616 | tf_op jit(solution)/shard_map/ppermute | solution.py:30
  6.4 0.0 copy-done.5
  6.4 0.1 copy.9.rows_ref
  6.5 0.0 copy-start.4
  6.5 0.7 %copy-done.4 = s32[1,8,1]{1,2,0:T(1,128)S(1)} copy-done((s32[1,8,1]{1,2,0:T(1,128)S(1)}, s32[1,8,1]{1,2,0:T(1,128)}, u32[]{:S(2)}) %copy-start.4) | copy-done | bytes 56
  7.1 0.0 copy-start.1
  7.1 1.0 %copy-done.1 = bf16[1,8,1,128,256]{4,3,2,1,0:T(8,128)(2,1)S(1)} copy-done((bf16[1,8,1,128,256]{4,3,2,1,0:T(8,128)(2,1)S(1)}, bf16[1,8,1,128,256]{4,3,2,1,0:T(8,128)(2,1)}, u32[]{:S(2)}) %copy-start.1) | copy-done | bytes 524312
  8.2 0.0 copy-start.2
  8.2 0.8 %shard_map.85.dense_ref = bf16[1024,512]{1,0:T(8,128)(2,1)S(1)} custom-call(s32[8,2]{1,0:T(8,128)S(1)} %copy.9.rows_ref, s32[8]{0:T(128)S(1)} %bitcast.4, bf16[8,128,256]{2,1,0:T(8,128)(2,1)S(1)} %bitcast.3), custom_call_target="tpu_custom_call" | custom-call | bytes 2097152 | tf_op jit(solution)/shard_map/pallas_call | solution.py:68
  9.0 0.0 collective-permute-done.refs_1_
  9.0 0.0 copy-done.2
  9.0 0.2 shard_map.87.refs_0_
  9.2 2.4 %collective-permute-done.1.refs_2_.refs_1_ = bf16[128,256]{1,0:T(8,128)(2,1)S(1)} collective-permute-done((bf16[128,256]{1,0:T(8,128)(2,1)}, bf16[128,256]{1,0:T(8,128)(2,1)S(1)}, u32[]{:S(2)}, u32[]{:S(2)}) %collective-permute-start.1) | collective-permute-done | bytes 65568 | tf_op jit(solution)/shard_map/ppermute | solution.py:30
  11.6 0.0 collective-permute-done.2.refs_3_.refs_2_
  11.6 0.2 shard_map.88
  11.7 0.1 collective-permute-start.3
  11.8 0.4 shard_map.86
  12.2 0.8 %collective-permute-done.3.other_ref = bf16[128,256]{1,0:T(8,128)(2,1)S(1)} collective-permute-done((bf16[128,256]{1,0:T(8,128)(2,1)S(1)}, bf16[128,256]{1,0:T(8,128)(2,1)S(1)}, u32[]{:S(2)}, u32[]{:S(2)}) %collective-permute-start.3) | collective-permute-done | bytes 65568 | tf_op jit(solution)/shard_map/ppermute | solution.py:30
  13.1 0.2 collective-permute-start.4
  13.2 0.0 copy-start
  13.2 0.0 copy-start.3
  13.3 2.5 %collective-permute-start.5 = (bf16[128,256]{1,0:T(8,128)(2,1)S(1)}, bf16[128,256]{1,0:T(8,128)(2,1)S(1)}, u32[]{:S(2)}, u32[]{:S(2)}) collective-permute-start(bf16[128,256]{1,0:T(8,128)(2,1)S(1)} %shard_map.90), channel_id=1, source_target_pairs={{0,24},{4,28},{8,16},{12,20},{16,8},{20,12},{24,0},{28,4},{1,25},{... | collective-permute-start | bytes 196616 | tf_op jit(solution)/shard_map/ppermute | solution.py:30
  15.8 0.0 collective-permute-done.4.other_ref
  15.8 0.6 %collective-permute-start.6 = (bf16[128,256]{1,0:T(8,128)(2,1)S(1)}, bf16[128,256]{1,0:T(8,128)(2,1)S(1)}, u32[]{:S(2)}, u32[]{:S(2)}) collective-permute-start(bf16[128,256]{1,0:T(8,128)(2,1)S(1)} %get-tuple-element.30), channel_id=1, source_target_pairs={{0,8},{4,12},{8,0},{12,4},{16,24},{20,28},{24,16},{28,20},{1,9},{5... | collective-permute-start | bytes 196616 | tf_op jit(solution)/shard_map/ppermute | solution.py:30
  16.4 1.2 %collective-permute-start.7 = (bf16[128,256]{1,0:T(8,128)(2,1)S(1)}, bf16[128,256]{1,0:T(8,128)(2,1)S(1)}, u32[]{:S(2)}, u32[]{:S(2)}) collective-permute-start(bf16[128,256]{1,0:T(8,128)(2,1)S(1)} %get-tuple-element.31), channel_id=1, source_target_pairs={{0,16},{4,20},{8,24},{12,28},{16,0},{20,4},{24,8},{28,12},{1,17},{... | collective-permute-start | bytes 196616 | tf_op jit(solution)/shard_map/ppermute | solution.py:30
  17.6 1.1 %collective-permute-done.5.refs_1_ = bf16[128,256]{1,0:T(8,128)(2,1)S(1)} collective-permute-done((bf16[128,256]{1,0:T(8,128)(2,1)S(1)}, bf16[128,256]{1,0:T(8,128)(2,1)S(1)}, u32[]{:S(2)}, u32[]{:S(2)}) %collective-permute-start.5) | collective-permute-done | bytes 65568 | tf_op jit(solution)/shard_map/ppermute | solution.py:30
  18.7 1.4 %collective-permute-done.6.refs_2_ = bf16[128,256]{1,0:T(8,128)(2,1)S(1)} collective-permute-done((bf16[128,256]{1,0:T(8,128)(2,1)S(1)}, bf16[128,256]{1,0:T(8,128)(2,1)S(1)}, u32[]{:S(2)}, u32[]{:S(2)}) %collective-permute-start.6) | collective-permute-done | bytes 65568 | tf_op jit(solution)/shard_map/ppermute | solution.py:30
  20.1 0.5 %collective-permute-done.7.refs_3_ = bf16[128,256]{1,0:T(8,128)(2,1)S(1)} collective-permute-done((bf16[128,256]{1,0:T(8,128)(2,1)S(1)}, bf16[128,256]{1,0:T(8,128)(2,1)S(1)}, u32[]{:S(2)}, u32[]{:S(2)}) %collective-permute-start.7) | collective-permute-done | bytes 65568 | tf_op jit(solution)/shard_map/ppermute | solution.py:30
  20.7 0.0 copy-done
  20.7 0.0 copy-done.3
  20.7 0.2 shard_map.91.pair_ref.refs_0_
  20.9 1.6 %collective-permute-start.8 = (bf16[256,256]{1,0:T(8,128)(2,1)S(1)}, bf16[256,256]{1,0:T(8,128)(2,1)S(1)}, u32[]{:S(2)}, u32[]{:S(2)}) collective-permute-start(bf16[256,256]{1,0:T(8,128)(2,1)S(1)} %shard_map.91.pair_ref.refs_0_), channel_id=1, source_target_pairs={{0,2},{1,3},{2,0},{3,1},{4,6},{5,7},{6,4},{7,5},{8,10},{9,11},{10,... | collective-permute-start | bytes 393224 | tf_op jit(solution)/shard_map/ppermute | solution.py:30
  22.6 1.7 %collective-permute-start.9 = (bf16[256,256]{1,0:T(8,128)(2,1)S(1)}, bf16[256,256]{1,0:T(8,128)(2,1)S(1)}, u32[]{:S(2)}, u32[]{:S(2)}) collective-permute-start(bf16[256,256]{1,0:T(8,128)(2,1)S(1)} %shard_map.91.pair_ref.refs_0_), channel_id=1, source_target_pairs={{0,1},{1,0},{2,3},{3,2},{4,5},{5,4},{6,7},{7,6},{8,9},{9,8},{10,11... | collective-permute-start | bytes 393224 | tf_op jit(solution)/shard_map/ppermute | solution.py:30
  24.3 1.1 %collective-permute-start.10 = (bf16[256,256]{1,0:T(8,128)(2,1)S(1)}, bf16[256,256]{1,0:T(8,128)(2,1)S(1)}, u32[]{:S(2)}, u32[]{:S(2)}) collective-permute-start(bf16[256,256]{1,0:T(8,128)(2,1)S(1)} %shard_map.91.pair_ref.refs_0_), channel_id=1, source_target_pairs={{0,3},{1,2},{2,1},{3,0},{4,7},{5,6},{6,5},{7,4},{8,11},{9,10},{10,... | collective-permute-start | bytes 393224 | tf_op jit(solution)/shard_map/ppermute | solution.py:30
  25.4 0.8 %shard_map.92 = bf16[128,256]{1,0:T(8,128)(2,1)} custom-call(bf16[256,256]{1,0:T(8,128)(2,1)S(1)} %shard_map.91.pair_ref.refs_0_, bf16[256,256]{1,0:T(8,128)(2,1)S(1)} %copy-done), custom_call_target="tpu_custom_call" | custom-call | flops 16777216 | bytes 262144 | tf_op jit(solution)/shard_map/pallas_call | solution.py:221
  26.2 4.9 %collective-permute-done.8.refs_3_.refs_1_ = bf16[256,256]{1,0:T(8,128)(2,1)S(1)} collective-permute-done((bf16[256,256]{1,0:T(8,128)(2,1)S(1)}, bf16[256,256]{1,0:T(8,128)(2,1)S(1)}, u32[]{:S(2)}, u32[]{:S(2)}) %collective-permute-start.8) | collective-permute-done | bytes 131104 | tf_op jit(solution)/shard_map/ppermute | solution.py:30
  31.1 0.0 collective-permute-done.9.refs_1_
  31.1 0.2 shard_map.94
  31.4 1.2 %collective-permute-done.10.refs_2_.refs_0_ = bf16[256,256]{1,0:T(8,128)(2,1)S(1)} collective-permute-done((bf16[256,256]{1,0:T(8,128)(2,1)S(1)}, bf16[256,256]{1,0:T(8,128)(2,1)S(1)}, u32[]{:S(2)}, u32[]{:S(2)}) %collective-permute-start.10) | collective-permute-done | bytes 131104 | tf_op jit(solution)/shard_map/ppermute | solution.py:30
  32.5 0.2 shard_map.95
  32.8 0.1 collective-permute-start.11
  32.9 0.4 shard_map.93
  33.3 0.9 %collective-permute-done.11.other_ref = bf16[256,256]{1,0:T(8,128)(2,1)S(1)} collective-permute-done((bf16[256,256]{1,0:T(8,128)(2,1)S(1)}, bf16[256,256]{1,0:T(8,128)(2,1)S(1)}, u32[]{:S(2)}, u32[]{:S(2)}) %collective-permute-start.11) | collective-permute-done | bytes 131104 | tf_op jit(solution)/shard_map/ppermute | solution.py:30
  34.2 0.1 collective-permute-start.13
  34.4 2.7 %collective-permute-start.12 = (bf16[256,256]{1,0:T(8,128)(2,1)S(1)}, bf16[256,256]{1,0:T(8,128)(2,1)S(1)}, u32[]{:S(2)}, u32[]{:S(2)}) collective-permute-start(bf16[256,256]{1,0:T(8,128)(2,1)S(1)} %get-tuple-element.42), channel_id=1, source_target_pairs={{0,24},{4,28},{8,16},{12,20},{16,8},{20,12},{24,0},{28,4},{1,25},{... | collective-permute-start | bytes 393224 | tf_op jit(solution)/shard_map/ppermute | solution.py:30
  37.1 0.0 collective-permute-done.13.other_ref
  37.1 0.3 collective-permute-start.14
  37.5 1.5 %collective-permute-start.15 = (bf16[256,256]{1,0:T(8,128)(2,1)S(1)}, bf16[256,256]{1,0:T(8,128)(2,1)S(1)}, u32[]{:S(2)}, u32[]{:S(2)}) collective-permute-start(bf16[256,256]{1,0:T(8,128)(2,1)S(1)} %get-tuple-element.45), channel_id=1, source_target_pairs={{0,16},{4,20},{8,24},{12,28},{16,0},{20,4},{24,8},{28,12},{1,17},{... | collective-permute-start | bytes 393224 | tf_op jit(solution)/shard_map/ppermute | solution.py:30
  39.0 2.7 %collective-permute-done.12.refs_0_ = bf16[256,256]{1,0:T(8,128)(2,1)S(1)} collective-permute-done((bf16[256,256]{1,0:T(8,128)(2,1)S(1)}, bf16[256,256]{1,0:T(8,128)(2,1)S(1)}, u32[]{:S(2)}, u32[]{:S(2)}) %collective-permute-start.12) | collective-permute-done | bytes 131104 | tf_op jit(solution)/shard_map/ppermute | solution.py:30
  41.7 2.2 %collective-permute-done.14.refs_1_ = bf16[256,256]{1,0:T(8,128)(2,1)S(1)} collective-permute-done((bf16[256,256]{1,0:T(8,128)(2,1)S(1)}, bf16[256,256]{1,0:T(8,128)(2,1)S(1)}, u32[]{:S(2)}, u32[]{:S(2)}) %collective-permute-start.14) | collective-permute-done | bytes 131104 | tf_op jit(solution)/shard_map/ppermute | solution.py:30
  43.9 0.0 collective-permute-done.15.refs_2_
  44.0 0.1 collective-permute-start.16
  44.1 0.8 %shard_map.99 = bf16[128,256]{1,0:T(8,128)(2,1)} custom-call(bf16[256,256]{1,0:T(8,128)(2,1)S(1)} %copy-done, f32[128,256]{1,0:T(8,128)S(1)} %get-tuple-element.46.own_ref, bf16[256,256]{1,0:T(8,128)(2,1)S(1)} %collective-permute-done.12.refs_0_, bf16[256,256]{1,0:T(8,128)(2,1)S(1)} %collective-permute-done.14.refs_1_, ...), custom_call_target="tpu_custom_call" | custom-call | flops 16777216 | bytes 393216 | tf_op jit(solution)/shard_map/pallas_call | solution.py:328
  44.9 0.4 collective-permute-done.16
  45.3 0.7 %fusion = f32[256,256]{1,0:T(8,128)} fusion(bf16[128,256]{1,0:T(8,128)(2,1)S(1)} %collective-permute-done.16, bf16[128,256]{1,0:T(8,128)(2,1)S(1)} %shard_map.98, pred[]{:T(512)S(6)} %eq.5), kind=kLoop, calls=%fused_computation.1 | loop fusion | flops 655360 | bytes 393217 | tf_op jit(solution)/shard_map/convert_element_type | solution.py:388
  (5 shorter events, 0.2 us)
Async XLA Ops:
  0.6 5.8 %copy-start.5 = (s32[1,8,1,2]{1,3,2,0:T(2,128)S(1)}, s32[1,8,1,2]{1,3,2,0:T(2,128)}, u32[]{:S(2)}) copy-start(s32[1,8,1,2]{1,3,2,0:T(2,128)} %param.9) | copy-start | bytes 196
  0.6 8.4 %collective-permute-start = (bf16[128,256]{1,0:T(8,128)(2,1)}, bf16[128,256]{1,0:T(8,128)(2,1)S(1)}, u32[]{:S(2)}, u32[]{:S(2)}) collective-permute-start(bf16[128,256]{1,0:T(8,128)(2,1)} %refs_0_.3), channel_id=1, source_target_pairs={{0,3},{1,2},{2,1},{3,0},{4,7},{5,6},{6,5},{7,4},{8,11},{9,10},{10,... | collective-permute-start | bytes 196616 | tf_op jit(solution)/shard_map/ppermute | solution.py:30
  5.8 5.8 %collective-permute-start.1 = (bf16[128,256]{1,0:T(8,128)(2,1)}, bf16[128,256]{1,0:T(8,128)(2,1)S(1)}, u32[]{:S(2)}, u32[]{:S(2)}) collective-permute-start(bf16[128,256]{1,0:T(8,128)(2,1)} %refs_0_.3), channel_id=1, source_target_pairs={{0,2},{1,3},{2,0},{3,1},{4,6},{5,7},{6,4},{7,5},{8,10},{9,11},{10,... | collective-permute-start | bytes 196616 | tf_op jit(solution)/shard_map/ppermute | solution.py:30
  5.8 5.8 %collective-permute-start.2 = (bf16[128,256]{1,0:T(8,128)(2,1)}, bf16[128,256]{1,0:T(8,128)(2,1)S(1)}, u32[]{:S(2)}, u32[]{:S(2)}) collective-permute-start(bf16[128,256]{1,0:T(8,128)(2,1)} %refs_0_.3), channel_id=1, source_target_pairs={{0,1},{1,0},{2,3},{3,2},{4,5},{5,4},{6,7},{7,6},{8,9},{9,8},{10,11... | collective-permute-start | bytes 196616 | tf_op jit(solution)/shard_map/ppermute | solution.py:30
  6.5 0.7 %copy-start.4 = (s32[1,8,1]{1,2,0:T(1,128)S(1)}, s32[1,8,1]{1,2,0:T(1,128)}, u32[]{:S(2)}) copy-start(s32[1,8,1]{1,2,0:T(1,128)} %param.10) | copy-start | bytes 100
  7.1 1.0 %copy-start.1 = (bf16[1,8,1,128,256]{4,3,2,1,0:T(8,128)(2,1)S(1)}, bf16[1,8,1,128,256]{4,3,2,1,0:T(8,128)(2,1)}, u32[]{:S(2)}) copy-start(bf16[1,8,1,128,256]{4,3,2,1,0:T(8,128)(2,1)} %param.11) | copy-start | bytes 1572868
  8.2 0.9 %copy-start.2 = (bf16[128,256]{1,0:T(8,128)(2,1)S(1)}, bf16[128,256]{1,0:T(8,128)(2,1)}, u32[]{:S(2)}) copy-start(bf16[128,256]{1,0:T(8,128)(2,1)} %refs_0_.3) | copy-start | bytes 196612
  11.7 1.3 %collective-permute-start.3 = (bf16[128,256]{1,0:T(8,128)(2,1)S(1)}, bf16[128,256]{1,0:T(8,128)(2,1)S(1)}, u32[]{:S(2)}, u32[]{:S(2)}) collective-permute-start(bf16[128,256]{1,0:T(8,128)(2,1)S(1)} %shard_map.88), channel_id=1, source_target_pairs={{0,4},{4,0},{8,12},{12,8},{16,20},{20,16},{24,28},{28,24},{1,5},{5... | collective-permute-start | bytes 196616 | tf_op jit(solution)/shard_map/ppermute | solution.py:30
  13.1 2.7 %collective-permute-start.4 = (bf16[384,256]{1,0:T(8,128)(2,1)S(1)}, bf16[384,256]{1,0:T(8,128)(2,1)S(1)}, u32[]{:S(2)}, u32[]{:S(2)}) collective-permute-start(bf16[384,256]{1,0:T(8,128)(2,1)S(1)} %get-tuple-element.27), channel_id=1, source_target_pairs={{0,4},{4,0},{8,12},{12,8},{16,20},{20,16},{24,28},{28,24},{1,5},{5... | collective-permute-start | bytes 589832 | tf_op jit(solution)/shard_map/ppermute | solution.py:30
  13.2 7.4 %copy-start = (bf16[256,256]{1,0:T(8,128)(2,1)S(1)}, bf16[256,256]{1,0:T(8,128)(2,1)}, u32[]{:S(2)}) copy-start(bf16[256,256]{1,0:T(8,128)(2,1)} %weight_ref.3) | copy-start | bytes 393220
  13.2 7.4 %copy-start.3 = (bf16[128,256]{1,0:T(8,128)(2,1)S(1)}, bf16[128,256]{1,0:T(8,128)(2,1)}, u32[]{:S(2)}) copy-start(bf16[128,256]{1,0:T(8,128)(2,1)} %refs_5_.1) | copy-start | bytes 196612
  13.3 5.4 %collective-permute-start.5 = (bf16[128,256]{1,0:T(8,128)(2,1)S(1)}, bf16[128,256]{1,0:T(8,128)(2,1)S(1)}, u32[]{:S(2)}, u32[]{:S(2)}) collective-permute-start(bf16[128,256]{1,0:T(8,128)(2,1)S(1)} %shard_map.90), channel_id=1, source_target_pairs={{0,24},{4,28},{8,16},{12,20},{16,8},{20,12},{24,0},{28,4},{1,25},{... | collective-permute-start | bytes 196616 | tf_op jit(solution)/shard_map/ppermute | solution.py:30
  15.8 4.3 %collective-permute-start.6 = (bf16[128,256]{1,0:T(8,128)(2,1)S(1)}, bf16[128,256]{1,0:T(8,128)(2,1)S(1)}, u32[]{:S(2)}, u32[]{:S(2)}) collective-permute-start(bf16[128,256]{1,0:T(8,128)(2,1)S(1)} %get-tuple-element.30), channel_id=1, source_target_pairs={{0,8},{4,12},{8,0},{12,4},{16,24},{20,28},{24,16},{28,20},{1,9},{5... | collective-permute-start | bytes 196616 | tf_op jit(solution)/shard_map/ppermute | solution.py:30
  16.4 4.3 %collective-permute-start.7 = (bf16[128,256]{1,0:T(8,128)(2,1)S(1)}, bf16[128,256]{1,0:T(8,128)(2,1)S(1)}, u32[]{:S(2)}, u32[]{:S(2)}) collective-permute-start(bf16[128,256]{1,0:T(8,128)(2,1)S(1)} %get-tuple-element.31), channel_id=1, source_target_pairs={{0,16},{4,20},{8,24},{12,28},{16,0},{20,4},{24,8},{28,12},{1,17},{... | collective-permute-start | bytes 196616 | tf_op jit(solution)/shard_map/ppermute | solution.py:30
  20.9 10.2 %collective-permute-start.8 = (bf16[256,256]{1,0:T(8,128)(2,1)S(1)}, bf16[256,256]{1,0:T(8,128)(2,1)S(1)}, u32[]{:S(2)}, u32[]{:S(2)}) collective-permute-start(bf16[256,256]{1,0:T(8,128)(2,1)S(1)} %shard_map.91.pair_ref.refs_0_), channel_id=1, source_target_pairs={{0,2},{1,3},{2,0},{3,1},{4,6},{5,7},{6,4},{7,5},{8,10},{9,11},{10,... | collective-permute-start | bytes 393224 | tf_op jit(solution)/shard_map/ppermute | solution.py:30
  22.6 8.6 %collective-permute-start.9 = (bf16[256,256]{1,0:T(8,128)(2,1)S(1)}, bf16[256,256]{1,0:T(8,128)(2,1)S(1)}, u32[]{:S(2)}, u32[]{:S(2)}) collective-permute-start(bf16[256,256]{1,0:T(8,128)(2,1)S(1)} %shard_map.91.pair_ref.refs_0_), channel_id=1, source_target_pairs={{0,1},{1,0},{2,3},{3,2},{4,5},{5,4},{6,7},{7,6},{8,9},{9,8},{10,11... | collective-permute-start | bytes 393224 | tf_op jit(solution)/shard_map/ppermute | solution.py:30
  24.3 8.3 %collective-permute-start.10 = (bf16[256,256]{1,0:T(8,128)(2,1)S(1)}, bf16[256,256]{1,0:T(8,128)(2,1)S(1)}, u32[]{:S(2)}, u32[]{:S(2)}) collective-permute-start(bf16[256,256]{1,0:T(8,128)(2,1)S(1)} %shard_map.91.pair_ref.refs_0_), channel_id=1, source_target_pairs={{0,3},{1,2},{2,1},{3,0},{4,7},{5,6},{6,5},{7,4},{8,11},{9,10},{10,... | collective-permute-start | bytes 393224 | tf_op jit(solution)/shard_map/ppermute | solution.py:30
  32.8 1.4 %collective-permute-start.11 = (bf16[256,256]{1,0:T(8,128)(2,1)S(1)}, bf16[256,256]{1,0:T(8,128)(2,1)S(1)}, u32[]{:S(2)}, u32[]{:S(2)}) collective-permute-start(bf16[256,256]{1,0:T(8,128)(2,1)S(1)} %get-tuple-element.38), channel_id=1, source_target_pairs={{0,4},{4,0},{8,12},{12,8},{16,20},{20,16},{24,28},{28,24},{1,5},{5... | collective-permute-start | bytes 393224 | tf_op jit(solution)/shard_map/ppermute | solution.py:30
  34.2 2.9 %collective-permute-start.13 = (bf16[384,256]{1,0:T(8,128)(2,1)S(1)}, bf16[384,256]{1,0:T(8,128)(2,1)S(1)}, u32[]{:S(2)}, u32[]{:S(2)}) collective-permute-start(bf16[384,256]{1,0:T(8,128)(2,1)S(1)} %get-tuple-element.43), channel_id=1, source_target_pairs={{0,4},{4,0},{8,12},{12,8},{16,20},{20,16},{24,28},{28,24},{1,5},{5... | collective-permute-start | bytes 589832 | tf_op jit(solution)/shard_map/ppermute | solution.py:30
  34.4 7.3 %collective-permute-start.12 = (bf16[256,256]{1,0:T(8,128)(2,1)S(1)}, bf16[256,256]{1,0:T(8,128)(2,1)S(1)}, u32[]{:S(2)}, u32[]{:S(2)}) collective-permute-start(bf16[256,256]{1,0:T(8,128)(2,1)S(1)} %get-tuple-element.42), channel_id=1, source_target_pairs={{0,24},{4,28},{8,16},{12,20},{16,8},{20,12},{24,0},{28,4},{1,25},{... | collective-permute-start | bytes 393224 | tf_op jit(solution)/shard_map/ppermute | solution.py:30
  37.1 6.8 %collective-permute-start.14 = (bf16[256,256]{1,0:T(8,128)(2,1)S(1)}, bf16[256,256]{1,0:T(8,128)(2,1)S(1)}, u32[]{:S(2)}, u32[]{:S(2)}) collective-permute-start(bf16[256,256]{1,0:T(8,128)(2,1)S(1)} %get-tuple-element.44), channel_id=1, source_target_pairs={{0,8},{4,12},{8,0},{12,4},{16,24},{20,28},{24,16},{28,20},{1,9},{5... | collective-permute-start | bytes 393224 | tf_op jit(solution)/shard_map/ppermute | solution.py:30
  37.5 6.4 %collective-permute-start.15 = (bf16[256,256]{1,0:T(8,128)(2,1)S(1)}, bf16[256,256]{1,0:T(8,128)(2,1)S(1)}, u32[]{:S(2)}, u32[]{:S(2)}) collective-permute-start(bf16[256,256]{1,0:T(8,128)(2,1)S(1)} %get-tuple-element.45), channel_id=1, source_target_pairs={{0,16},{4,20},{8,24},{12,28},{16,0},{20,4},{24,8},{28,12},{1,17},{... | collective-permute-start | bytes 393224 | tf_op jit(solution)/shard_map/ppermute | solution.py:30
  44.0 1.3 %collective-permute-start.16 = (bf16[128,256]{1,0:T(8,128)(2,1)S(1)}, bf16[128,256]{1,0:T(8,128)(2,1)S(1)}, u32[]{:S(2)}, u32[]{:S(2)}) collective-permute-start(bf16[128,256]{1,0:T(8,128)(2,1)S(1)} %shard_map.98), channel_id=1, source_target_pairs={{0,4},{4,0},{8,12},{12,8},{16,20},{20,16},{24,28},{28,24},{1,5},{5... | collective-permute-start | bytes 196616 | tf_op jit(solution)/shard_map/ppermute | solution.py:30
